TPU v7x, 32 devices: a whole 2x2x4 slice. The times are simulated.
32 devices in a mesh: dp: 8 (over z, x), vocab: 4 (over y, core).
Axes of the slice: x: 2, y: 2, z: 4, core: 2. Of those that a mesh axis runs over, the one named last changes fastest.
Arguments:
- token_ids: int32 [64, 2, 64], P('dp'), may hold values from 0 to 31999
- lengths: int32 [64, 2], P('dp'), may hold values from 32 to 64
- comp_mask: int32 [64, 2, 16], P('dp'), may hold values 0 or 1
- ref_logp: float32 [64, 2], P('dp'), may hold values from -240 to 240
- owner: int32 [32], replicated, may hold values from 0 to 31, as said below
- blocks: float32 [32, 768, 384], P('dp', 'vocab')
- left_stat: float32 [32, 768, 768], P('dp'), as said below
- right_stat: float32 [32, 384, 384], P('dp'), as said below
- left_root: float32 [32, 768, 768], P('dp')
- right_root: float32 [32, 384, 384], P('dp')
- tables: float32 [2, 32000, 768], P(None, ('vocab', 'dp'))
- table_moment: float32 [2, 32000, 768], P(None, ('vocab', 'dp')), may hold values from -0.00096 to 0.00096
- table_second: float32 [2, 32000, 768], P(None, ('vocab', 'dp')), may hold values from 2.56e-09 to 1.024e-08
- gains: float32 [3, 768], replicated, may hold values from 0.5 to 1.5
- gain_moment: float32 [3, 768], replicated, may hold values from -0.0384 to 0.0384
- gain_second: float32 [3, 768], replicated, may hold values from 4.096e-06 to 1.6384e-05
Outputs:
- new_blocks: float32 [32, 768, 384], P('dp', 'vocab')
- block_grads: float32 [32, 768, 384], P('dp', 'vocab')
- new_left: float32 [32, 768, 768], P('dp')
- new_right: float32 [32, 384, 384], P('dp')
- new_tables: float32 [2, 32000, 768], P(None, ('vocab', 'dp'))
- new_table_moment: float32 [2, 32000, 768], P(None, ('vocab', 'dp'))
- new_table_second: float32 [2, 32000, 768], P(None, ('vocab', 'dp'))
- new_gains: float32 [3, 768], replicated
- new_gain_moment: float32 [3, 768], replicated
- new_gain_second: float32 [3, 768], replicated
- loss_sum: float32 [], replicated
Inputs may be any that keep to these rules, and one draw needn't show every extreme that they name: `owner`: each slot number appears once. `left_stat`: symmetric positive definite. `right_stat`: symmetric positive definite.
All inputs are finite; a program needn't handle non-finite values. No bound on the sum of `comp_mask` on one device may be relied on, other than what follows from the above.
Results may differ from a plain program's by a relative error of at most 0.02.
Values may be sent and summed in bfloat16 or wider, within the bound.
No kernel may reach another device: no remote copies, remote signals or barrier semaphores. Data moves between devices by JAX's collectives and lax.ppermute only.
A program may use at most 320 MiB of HBM per device.

v0:
```python
import math

import jax
import jax.numpy as jnp
from jax import lax
from jax.sharding import PartitionSpec as P

D = 768
HEADS = 12
HDIM = 64
FF = 3072
SLOT = 64
MB = 2
CMP = 16
STEP = 10
BC = 384
NBLK = 32


NORM_EPS = 1e-05
DPO_BETA = 0.02
ROPE_BASE = 10000.0
ADAM_ONE = 0.9
ADAM_TWO = 0.999
ADAM_EPS = 1e-08
WEIGHT_DECAY = 0.01
GAIN_RATE = 0.3
STAT_DECAY = 0.5
SHAMPOO_RATE = 0.5
MASKED = -1e30


def joined(value, axis, join):
    pieces = jax.tree.map(lambda part: lax.all_gather(part, axis), value)
    head = jax.tree.map(lambda part: part[0], pieces)
    tail = jax.tree.map(lambda part: part[1:], pieces)
    so_far, _ = lax.scan(lambda so_far, section: (join(so_far, section), None), head, tail)
    return so_far


def mult(left, right):
    return jnp.dot(left, right, preferred_element_type=jnp.float32)


def mult_t(left, right):
    return lax.dot_general(
        left, right, (((0,), (0,)), ((), ())), preferred_element_type=jnp.float32
    )


def mult_nt(left, right):
    return lax.dot_general(
        left, right, (((1,), (1,)), ((), ())), preferred_element_type=jnp.float32
    )


def project(rows, group):
    product = jnp.einsum("td,ndk->tnk", rows, group, preferred_element_type=jnp.float32)
    return product.reshape(rows.shape[0], group.shape[0] * BC)


def project_back(grad, group):
    return jnp.einsum(
        "tnk,ndk->td",
        grad.reshape(grad.shape[0], group.shape[0], BC),
        group,
        preferred_element_type=jnp.float32,
    )


def block_grad(rows, grad, number):
    return jnp.einsum(
        "td,tnk->ndk",
        rows,
        grad.reshape(grad.shape[0], number, BC),
        preferred_element_type=jnp.float32,
    )


def down_forward(mix, down):
    row_total = mix.shape[0]
    product = jnp.einsum(
        "trd,rjdk->tjk",
        mix.reshape(row_total, FF // D, D),
        down.reshape(FF // D, D // BC, D, BC),
        preferred_element_type=jnp.float32,
    )
    return product.reshape(row_total, D)


def down_back(grad, down):
    row_total = grad.shape[0]
    product = jnp.einsum(
        "tjk,rjdk->trd",
        grad.reshape(row_total, D // BC, BC),
        down.reshape(FF // D, D // BC, D, BC),
        preferred_element_type=jnp.float32,
    )
    return product.reshape(row_total, FF)


def down_grad(mix, grad):
    row_total = mix.shape[0]
    product = jnp.einsum(
        "trd,tjk->rjdk",
        mix.reshape(row_total, FF // D, D),
        grad.reshape(row_total, D // BC, BC),
        preferred_element_type=jnp.float32,
    )
    return product.reshape(-1, D, BC)


def groups(weights):
    col_blocks = D // BC
    ff_blocks = FF // BC
    base_gate = 4 * col_blocks
    return (
        weights[0:col_blocks],
        weights[col_blocks : 2 * col_blocks],
        weights[2 * col_blocks : 3 * col_blocks],
        weights[3 * col_blocks : base_gate],
        weights[base_gate : base_gate + ff_blocks],
        weights[base_gate + ff_blocks : base_gate + 2 * ff_blocks],
        weights[base_gate + 2 * ff_blocks :],
    )


def rms_forward(values, gain):
    return values * lax.rsqrt(jnp.mean(values * values, axis=-1, keepdims=True) + NORM_EPS) * gain


def rms_backward(values, gain, grad):
    scale = lax.rsqrt(jnp.mean(values * values, axis=-1, keepdims=True) + NORM_EPS)
    inner = jnp.mean(values * gain * grad, axis=-1, keepdims=True)
    back = scale * gain * grad - values * scale**3 * inner
    return (back, jnp.sum(grad * values * scale, axis=0))


def angles():
    inv_freq = ROPE_BASE ** (-jnp.arange(HDIM // 2).astype(jnp.float32) * 2.0 / HDIM)
    phase_grid = jnp.arange(SLOT).astype(jnp.float32)[:, None] * inv_freq[None, :]
    return (jnp.cos(phase_grid), jnp.sin(phase_grid))


def rotate(values, cosine, sine, direction):
    half_dim = HDIM // 2
    lead_half = values[..., :half_dim]
    tail_half = values[..., half_dim:]
    cos_grid = cosine[None, :, None, :]
    sin_grid = direction * sine[None, :, None, :]
    return jnp.concatenate(
        [lead_half * cos_grid - tail_half * sin_grid, tail_half * cos_grid + lead_half * sin_grid],
        axis=-1,
    )


def attend_scores(q_rot, k_rot, len_vec):
    raw = jnp.einsum(
        "nqhd,nkhd->nhqk", q_rot, k_rot, preferred_element_type=jnp.float32
    ) / math.sqrt(HDIM)
    places = jnp.arange(SLOT)
    valid = (places[None, :] <= places[:, None])[None, None] & (
        places[None, None, None, :] < len_vec[:, None, None, None]
    )
    return jnp.where(valid, raw, MASKED)


def layer_forward(inputs, len_vec, gains, mats, cosine, sine):
    w_query, w_key, w_value, w_out, w_gate, w_up, w_down = mats
    seq_count = inputs.shape[0] // SLOT

    def to_heads(values):
        return values.reshape(seq_count, SLOT, HEADS, HDIM)

    a_low = rms_forward(inputs, gains[0]).astype(jnp.bfloat16)
    q_rot = rotate(to_heads(project(a_low, w_query)), cosine, sine, 1.0).astype(jnp.bfloat16)
    k_rot = rotate(to_heads(project(a_low, w_key)), cosine, sine, 1.0).astype(jnp.bfloat16)
    v_heads = to_heads(project(a_low, w_value)).astype(jnp.bfloat16)
    scores = attend_scores(q_rot, k_rot, len_vec)
    row_max = jnp.max(scores, axis=-1, keepdims=True)
    log_total = jnp.log(jnp.sum(jnp.exp(scores - row_max), axis=-1, keepdims=True)) + row_max
    p_low = jnp.exp(scores - log_total).astype(jnp.bfloat16)
    att_out = jnp.einsum("nhqk,nkhd->nqhd", p_low, v_heads, preferred_element_type=jnp.float32)
    att_out = att_out.reshape(seq_count * SLOT, D).astype(jnp.bfloat16)
    h_mid = inputs + project(att_out, w_out)
    b_low = rms_forward(h_mid, gains[1]).astype(jnp.bfloat16)
    gate_pre = project(b_low, w_gate)
    up_pre = project(b_low, w_up)
    mix_low = (jax.nn.silu(gate_pre) * up_pre).astype(jnp.bfloat16)
    h_out = h_mid + down_forward(mix_low, w_down)
    return (
        h_out,
        (a_low, q_rot, k_rot, v_heads, log_total, att_out, h_mid, b_low, gate_pre, up_pre, mix_low),
    )


def layer_backward(inputs, len_vec, gains, mats, cosine, sine, saved, grad_out):
    w_query, w_key, w_value, w_out, w_gate, w_up, w_down = mats
    a_low, q_rot, k_rot, v_heads, log_total, att_out, h_mid, b_low, gate_pre, up_pre, mix_low = (
        saved
    )
    seq_count = inputs.shape[0] // SLOT
    grad_branch = grad_out.astype(jnp.bfloat16)
    grad_mix = down_back(grad_branch, w_down)
    sigmoid_gate = jax.nn.sigmoid(gate_pre)
    grad_gate = (grad_mix * up_pre * sigmoid_gate * (1.0 + gate_pre * (1.0 - sigmoid_gate))).astype(
        jnp.bfloat16
    )
    grad_up = (grad_mix * gate_pre * sigmoid_gate).astype(jnp.bfloat16)
    grad_b = project_back(grad_gate, w_gate) + project_back(grad_up, w_up)
    back_mid, gain_mid = rms_backward(h_mid, gains[1], grad_b)
    grad_mid = grad_out + back_mid
    grad_attn = grad_mid.astype(jnp.bfloat16)
    grad_att = (
        project_back(grad_attn, w_out).astype(jnp.bfloat16).reshape(seq_count, SLOT, HEADS, HDIM)
    )
    p_full = jnp.exp(attend_scores(q_rot, k_rot, len_vec) - log_total)
    grad_p = jnp.einsum("nqhd,nkhd->nhqk", grad_att, v_heads, preferred_element_type=jnp.float32)
    grad_s = (p_full * (grad_p - jnp.sum(p_full * grad_p, axis=-1, keepdims=True))).astype(
        jnp.bfloat16
    )
    grad_q = jnp.einsum(
        "nhqk,nkhd->nqhd", grad_s, k_rot, preferred_element_type=jnp.float32
    ) / math.sqrt(HDIM)
    grad_k = jnp.einsum(
        "nhqk,nqhd->nkhd", grad_s, q_rot, preferred_element_type=jnp.float32
    ) / math.sqrt(HDIM)
    grad_v = jnp.einsum(
        "nhqk,nqhd->nkhd", p_full.astype(jnp.bfloat16), grad_att, preferred_element_type=jnp.float32
    )
    row_total = seq_count * SLOT
    grad_q = rotate(grad_q, cosine, sine, -1.0).reshape(row_total, D).astype(jnp.bfloat16)
    grad_k = rotate(grad_k, cosine, sine, -1.0).reshape(row_total, D).astype(jnp.bfloat16)
    grad_v = grad_v.reshape(row_total, D).astype(jnp.bfloat16)
    grad_a = (
        project_back(grad_q, w_query) + project_back(grad_k, w_key) + project_back(grad_v, w_value)
    )
    back_in, gain_in = rms_backward(inputs, gains[0], grad_a)
    operands = (
        a_low,
        grad_q,
        grad_k,
        grad_v,
        att_out,
        grad_attn,
        b_low,
        grad_gate,
        grad_up,
        mix_low,
        grad_branch,
    )
    return (grad_mid + back_in, operands, jnp.stack([gain_in, gain_mid]))


def weight_grads(operands):
    (
        a_low,
        grad_q,
        grad_k,
        grad_v,
        att_out,
        grad_attn,
        b_low,
        grad_gate,
        grad_up,
        mix_low,
        grad_branch,
    ) = operands
    col_blocks = D // BC
    ff_blocks = FF // BC
    return jnp.concatenate(
        [
            block_grad(a_low, grad_q, col_blocks),
            block_grad(a_low, grad_k, col_blocks),
            block_grad(a_low, grad_v, col_blocks),
            block_grad(att_out, grad_attn, col_blocks),
            block_grad(b_low, grad_gate, ff_blocks),
            block_grad(b_low, grad_up, ff_blocks),
            down_grad(mix_low, grad_branch),
        ],
        axis=0,
    )


def combine_parts(earlier, later):
    max_one, sum_one, pick_one = earlier
    max_two, sum_two, pick_two = later
    joint_max = jnp.maximum(max_one, max_two)
    joint_sum = sum_one * jnp.exp(max_one - joint_max) + sum_two * jnp.exp(max_two - joint_max)
    return (joint_max, joint_sum, pick_one + pick_two)


def adam_step(weight, grad, moment, second, rate):
    moment = ADAM_ONE * moment + (1.0 - ADAM_ONE) * grad
    second = ADAM_TWO * second + (1.0 - ADAM_TWO) * grad * grad
    ratio = moment / (1.0 - ADAM_ONE**STEP) / (jnp.sqrt(second / (1.0 - ADAM_TWO**STEP)) + ADAM_EPS)
    return (weight - rate * (ratio + WEIGHT_DECAY * weight), moment, second)


def per_device(
    token_ids,
    lengths,
    comp_mask,
    ref_logp,
    owner,
    blocks,
    left_stat,
    right_stat,
    left_root,
    right_root,
    tables,
    table_moment,
    table_second,
    gains,
    gain_moment,
    gain_second,
):
    vocab_count = lax.axis_size("vocab")
    vocab_index = lax.axis_index("vocab")
    row_share = blocks.shape[1]
    cosine, sine = angles()
    tables_low = lax.all_gather(tables.astype(jnp.bfloat16), "dp", axis=1, tiled=True)
    vocab_rows = tables_low.shape[1]
    local_ids = token_ids.reshape(-1) - vocab_index * vocab_rows
    inside = (local_ids >= 0) & (local_ids < vocab_rows)
    safe_ids = jnp.clip(local_ids, 0, vocab_rows - 1)
    looked = jnp.where(inside[:, None], jnp.take(tables_low[0], safe_ids, axis=0), 0).astype(
        jnp.float32
    )
    embedded = lax.psum_scatter(
        looked.astype(jnp.bfloat16), "vocab", scatter_dimension=0, tiled=True
    ).astype(jnp.float32)
    rows_all = lax.all_gather(blocks.astype(jnp.bfloat16), "vocab", axis=1, tiled=True)
    slots_all = lax.all_gather(rows_all, "dp", axis=0, tiled=True)
    kept_mats = groups(jnp.take(slots_all, owner, axis=0))
    gain_total = jnp.zeros((3, D), jnp.float32)
    loss_own = jnp.zeros((), jnp.float32)
    grad_inputs = []
    operand_list = []
    logit_grads = []
    head_inputs = []
    for micro in range(MB):
        own_pair = vocab_index * MB + micro
        rows_in = embedded[micro * 2 * SLOT : (micro + 1) * 2 * SLOT]
        len_own = lax.dynamic_index_in_dim(lengths, own_pair, 0, keepdims=False)
        h_out, saved = layer_forward(rows_in, len_own, gains, kept_mats, cosine, sine)
        pos_own = len_own[:, None] - 1 - CMP + jnp.arange(CMP)[None, :]
        picked_rows = jnp.take_along_axis(
            h_out.reshape(2, SLOT, D), pos_own[:, :, None], axis=1
        ).reshape(2 * CMP, D)
        c_low = rms_forward(picked_rows, gains[2]).astype(jnp.bfloat16)
        all_rows = lax.all_gather(c_low, "vocab", axis=0, tiled=True)
        ids_sel = token_ids[micro::MB]
        lens_sel = lengths[micro::MB]
        mask_sel = comp_mask[micro::MB].astype(jnp.float32)
        ref_sel = ref_logp[micro::MB]
        pos_sel = lens_sel[:, :, None] - 1 - CMP + jnp.arange(CMP)[None, None, :]
        target = (
            jnp.take_along_axis(ids_sel, pos_sel + 1, axis=2).reshape(-1) - vocab_index * vocab_rows
        )
        logits = mult_nt(all_rows, tables_low[1])
        one_hot = jnp.arange(vocab_rows)[None, :] == target[:, None]
        row_max = jnp.max(logits, axis=1)
        row_sum = jnp.sum(jnp.exp(logits - row_max[:, None]), axis=1)
        row_pick = jnp.sum(jnp.where(one_hot, logits, 0.0), axis=1)
        full_max, full_sum, full_pick = joined((row_max, row_sum, row_pick), "vocab", combine_parts)
        log_norm = full_max + jnp.log(full_sum)
        seq_logp = jnp.sum((full_pick - log_norm).reshape(vocab_count, 2, CMP) * mask_sel, axis=2)
        margin = DPO_BETA * (seq_logp[:, 0] - ref_sel[:, 0] - (seq_logp[:, 1] - ref_sel[:, 1]))
        loss_own = loss_own + jnp.take(jax.nn.softplus(-margin), vocab_index)
        pair_weight = -DPO_BETA * jax.nn.sigmoid(-margin)
        grad_tok = (jnp.stack([pair_weight, -pair_weight], axis=1)[:, :, None] * mask_sel).reshape(
            -1
        )
        grad_logits = (
            grad_tok[:, None] * (one_hot.astype(jnp.float32) - jnp.exp(logits - log_norm[:, None]))
        ).astype(jnp.bfloat16)
        logit_grads.append(grad_logits)
        head_inputs.append(all_rows)
        grad_c = lax.psum_scatter(
            mult(grad_logits, tables_low[1]), "vocab", scatter_dimension=0, tiled=True
        )
        back_rows, gain_head = rms_backward(picked_rows, gains[2], grad_c)
        seq_index = jnp.arange(2)[:, None]
        grad_top = (
            jnp.zeros((2, SLOT, D), jnp.float32)
            .at[seq_index, pos_own]
            .add(back_rows.reshape(2, CMP, D))
        )
        grad_in, operands, gains_now = layer_backward(
            rows_in, len_own, gains, kept_mats, cosine, sine, saved, grad_top.reshape(2 * SLOT, D)
        )
        operand_list.append(operands)
        gain_total = gain_total + jnp.concatenate([gains_now, gain_head[None]], axis=0)
        grad_inputs.append(grad_in)
    joined_ops = tuple(
        (
            jnp.concatenate([ops[i] for ops in operand_list], axis=0)
            for i in range(len(operand_list[0]))
        )
    )
    block_order = weight_grads(joined_ops)
    grad_head = mult_t(jnp.concatenate(logit_grads, axis=0), jnp.concatenate(head_inputs, axis=0))
    grad_rows = lax.all_gather(
        jnp.concatenate(grad_inputs, axis=0).astype(jnp.bfloat16), "vocab", axis=0, tiled=True
    ).astype(jnp.float32)
    grad_embed = (
        jnp.zeros((vocab_rows, D), jnp.float32)
        .at[safe_ids]
        .add(jnp.where(inside[:, None], grad_rows, 0.0))
    )
    table_grad = lax.psum_scatter(
        jnp.stack([grad_embed, grad_head]).astype(jnp.bfloat16),
        "dp",
        scatter_dimension=1,
        tiled=True,
    ).astype(jnp.float32)
    inverse = jnp.zeros((NBLK,), jnp.int32).at[owner].set(jnp.arange(NBLK, dtype=jnp.int32))
    slotted = jnp.take(block_order, inverse, axis=0)
    summed = lax.psum_scatter(slotted.astype(jnp.bfloat16), "dp", scatter_dimension=0, tiled=True)
    share_part = lax.psum_scatter(summed, "vocab", scatter_dimension=1, tiled=True).astype(
        jnp.float32
    )
    whole = lax.all_gather(share_part.astype(jnp.bfloat16), "vocab", axis=1, tiled=True).astype(
        share_part.dtype
    )
    highest = lax.Precision.HIGHEST
    new_left = STAT_DECAY * left_stat + (1.0 - STAT_DECAY) * jnp.einsum(
        "bij,bkj->bik", whole, whole, precision=highest
    )
    new_right = STAT_DECAY * right_stat + (1.0 - STAT_DECAY) * jnp.einsum(
        "bji,bjk->bik", whole, whole, precision=highest
    )
    direction = jnp.einsum("bij,bjk->bik", left_root, whole, precision=highest)
    direction = jnp.einsum("bij,bjk->bik", direction, right_root, precision=highest)
    new_blocks = blocks - SHAMPOO_RATE * lax.dynamic_slice_in_dim(
        direction, vocab_index * row_share, row_share, 1
    )
    loss_sum, gain_grad = lax.psum((loss_own, gain_total), ("dp", "vocab"))
    rates = jnp.array([0.3, 0.02], jnp.float32)[:, None, None]
    new_tables, new_table_moment, new_table_second = adam_step(
        tables, table_grad, table_moment, table_second, rates
    )
    new_gains, new_gain_moment, new_gain_second = adam_step(
        gains, gain_grad, gain_moment, gain_second, GAIN_RATE
    )
    return (
        new_blocks,
        share_part,
        new_left,
        new_right,
        new_tables,
        new_table_moment,
        new_table_second,
        new_gains,
        new_gain_moment,
        new_gain_second,
        loss_sum,
    )


def solution(mesh):
    placed = (
        P("dp", None, None),
        P("dp", None),
        P("dp", None, None),
        P("dp", None),
        P(),
        P("dp", "vocab", None),
        P("dp", None, None),
        P("dp", None, None),
        P("dp", None, None),
        P("dp", None, None),
        P(None, ("vocab", "dp"), None),
        P(None, ("vocab", "dp"), None),
        P(None, ("vocab", "dp"), None),
        P(),
        P(),
        P(),
    )
    return jax.shard_map(
        per_device,
        mesh=mesh,
        in_specs=placed,
        out_specs=(
            P("dp", "vocab", None),
            P("dp", "vocab", None),
            P("dp", None, None),
            P("dp", None, None),
            P(None, ("vocab", "dp"), None),
            P(None, ("vocab", "dp"), None),
            P(None, ("vocab", "dp"), None),
            P(),
            P(),
            P(),
            P(),
        ),
        check_vma=False,
    )
```

profile of v0, /device:TPU:0, one launch (start us, length us, event | category | flops | bytes accessed | tf_op | source)
XLA Modules:
  0.0 2527.1 jit_solution(1850436785781250671)
XLA Ops:
  14.4 22.6 all-gather.20.cloned.1.call-done
  49.0 459.5 %all-gather.18.cloned.1.call-done = bf16[2,8000,768]{2,1,0:T(8,128)(2,1)} async-done(((bf16[2,1000,768]{2,1,0:T(8,128)(2,1)}), bf16[2,8000,768]{2,1,0:T(8,128)(2,1)}) %all-gather.18.cloned.1.call-update) | async-done | bytes 24576016 | tf_op jit(solution)/shard_map/all_gather | solution.py:322
  508.5 10.6 slice_bitcast_fusion.1
  519.1 11.6 gather_fusion
  536.0 336.5 %all-gather.22.cloned.1.call-done = bf16[32,768,384]{2,1,0:T(8,128)(2,1)} async-done(((bf16[4,768,384]{2,1,0:T(8,128)(2,1)}), bf16[32,768,384]{2,1,0:T(8,128)(2,1)}) %all-gather.22.cloned.1.call-update) | async-done | bytes 18874384 | tf_op jit(solution)/shard_map/all_gather | solution.py:334
  872.6 14.9 gather_fusion.1
  887.5 10.5 broadcast_select_fusion
  907.4 6.6 copy.302
  1007.7 5.5 fusion.34
  1054.0 5.8 all_gather.67
  1059.8 6.4 fusion.212
  1082.4 5.6 all_gather.60
  1088.0 6.4 fusion.211
  1119.8 7.2 fusion.17
  1132.0 7.3 fusion.19
  1157.8 14.2 reduce-scatter.8.cloned.1.call-done
  1183.1 6.0 multiply_convert_fusion.5
  1195.5 5.7 scatter_fusion.1
  1323.2 14.6 gather_fusion.2
  1337.9 20.2 select_convert_fusion
  1359.1 10.2 fusion.16
  1369.3 18.2 scatter_custom_fusion.3
  1387.5 13.1 convert_bitcast_fusion
  1400.6 270.8 %reduce-scatter.12.cloned.1.call-done = bf16[4,768,384]{1,2,0:T(8,128)(2,1)} async-done(((bf16[32,768,384]{1,2,0:T(8,128)(2,1)}), bf16[4,768,384]{1,2,0:T(8,128)(2,1)}) %reduce-scatter.12.cloned.1.call-update) | async-done | bytes 2359312 | tf_op jit(solution)/shard_map/reduce_scatter | solution.py:420
  1676.9 20.5 pad_maximum_fusion
  1699.3 32.5 %all-reduce.6.cloned.1.call-done = bf16[4,768,384]{2,0,1:T(4,128)(2,1)} async-done(((bf16[4,768,384]{2,0,1:T(4,128)(2,1)}), bf16[4,768,384]{2,0,1:T(4,128)(2,1)}) %all-reduce.6.cloned.1.call-update) | async-done | bytes 2359312
  1737.8 45.8 %all-reduce.2 = (f32[3,768]{1,0:T(4,128)S(1)}, f32[]{:T(128)}) all-reduce(f32[3,768]{1,0:T(4,128)S(1)} %maximum_add_fusion, f32[]{:T(128)} %bitcast.94), channel_id=1, replica_groups=mesh['dp'=8,'vocab'=4] {'dp','vocab'}, use_global_device_ids=true, to_apply=%region_46.49 | all-reduce | flops 2305 | bytes 18440 | tf_op jit(solution)/shard_map/psum | solution.py:439
  1784.3 679.3 %all-reduce.8.cloned.1.call-done = bf16[2,8000,768]{2,1,0:T(8,128)(2,1)} async-done(((bf16[2,8000,768]{2,1,0:T(8,128)(2,1)}), bf16[2,8000,768]{2,1,0:T(8,128)(2,1)}) %all-reduce.8.cloned.1.call-update) | async-done | bytes 24576016
  2463.6 15.4 multiply_subtract_fusion
  2480.1 8.8 all-gather.24.cloned.1.call-done
  2489.0 11.7 fusion.47
  2500.7 9.4 fusion.213
  (634 shorter events, 395.1 us)
Async XLA Ops:
  7.2 2493.5 %copy-start = (f32[4,384,384]{2,1,0:T(8,128)S(1)}, f32[4,384,384]{2,1,0:T(8,128)}, u32[]{:S(2)}) copy-start(f32[4,384,384]{2,1,0:T(8,128)} %param.34) | copy-start | bytes 7077892
  7.2 29.8 %all-gather.20.cloned.1.call-start = ((), (), s32[]{:S(2)}) async-start(), calls=%async_computation.6 | async-start | bytes 2949120 | tf_op jit(solution)/shard_map/all_gather | solution.py:333
  9.6 498.9 %all-gather.18.cloned.1.call-start = ((), (), s32[]{:S(2)}) async-start(), calls=%async_computation.4 | async-start | bytes 27648000 | tf_op jit(solution)/shard_map/all_gather | solution.py:322
  14.3 22.8 copy-start.97
  14.3 22.9 copy-start.109
  14.3 23.1 copy-start.133
  14.3 858.2 %all-gather.22.cloned.1.call-start = ((), (), s32[]{:S(2)}) async-start(), calls=%async_computation.7 | async-start | bytes 21233664 | tf_op jit(solution)/shard_map/all_gather | solution.py:334
  37.0 877.0 %reduce-scatter.6.cloned.1.call-start = ((), (), s32[]{:S(2)}) async-start(), calls=%async_computation.5 | async-start | bytes 1966080 | tf_op jit(solution)/shard_map/reduce_scatter | solution.py:330
  37.7 493.0 %copy-start.112 = (pred[1024]{0:T(1024)(128)(4,1)}, pred[1024]{0:T(1024)(128)(4,1)S(1)}, u32[]{:S(2)}) copy-start(pred[1024]{0:T(1024)(128)(4,1)S(1)} %and.92) | copy-start | bytes 3076
  48.9 866.9 %copy-start.98 = (f32[768]{0:T(1024)}, f32[768]{0:T(1024)S(1)}, u32[]{:S(2)}) copy-start(f32[768]{0:T(1024)S(1)} %get-tuple-element.185) | copy-start | bytes 9220
  49.0 470.1 %copy-start.108 = (s32[1024,1]{0,1:T(1,128)}, s32[1024,1]{0,1:T(1,128)S(1)}, u32[]{:S(2)}) copy-start(s32[1024,1]{0,1:T(1,128)S(1)} %compare_select_fusion) | copy-start | bytes 12292
  533.6 624.2 %reduce-scatter.10.cloned.1.call-start = ((), (), s32[]{:S(2)}) async-start(), calls=%async_computation.9 | async-start | bytes 491520 | tf_op jit(solution)/shard_map/reduce_scatter | solution.py:380
  976.6 51.0 %copy-start.20 = (f32[128,768]{1,0:T(8,128)}, f32[128,768]{1,0:T(8,128)S(1)}, u32[]{:S(2)}) copy-start(f32[128,768]{1,0:T(8,128)S(1)} %get-tuple-element.340) | copy-start | bytes 1179652
  1066.2 28.2 %copy-start.7 = (f32[128,8000]{0,1:T(8,128)}, f32[128,8000]{0,1:T(8,128)S(1)}, u32[]{:S(2)}) copy-start(f32[128,8000]{0,1:T(8,128)S(1)} %get-tuple-element.344) | copy-start | bytes 12288004
  1127.0 45.0 %reduce-scatter.8.cloned.1.call-start = ((), (), s32[]{:S(2)}) async-start(), calls=%async_computation.8 | async-start | bytes 491520 | tf_op jit(solution)/shard_map/reduce_scatter | solution.py:380
  1139.4 229.9 %all-gather.26.cloned.1.call-start = ((), (), s32[]{:S(2)}) async-start(), calls=%async_computation.12 | async-start | bytes 1966080 | tf_op jit(solution)/shard_map/all_gather | solution.py:404
  1300.0 371.4 %reduce-scatter.12.cloned.1.call-start = ((), (), s32[]{:S(2)}) async-start(), calls=%async_computation.10 | async-start | bytes 21233664 | tf_op jit(solution)/shard_map/reduce_scatter | solution.py:420
  1358.1 373.7 %all-reduce.6.cloned.1.call-start = ((), (), s32[]{:S(2)}) async-start(), calls=%async_computation.13 | async-start | bytes 4718592
  1676.8 786.8 %all-reduce.8.cloned.1.call-start = ((), (), s32[]{:S(2)}) async-start(), calls=%async_computation.14 | async-start | bytes 49152000
  1697.4 36.5 %copy-start.148 = (u32[32]{0:T(128)S(1)}, u32[32]{0:T(128)}, u32[]{:S(2)}) copy-start(u32[32]{0:T(128)} %constant.422) | copy-start | bytes 388
  1697.4 37.8 %copy-start.145 = (f32[4]{0:T(128)S(1)}, f32[4]{0:T(128)}, u32[]{:S(2)}) copy-start(f32[4]{0:T(128)} %get-tuple-element.227) | copy-start | bytes 52
  1697.4 38.4 %copy-start.146 = (f32[4]{0:T(128)S(1)}, f32[4]{0:T(128)}, u32[]{:S(2)}) copy-start(f32[4]{0:T(128)} %get-tuple-element.229) | copy-start | bytes 52
  1697.4 40.3 %copy-start.132 = (f32[768]{0:T(1024)S(1)}, f32[768]{0:T(1024)}, u32[]{:S(2)}) copy-start(f32[768]{0:T(1024)} %get-tuple-element.175) | copy-start | bytes 9220
  1697.4 40.3 %copy-start.131 = (f32[768]{0:T(1024)S(1)}, f32[768]{0:T(1024)}, u32[]{:S(2)}) copy-start(f32[768]{0:T(1024)} %get-tuple-element.305) | copy-start | bytes 9220
  1697.4 40.3 %copy-start.107 = (f32[768]{0:T(1024)S(1)}, f32[768]{0:T(1024)}, u32[]{:S(2)}) copy-start(f32[768]{0:T(1024)} %get-tuple-element.181) | copy-start | bytes 9220
  1697.4 40.3 %copy-start.106 = (f32[768]{0:T(1024)S(1)}, f32[768]{0:T(1024)}, u32[]{:S(2)}) copy-start(f32[768]{0:T(1024)} %get-tuple-element.309) | copy-start | bytes 9220
  1697.4 86.2 %copy-start.102 = (f32[3,768]{1,0:T(4,128)S(1)}, f32[3,768]{1,0:T(4,128)}, u32[]{:S(2)}) copy-start(f32[3,768]{1,0:T(4,128)} %param.38) | copy-start | bytes 27652
  1697.4 86.2 %copy-start.110 = (f32[3,768]{1,0:T(4,128)S(1)}, f32[3,768]{1,0:T(4,128)}, u32[]{:S(2)}) copy-start(f32[3,768]{1,0:T(4,128)} %param.39) | copy-start | bytes 27652
  1697.4 86.2 %copy-start.111 = (f32[3,768]{1,0:T(4,128)S(1)}, f32[3,768]{1,0:T(4,128)}, u32[]{:S(2)}) copy-start(f32[3,768]{1,0:T(4,128)} %param.40) | copy-start | bytes 27652
  1697.5 766.2 %copy-start.141 = (f32[2]{0:T(128)S(1)}, f32[2]{0:T(128)}, u32[]{:S(2)}) copy-start(f32[2]{0:T(128)} %constant.247.clone) | copy-start | bytes 28
  1697.5 791.5 %all-gather.24.cloned.1.call-start = ((), (), s32[]{:S(2)}) async-start(), calls=%async_computation.11 | async-start | bytes 2949120 | tf_op jit(solution)/shard_map/all_gather | solution.py:424
  1784.3 694.7 %copy-start.27 = (bf16[4,192,384]{2,0,1:T(4,128)(2,1)S(1)}, bf16[4,192,384]{2,0,1:T(4,128)(2,1)}, u32[]{:S(2)}) copy-start(bf16[4,192,384]{2,0,1:T(4,128)(2,1)} %constant_dynamic-slice_fusion.6) | copy-start | bytes 1769476
  (137 other events, 1012.9 us)
Sparse Core Ops, SparseCore 0:
  10.2 26.7 all-gather.19
  39.1 469.3 all-gather.17
  510.1 362.4 all-gather.21
  875.5 28.1 reduce-scatter.5
  1127.1 20.9 reduce-scatter.9
  1151.2 20.8 reduce-scatter.7
  1300.1 19.5 all-gather.25
  1358.2 313.1 reduce-scatter.11
  1676.9 54.7 all-reduce.5
  1736.5 727.1 all-reduce.7
  2465.8 23.0 all-gather.23
where the time goes:
time: 2540 us; the launch traced here: 2530 us
  waiting for transfers between devices  1820 us (72%)
  local copies, waits for them, and re-layouts  225 us (9%)
  matrix products  196 us (8%)
  other arithmetic  175 us (7%)
  blocking collectives  87.4 us (3%)
    unnamed x13, waiting for transfers between devices  712 us
    all_gather x1, waiting for transfers between devices, per_device(): lax.all_gather(tables.astype(jnp.bfloat16), 'dp', axis=1, tiled=True)  459 us
    all_gather x1, waiting for transfers between devices, per_device(): slots_all = lax.all_gather(rows_all, 'dp', axis=0, tiled=True)  337 us
    reduce_scatter x1, waiting for transfers between devices, per_device(): lax.psum_scatter(slotted.astype(jnp.bfloat16), 'dp', scatter_dimension=0,...  271 us
  transfers between devices with their start and end apart: 11, of which 8 were waited for; matrix products, arithmetic and copies ran while one was open for 10% of the time, Pallas kernels for 0%

commit v1 on v0

--- a/solution.py
+++ b/solution.py
@@ -1,8 +1,12 @@
+import functools
 import math
 
 import jax
 import jax.numpy as jnp
 from jax import lax
+from jax.experimental import pallas as pl
+from jax.experimental.pallas import tpu as pltpu
+from jax.sharding import Mesh
 from jax.sharding import PartitionSpec as P
 
 D = 768
@@ -459,37 +463,968 @@
     )
 
 
+PAIR_ROWS = MB * 2 * CMP
+TOKENS = MB * 2 * SLOT
+CAP = 24
+MSG = 32
+EXT = D + 128
+AXES = ("z", "x", "y", "core")
+SHARD_AXES = ("y", "core", "z", "x")
+VMEM_LIMIT = 60 * 1024 * 1024
+
+AT_A = 0
+AT_DK = AT_A + TOKENS
+AT_DV = AT_DK + TOKENS
+AT_AP = AT_DV + TOKENS
+AT_DQ = AT_AP + PAIR_ROWS
+AT_O = AT_DQ + PAIR_ROWS
+AT_DO = AT_O + PAIR_ROWS
+AT_B = AT_DO + PAIR_ROWS
+AT_Z = AT_B + PAIR_ROWS
+AT_DGATE = AT_Z + (FF // D) * PAIR_ROWS
+AT_DUP = AT_DGATE + (FF // D) * PAIR_ROWS
+AT_DH = AT_DUP + (FF // D) * PAIR_ROWS
+ACT_ROWS = AT_DH + PAIR_ROWS
+
+
+def flat_of(z, x, y, c):
+    return ((z * 2 + x) * 2 + y) * 2 + c
+
+
+def moves(target):
+    pairs = []
+    for z in range(4):
+        for x in range(2):
+            for y in range(2):
+                for c in range(2):
+                    pairs.append((flat_of(z, x, y, c), flat_of(*target(z, x, y, c))))
+    return pairs
+
+
+def hop_one(value):
+    return lax.ppermute(
+        value,
+        AXES,
+        moves(lambda z, x, y, c: (z, 1 - x, y, c) if c == 0 else (z, x, 1 - y, c)),
+    )
+
+
+def hop_two(value):
+    return lax.ppermute(
+        value,
+        AXES,
+        moves(lambda z, x, y, c: (z, x, 1 - y, c) if c == 0 else (z, 1 - x, y, c)),
+    )
+
+
+def hop_core(value):
+    return lax.ppermute(value, AXES, moves(lambda z, x, y, c: (z, x, y, 1 - c)))
+
+
+def hop_y(value):
+    return lax.ppermute(value, AXES, moves(lambda z, x, y, c: (z, x, 1 - y, c)))
+
+
+def ring(value, step):
+    return lax.ppermute(value, AXES, moves(lambda z, x, y, c: ((z + step) % 4, x, y, c)))
+
+
+def spread(chunk):
+    line = jnp.stack([chunk] + [ring(chunk, step) for step in range(1, 4)])
+    one = hop_one(line)
+    two = hop_two(line)
+    both = hop_two(one)
+    plane = jnp.stack([line, one, two, both])
+    return plane, hop_core(plane)
+
+
+def dot_nn(left, right):
+    return lax.dot_general(left, right, (((1,), (0,)), ((), ())), preferred_element_type=jnp.float32)
+
+
+def dot_nt(left, right):
+    return lax.dot_general(left, right, (((1,), (1,)), ((), ())), preferred_element_type=jnp.float32)
+
+
+def dot_tn(left, right):
+    return lax.dot_general(left, right, (((0,), (0,)), ((), ())), preferred_element_type=jnp.float32)
+
+
+def low(value):
+    return value.astype(jnp.bfloat16)
+
+
+def high(value):
+    return value.astype(jnp.float32)
+
+
+def source_of(coord, other_core, rel, back):
+    core = coord[3] + other_core * (1 - 2 * coord[3])
+    first = rel & 1
+    second = rel >> 1
+    x_flip = first + core * (second - first)
+    y_flip = second + core * (first - second)
+    z = (coord[0] + 4 - back) & 3
+    x = coord[1] + x_flip * (1 - 2 * coord[1])
+    y = coord[2] + y_flip * (1 - 2 * coord[2])
+    return z, x, y, core
+
+
+def start_weights(coord, parts, held, sem):
+    for index in range(8):
+        slot_low, other_core = index // 2, index % 2
+
+        def one(i, carry):
+            rel, back = i >> 2, i & 3
+            z, x, y, core = source_of(coord, other_core, rel, back)
+            slot = 8 * z + 4 * x + slot_low
+            row = pl.multiple_of(192 * (2 * y + core), 64)
+            pltpu.make_async_copy(
+                parts[index].at[rel, back], held.at[slot, pl.ds(row, 192)], sem
+            ).start()
+            return carry
+
+        lax.fori_loop(0, 16, one, 0)
+
+
+def wait_weights(held, sem):
+    pltpu.make_async_copy(held, held, sem).wait()
+
+
+def iota(shape, axis):
+    return lax.broadcasted_iota(jnp.int32, shape, axis)
+
+
+def pick_rows(lens):
+    row = iota((PAIR_ROWS, 1), 0)
+    seq = row >> 4
+    length = jnp.where(
+        seq == 0, lens[0], jnp.where(seq == 1, lens[1], jnp.where(seq == 2, lens[2], lens[3]))
+    )
+    return seq, length - 1 - CMP + (row & 15)
+
+
+def masks(lens):
+    seq, pos = pick_rows(lens)
+    col = iota((PAIR_ROWS, TOKENS), 1)
+    same = (col >> 6) == seq
+    key = col & 63
+    return same & (key <= pos), same & (key == pos)
+
+
+def turn(chunk, cosine, sine, sign):
+    lane = iota(chunk.shape, 1)
+    swapped = jnp.where((lane & 63) < 32, pltpu.roll(chunk, 96, 1), pltpu.roll(chunk, 32, 1))
+    return chunk * cosine + swapped * (sine * sign)
+
+
+def scale_of(values):
+    return lax.rsqrt(jnp.mean(values * values, axis=-1, keepdims=True) + NORM_EPS)
+
+
+def rms_back(values, gain, grad):
+    scale = scale_of(values)
+    inner = jnp.mean(values * gain * grad, axis=-1, keepdims=True)
+    back = scale * gain * grad - values * (scale * scale * scale) * inner
+    return back, jnp.sum(grad * values * scale, axis=0, keepdims=True)
+
+
+def forward_kernel(owner, coord, lens, x, gains, cos_q, sin_q, cos_k, sin_k, *rest):
+    parts, rest = rest[:8], rest[8:]
+    a_out, ap_out, q_out, k_out, v_out, o_out, h1_out, b_out, gate_out, up_out, z_out, h2_out, c_out = rest[:13]
+    held, sem = rest[13:]
+    start_weights(coord, parts, held, sem)
+    values = high(x[...])
+    a_low = low(values * scale_of(values) * gains[0:1, :])
+    a_out[...] = a_low
+    valid, chosen = masks(lens)
+    select = jnp.where(chosen, 1.0, 0.0).astype(jnp.bfloat16)
+    a_pick = low(dot_nn(select, a_low))
+    ap_out[...] = a_pick
+    x_pick = dot_nn(select, x[...])
+    wait_weights(held, sem)
+    for j in range(2):
+        q = dot_nn(a_pick, held[owner[j]])
+        k = dot_nn(a_low, held[owner[2 + j]])
+        v_out[:, j * BC : (j + 1) * BC] = low(dot_nn(a_low, held[owner[4 + j]]))
+        for i in range(3):
+            at = slice(j * BC + i * 128, j * BC + (i + 1) * 128)
+            q_out[:, at] = low(turn(q[:, i * 128 : (i + 1) * 128], cos_q[...], sin_q[...], 1.0))
+            k_out[:, at] = low(turn(k[:, i * 128 : (i + 1) * 128], cos_k[...], sin_k[...], 1.0))
+    lane = iota((TOKENS, 128), 1)
+    zero = jnp.zeros((TOKENS, 128), jnp.bfloat16)
+    for p in range(HEADS // 2):
+        at = slice(p * 128, (p + 1) * 128)
+        total = jnp.zeros((PAIR_ROWS, 128), jnp.float32)
+        for h in range(2):
+            mine = (lane >> 6) == h
+            s = dot_nt(q_out[:, at], jnp.where(mine, k_out[:, at], zero)) * (1.0 / math.sqrt(HDIM))
+            s = jnp.where(valid, s, MASKED)
+            e = jnp.exp(s - jnp.max(s, axis=-1, keepdims=True))
+            prob = low(e / jnp.sum(e, axis=-1, keepdims=True))
+            total = total + dot_nn(prob, jnp.where(mine, v_out[:, at], zero))
+        o_out[:, at] = low(total)
+    for j in range(2):
+        at = slice(j * BC, (j + 1) * BC)
+        h1_out[:, at] = x_pick[:, at] + dot_nn(o_out[...], held[owner[6 + j]])
+    h1 = h1_out[...]
+    b_low = low(h1 * scale_of(h1) * gains[1:2, :])
+    b_out[...] = b_low
+    for j in range(FF // BC):
+        at = slice(j * BC, (j + 1) * BC)
+        gate = dot_nn(b_low, held[owner[8 + j]])
+        up = dot_nn(b_low, held[owner[16 + j]])
+        gate_out[:, at] = gate
+        up_out[:, at] = up
+        z_out[:, at] = low(gate * jax.nn.sigmoid(gate) * up)
+    for j in range(2):
+        total = h1[:, j * BC : (j + 1) * BC]
+        for r in range(FF // D):
+            total = total + dot_nn(z_out[:, r * D : (r + 1) * D], held[owner[24 + 2 * r + j]])
+        h2_out[:, j * BC : (j + 1) * BC] = total
+    h2 = h2_out[...]
+    c_out[...] = low(h2 * scale_of(h2) * gains[2:3, :])
+
+
+def vmem(number):
+    return [pl.BlockSpec(memory_space=pltpu.VMEM)] * number
+
+
+def smem(number):
+    return [pl.BlockSpec(memory_space=pltpu.SMEM)] * number
+
+
+def anywhere(number):
+    return [pl.BlockSpec(memory_space=pl.ANY)] * number
+
+
+def forward_call(owner, coord, lens, x, gains, turns, parts):
+    def made(rows, columns, kind):
+        return jax.ShapeDtypeStruct((rows, columns), kind)
+
+    return pl.pallas_call(
+        forward_kernel,
+        out_shape=(
+            made(TOKENS, D, jnp.bfloat16),
+            made(PAIR_ROWS, D, jnp.bfloat16),
+            made(PAIR_ROWS, D, jnp.bfloat16),
+            made(TOKENS, D, jnp.bfloat16),
+            made(TOKENS, D, jnp.bfloat16),
+            made(PAIR_ROWS, D, jnp.bfloat16),
+            made(PAIR_ROWS, D, jnp.float32),
+            made(PAIR_ROWS, D, jnp.bfloat16),
+            made(PAIR_ROWS, FF, jnp.float32),
+            made(PAIR_ROWS, FF, jnp.float32),
+            made(PAIR_ROWS, FF, jnp.bfloat16),
+            made(PAIR_ROWS, D, jnp.float32),
+            made(PAIR_ROWS, D, jnp.bfloat16),
+        ),
+        in_specs=smem(3) + vmem(6) + anywhere(8),
+        out_specs=tuple(vmem(13)),
+        scratch_shapes=[
+            pltpu.VMEM((NBLK, D, BC), jnp.bfloat16),
+            pltpu.SemaphoreType.DMA,
+        ],
+        compiler_params=pltpu.CompilerParams(vmem_limit_bytes=VMEM_LIMIT),
+        name="layer_forward",
+    )(owner, coord, lens, x, gains, *turns, *parts)
+
+
+def unpack(ext):
+    stat = high(ext[:, D:EXT])
+    top = (stat[:, 0:1] + stat[:, 1:2]) + stat[:, 2:3]
+    total = (stat[:, 3:4] + stat[:, 4:5]) + stat[:, 5:6]
+    return top, total, high(ext[:, :D])
+
+
+def pack_stat(top, total):
+    lane = iota((top.shape[0], 128), 1)
+    out = jnp.zeros((top.shape[0], 128), jnp.float32)
+    for first, value in ((0, top), (3, total)):
+        for i in range(3):
+            piece = high(low(value))
+            out = jnp.where(lane == first + i, piece, out)
+            value = value - piece
+    return low(out)
+
+
+def merge(items):
+    top = items[0][0]
+    for item in items[1:]:
+        top = jnp.maximum(top, item[0])
+    total = 0.0
+    mixed = 0.0
+    for item_top, item_total, item_mixed in items:
+        factor = jnp.exp(item_top - top)
+        total = total + item_total * factor
+        mixed = mixed + item_mixed * factor
+    return top, total, mixed
+
+
+def merge_kernel(*refs):
+    out = refs[-1]
+    top, total, mixed = merge([unpack(ref[...]) for ref in refs[:-1]])
+    out[:, :D] = low(mixed)
+    out[:, D:EXT] = pack_stat(top, total)
+
+
+def merge_call(*parts):
+    rows = parts[0].shape[0]
+    block = min(rows, 256)
+    spec = pl.BlockSpec((block, EXT), lambda i: (i, 0))
+    return pl.pallas_call(
+        merge_kernel,
+        grid=(rows // block,),
+        out_shape=jax.ShapeDtypeStruct((rows, EXT), jnp.bfloat16),
+        in_specs=[spec] * len(parts),
+        out_specs=spec,
+        compiler_params=pltpu.CompilerParams(vmem_limit_bytes=VMEM_LIMIT),
+        name="merge_parts",
+    )(*parts)
+
+
+def head_kernel(real, rows, head, ext, kept, stat):
+    logits = dot_nt(rows[...], head[...])
+    col = iota(logits.shape, 1)
+    logits = jnp.where(col < real, logits, MASKED)
+    top = jnp.max(logits, axis=-1, keepdims=True)
+    e = jnp.exp(logits - top)
+    total = jnp.sum(e, axis=-1, keepdims=True)
+    e_low = low(e)
+    kept[...] = e_low
+    ext[:, :D] = low(dot_nn(e_low, head[...]))
+    ext[:, D:EXT] = pack_stat(top, total)
+    stat[...] = jnp.broadcast_to(top, stat.shape)
+
+
+def head_call(rows, head, real):
+    number, wide = rows.shape[0], head.shape[0]
+    return pl.pallas_call(
+        functools.partial(head_kernel, real),
+        grid=(number // 256,),
+        out_shape=(
+            jax.ShapeDtypeStruct((number, EXT), jnp.bfloat16),
+            jax.ShapeDtypeStruct((number, wide), jnp.bfloat16),
+            jax.ShapeDtypeStruct((number, 128), jnp.float32),
+        ),
+        in_specs=[
+            pl.BlockSpec((256, D), lambda i: (i, 0)),
+            pl.BlockSpec((wide, D), lambda i: (0, 0)),
+        ],
+        out_specs=(
+            pl.BlockSpec((256, EXT), lambda i: (i, 0)),
+            pl.BlockSpec((256, wide), lambda i: (i, 0)),
+            pl.BlockSpec((256, 128), lambda i: (i, 0)),
+        ),
+        compiler_params=pltpu.CompilerParams(vmem_limit_bytes=VMEM_LIMIT),
+        name="head_forward",
+    )(rows, head)
+
+
+def head_grad_kernel(rows, kept, stat, info, out):
+    weight = info[:, 0:1]
+    factor = weight * jnp.exp(stat[:, 0:1] - info[:, 1:2])
+    col = iota(kept.shape, 1)
+    hit = col == info[:, 2:3].astype(jnp.int32)
+    grad = low(jnp.where(hit, weight, 0.0) - high(kept[...]) * factor)
+
+    @pl.when(pl.program_id(0) == 0)
+    def _():
+        out[...] = jnp.zeros(out.shape, jnp.float32)
+
+    out[...] += dot_tn(grad, rows[...])
+
+
+def head_grad_call(rows, kept, stat, info):
+    number, wide = kept.shape
+    return pl.pallas_call(
+        head_grad_kernel,
+        grid=(number // 256,),
+        out_shape=jax.ShapeDtypeStruct((wide, D), jnp.float32),
+        in_specs=[
+            pl.BlockSpec((256, D), lambda i: (i, 0)),
+            pl.BlockSpec((256, wide), lambda i: (i, 0)),
+            pl.BlockSpec((256, 128), lambda i: (i, 0)),
+            pl.BlockSpec((256, 128), lambda i: (i, 0)),
+        ],
+        out_specs=pl.BlockSpec((wide, D), lambda i: (0, 0)),
+        compiler_params=pltpu.CompilerParams(vmem_limit_bytes=VMEM_LIMIT),
+        name="head_grad",
+    )(rows, kept, stat, info)
+
+
+def backward_kernel(owner, coord, lens, refs, x, gains, cos_q, sin_q, cos_k, sin_k, *rest):
+    a, ap, q, k, v, o, h1, b, gate, up, z, h2, c = rest[:13]
+    truth, wanted, u0, u1, u2, u3 = rest[13:19]
+    parts = rest[19:27]
+    act, dx_out, gain_out, info_out, loss_out = rest[27:32]
+    held, sem, dk_acc = rest[32:]
+    start_weights(coord, parts, held, sem)
+    valid, chosen = masks(lens)
+    select = jnp.where(chosen, 1.0, 0.0).astype(jnp.bfloat16)
+    act[AT_A:AT_DK] = a[...]
+    act[AT_AP:AT_DQ] = ap[...]
+    act[AT_O:AT_DO] = o[...]
+    act[AT_B:AT_Z] = b[...]
+    for r in range(FF // D):
+        act[AT_Z + r * PAIR_ROWS : AT_Z + (r + 1) * PAIR_ROWS] = z[:, r * D : (r + 1) * D]
+    top, total, mixed = merge([unpack(part[...]) for part in (u0, u1, u2, u3)])
+    norm = top + jnp.log(total)
+    target = high(truth[...])
+    picked = jnp.sum(high(c[...]) * target, axis=-1, keepdims=True)
+    scored = wanted[:, 0:1]
+    terms = (picked - norm) * scored
+    seq = iota((PAIR_ROWS, 1), 0) >> 4
+    logp = [jnp.sum(jnp.where(seq == n, terms, 0.0), axis=0, keepdims=True) for n in range(2 * MB)]
+    weight = jnp.zeros((PAIR_ROWS, 1), jnp.float32)
+    loss = jnp.zeros((1, 1), jnp.float32)
+    for n in range(MB):
+        margin = DPO_BETA * ((logp[2 * n] - refs[2 * n]) - (logp[2 * n + 1] - refs[2 * n + 1]))
+        loss = loss + jnp.maximum(-margin, 0.0) + jnp.log1p(jnp.exp(-jnp.abs(margin)))
+        slope = -DPO_BETA * jax.nn.sigmoid(-margin)
+        weight = jnp.where(seq == 2 * n, slope, jnp.where(seq == 2 * n + 1, -slope, weight))
+    weight = weight * scored
+    loss_out[...] = jnp.broadcast_to(loss, loss_out.shape)
+    lane = iota((PAIR_ROWS, 128), 1)
+    info_out[...] = jnp.where(
+        lane == 0, weight, jnp.where(lane == 1, norm, jnp.where(lane == 2, wanted[:, 1:2], 0.0))
+    )
+    grad_c = weight * (target - mixed / total)
+    d2, gain_top = rms_back(h2[...], gains[2:3, :], grad_c)
+    gain_out[2:3, :] = gain_top
+    d2_low = low(d2)
+    act[AT_DH:ACT_ROWS] = d2_low
+    wait_weights(held, sem)
+    grad_b = jnp.zeros((PAIR_ROWS, D), jnp.float32)
+    for r in range(FF // D):
+        grad_mix = dot_nt(d2_low[:, :BC], held[owner[24 + 2 * r]]) + dot_nt(
+            d2_low[:, BC:], held[owner[25 + 2 * r]]
+        )
+        at = slice(r * D, (r + 1) * D)
+        gate_pre = gate[:, at]
+        sig = jax.nn.sigmoid(gate_pre)
+        d_gate = low(grad_mix * up[:, at] * sig * (1.0 + gate_pre * (1.0 - sig)))
+        d_up = low(grad_mix * gate_pre * sig)
+        act[AT_DGATE + r * PAIR_ROWS : AT_DGATE + (r + 1) * PAIR_ROWS] = d_gate
+        act[AT_DUP + r * PAIR_ROWS : AT_DUP + (r + 1) * PAIR_ROWS] = d_up
+        for j in range(2):
+            cut = slice(j * BC, (j + 1) * BC)
+            grad_b = grad_b + dot_nt(d_gate[:, cut], held[owner[8 + 2 * r + j]])
+            grad_b = grad_b + dot_nt(d_up[:, cut], held[owner[16 + 2 * r + j]])
+    back, gain_mid = rms_back(h1[...], gains[1:2, :], grad_b)
+    gain_out[1:2, :] = gain_mid
+    d1 = d2 + back
+    d1_low = low(d1)
+    act[AT_DO:AT_B] = d1_low
+    d_att = low(
+        dot_nt(d1_low[:, :BC], held[owner[6]]) + dot_nt(d1_low[:, BC:], held[owner[7]])
+    )
+    lane_k = iota((TOKENS, 128), 1)
+    zero_k = jnp.zeros((TOKENS, 128), jnp.bfloat16)
+    zero_q = jnp.zeros((PAIR_ROWS, 128), jnp.bfloat16)
+    root = 1.0 / math.sqrt(HDIM)
+    for p in range(HEADS // 2):
+        at = slice(p * 128, (p + 1) * 128)
+        d_q = jnp.zeros((PAIR_ROWS, 128), jnp.float32)
+        d_k = jnp.zeros((TOKENS, 128), jnp.float32)
+        d_v = jnp.zeros((TOKENS, 128), jnp.float32)
+        for h in range(2):
+            mine_k = (lane_k >> 6) == h
+            mine_q = (lane >> 6) == h
+            k_one = jnp.where(mine_k, k[:, at], zero_k)
+            q_one = jnp.where(mine_q, q[:, at], zero_q)
+            do_one = jnp.where(mine_q, d_att[:, at], zero_q)
+            s = dot_nt(q_one, k_one) * root
+            s = jnp.where(valid, s, MASKED)
+            e = jnp.exp(s - jnp.max(s, axis=-1, keepdims=True))
+            prob = e / jnp.sum(e, axis=-1, keepdims=True)
+            d_p = dot_nt(do_one, v[:, at])
+            d_s = low(prob * (d_p - jnp.sum(prob * d_p, axis=-1, keepdims=True)))
+            d_q = d_q + dot_nn(d_s, k_one)
+            d_k = d_k + dot_tn(d_s, q_one)
+            d_v = d_v + dot_tn(low(prob), do_one)
+        act[AT_DQ:AT_O, at] = low(turn(d_q * root, cos_q[...], sin_q[...], -1.0))
+        act[AT_DK:AT_DV, at] = low(turn(d_k * root, cos_k[...], sin_k[...], -1.0))
+        act[AT_DV:AT_AP, at] = low(d_v)
+    d_q_all = low(dot_tn(select, act[AT_DQ:AT_O]))
+    grad_a = jnp.zeros((TOKENS, D), jnp.float32)
+    for j in range(2):
+        cut = slice(j * BC, (j + 1) * BC)
+        grad_a = grad_a + dot_nt(d_q_all[:, cut], held[owner[j]])
+        grad_a = grad_a + dot_nt(act[AT_DK:AT_DV, cut], held[owner[2 + j]])
+        grad_a = grad_a + dot_nt(act[AT_DV:AT_AP, cut], held[owner[4 + j]])
+    back_in, gain_in = rms_back(high(x[...]), gains[0:1, :], grad_a)
+    gain_out[0:1, :] = gain_in
+    rest_low = low(d1 - high(d1_low))
+    dx_out[...] = low(back_in + dot_tn(select, d1_low) + dot_tn(select, rest_low))
+
+
+def backward_call(owner, coord, lens, refs, x, gains, turns, saved, truth, wanted, parts_u, parts):
+    return pl.pallas_call(
+        backward_kernel,
+        out_shape=(
+            jax.ShapeDtypeStruct((ACT_ROWS, D), jnp.bfloat16),
+            jax.ShapeDtypeStruct((TOKENS, D), jnp.bfloat16),
+            jax.ShapeDtypeStruct((3, D), jnp.float32),
+            jax.ShapeDtypeStruct((PAIR_ROWS, 128), jnp.float32),
+            jax.ShapeDtypeStruct((1, 128), jnp.float32),
+        ),
+        in_specs=smem(4) + vmem(6 + 13 + 2 + 4) + anywhere(8),
+        out_specs=tuple(vmem(5)),
+        scratch_shapes=[
+            pltpu.VMEM((NBLK, D, BC), jnp.bfloat16),
+            pltpu.SemaphoreType.DMA,
+            pltpu.VMEM((8, 128), jnp.float32),
+        ],
+        compiler_params=pltpu.CompilerParams(vmem_limit_bytes=VMEM_LIMIT),
+        name="layer_backward",
+    )(owner, coord, lens, refs, x, gains, *turns, *saved, truth, wanted, *parts_u, *parts)
+
+
+def weight_grad_kernel(block_of, x_at, y_at, coord, mine, theirs, *outs):
+    core = coord[3]
+    for k in range(4):
+        own, one, two, both = outs[4 * k : 4 * k + 4]
+        for x_flip in range(2):
+
+            def step(back, carry):
+                z = (coord[0] + 4 - back) & 3
+                x = coord[1] + x_flip * (1 - 2 * coord[1])
+                slot = 8 * z + 4 * x + k
+                block = block_of[slot]
+                cut = pl.ds(pl.multiple_of((block & 1) * BC, 128), BC)
+                x_row = pl.multiple_of(x_at[slot], 64)
+                y_row = pl.multiple_of(y_at[slot], 64)
+
+                def put(grad):
+                    grad_low = low(grad)
+                    quarter = [grad_low[192 * n : 192 * (n + 1)] for n in range(4)]
+                    even = coord[2] == 0
+                    first = core == 0
+                    near = jnp.where(
+                        even,
+                        jnp.where(first, quarter[0], quarter[1]),
+                        jnp.where(first, quarter[2], quarter[3]),
+                    )
+                    far = jnp.where(
+                        even,
+                        jnp.where(first, quarter[2], quarter[3]),
+                        jnp.where(first, quarter[0], quarter[1]),
+                    )
+                    if x_flip == 0:
+                        own[back] = near
+
+                        @pl.when(first)
+                        def _():
+                            two[back] = far
+
+                        @pl.when(jnp.logical_not(first))
+                        def _():
+                            one[back] = far
+                    else:
+                        both[back] = far
+
+                        @pl.when(first)
+                        def _():
+                            one[back] = near
+
+                        @pl.when(jnp.logical_not(first))
+                        def _():
+                            two[back] = near
+
+                wide = (block >= 2) & (block < 6)
+
+                @pl.when(wide)
+                def _():
+                    left = jnp.concatenate(
+                        [mine[pl.ds(x_row, TOKENS), :], theirs[pl.ds(x_row, TOKENS), :]], axis=0
+                    )
+                    right = jnp.concatenate(
+                        [mine[pl.ds(y_row, TOKENS), cut], theirs[pl.ds(y_row, TOKENS), cut]], axis=0
+                    )
+                    put(dot_tn(left, right))
+
+                @pl.when(jnp.logical_not(wide))
+                def _():
+                    left = jnp.concatenate(
+                        [mine[pl.ds(x_row, PAIR_ROWS), :], theirs[pl.ds(x_row, PAIR_ROWS), :]],
+                        axis=0,
+                    )
+                    right = jnp.concatenate(
+                        [mine[pl.ds(y_row, PAIR_ROWS), cut], theirs[pl.ds(y_row, PAIR_ROWS), cut]],
+                        axis=0,
+                    )
+                    put(dot_tn(left, right))
+
+                return carry
+
+            lax.fori_loop(0, 4, step, 0)
+
+
+def weight_grad_call(block_of, x_at, y_at, coord, mine, theirs):
+    return pl.pallas_call(
+        weight_grad_kernel,
+        out_shape=tuple([jax.ShapeDtypeStruct((4, 192, BC), jnp.bfloat16)] * 16),
+        in_specs=smem(4) + vmem(2),
+        out_specs=tuple(vmem(16)),
+        compiler_params=pltpu.CompilerParams(vmem_limit_bytes=VMEM_LIMIT),
+        name="weight_grads",
+    )(block_of, x_at, y_at, coord, mine, theirs)
+
+
+def shampoo_kernel(coord, own, by_y, by_core, by_both, lstat, rstat, lroot, rroot, blk, new_l, new_r, new_b, whole):
+    y, core = coord[2], coord[3]
+    for piece, y_at, core_at in (
+        (own, y, core),
+        (by_y, 1 - y, core),
+        (by_core, y, 1 - core),
+        (by_both, 1 - y, 1 - core),
+    ):
+        row = pl.multiple_of(192 * (2 * y_at + core_at), 64)
+        whole[pl.ds(row, 192), :] = piece[0]
+    grad = whole[...]
+    new_l[0] = STAT_DECAY * lstat[0] + (1.0 - STAT_DECAY) * dot_nt(grad, grad)
+    new_r[0] = STAT_DECAY * rstat[0] + (1.0 - STAT_DECAY) * dot_tn(grad, grad)
+    turned = dot_nn(low(lroot[0]), grad)
+    new_b[0] = blk[0] - SHAMPOO_RATE * dot_nn(low(turned), low(rroot[0]))
+
+
+def shampoo_call(coord, pieces, lstat, rstat, lroot, rroot, blk):
+    slots = lstat.shape[0]
+
+    def one(rows, columns):
+        return pl.BlockSpec((1, rows, columns), lambda i, coord: (i, 0, 0))
+
+    return pl.pallas_call(
+        shampoo_kernel,
+        grid_spec=pltpu.PrefetchScalarGridSpec(
+            num_scalar_prefetch=1,
+            grid=(slots,),
+            in_specs=[one(192, BC)] * 4
+            + [
+                one(D, D),
+                one(BC, BC),
+                pl.BlockSpec((1, 192, D), lambda i, coord: (i, 2 * coord[2] + coord[3], 0)),
+                one(BC, BC),
+                one(192, BC),
+            ],
+            out_specs=(one(D, D), one(BC, BC), one(192, BC)),
+            scratch_shapes=[pltpu.VMEM((D, BC), jnp.bfloat16)],
+        ),
+        out_shape=(
+            jax.ShapeDtypeStruct(lstat.shape, jnp.float32),
+            jax.ShapeDtypeStruct(rstat.shape, jnp.float32),
+            jax.ShapeDtypeStruct(blk.shape, jnp.float32),
+        ),
+        compiler_params=pltpu.CompilerParams(vmem_limit_bytes=VMEM_LIMIT),
+        name="shampoo",
+    )(coord, *pieces, lstat, rstat, lroot, rroot, blk)
+
+
+def block_rows():
+    x_at, y_at = [], []
+    for b in range(NBLK):
+        if b < 2:
+            x_at.append(AT_AP), y_at.append(AT_DQ)
+        elif b < 4:
+            x_at.append(AT_A), y_at.append(AT_DK)
+        elif b < 6:
+            x_at.append(AT_A), y_at.append(AT_DV)
+        elif b < 8:
+            x_at.append(AT_O), y_at.append(AT_DO)
+        elif b < 16:
+            x_at.append(AT_B), y_at.append(AT_DGATE + (b - 8) // 2 * PAIR_ROWS)
+        elif b < 24:
+            x_at.append(AT_B), y_at.append(AT_DUP + (b - 16) // 2 * PAIR_ROWS)
+        else:
+            x_at.append(AT_Z + (b - 24) // 2 * PAIR_ROWS), y_at.append(AT_DH)
+    return jnp.array(x_at, jnp.int32), jnp.array(y_at, jnp.int32)
+
+
+def per_core(
+    token_ids,
+    lengths,
+    comp_mask,
+    ref_logp,
+    owner,
+    blocks,
+    left_stat,
+    right_stat,
+    left_root,
+    right_root,
+    tables,
+    table_moment,
+    table_second,
+    gains,
+    gain_moment,
+    gain_second,
+):
+    zi, xi, yi, ci = (lax.axis_index(name) for name in AXES)
+    coord = jnp.stack([zi, xi, yi, ci]).astype(jnp.int32)
+    vocab_index = 2 * yi + ci
+    shard = vocab_index * 8 + 2 * zi + xi
+    table_rows = tables.shape[1]
+    vocab = table_rows * 32
+    seqs = 2 * MB
+    shares = blocks.astype(jnp.bfloat16)
+    parts = []
+    for slot in range(4):
+        parts.extend(spread(shares[slot]))
+    first_pair = vocab_index * MB
+    ids = lax.dynamic_slice_in_dim(token_ids, first_pair, MB, 0).reshape(seqs, SLOT)
+    lens = lax.dynamic_slice_in_dim(lengths, first_pair, MB, 0).reshape(seqs)
+    wanted = lax.dynamic_slice_in_dim(comp_mask, first_pair, MB, 0).reshape(PAIR_ROWS)
+    refs = lax.dynamic_slice_in_dim(ref_logp, first_pair, MB, 0).reshape(seqs)
+    places = jnp.arange(SLOT)
+    pos = (lens[:, None] - 1 - CMP + jnp.arange(CMP)[None, :]).astype(jnp.int32)
+    targets = jnp.sum(
+        jnp.where(places[None, None, :] == (pos + 1)[:, :, None], ids[:, None, :], 0), axis=-1
+    ).reshape(PAIR_ROWS)
+    asked = jnp.concatenate([ids.reshape(TOKENS), targets + vocab])
+    used = jnp.concatenate(
+        [(places[None, :] < lens[:, None]).reshape(TOKENS), jnp.ones((PAIR_ROWS,), bool)]
+    )
+    number = jnp.where(asked >= vocab, asked - vocab, asked)
+    holder = number // table_rows
+    local_row = number - holder * table_rows + jnp.where(asked >= vocab, table_rows, 0)
+    total = asked.shape[0]
+    earlier = jnp.arange(total)[None, :] < jnp.arange(total)[:, None]
+    same = (asked[:, None] == asked[None, :]) & used[:, None] & used[None, :]
+    first = used & jnp.logical_not(jnp.any(same & earlier, axis=1))
+    rank = jnp.sum(
+        ((holder[:, None] == holder[None, :]) & earlier & first[None, :]).astype(jnp.int32), axis=1
+    )
+    spill = jnp.any(first & (rank >= CAP))
+    seat_first = jnp.where(first & (rank < CAP), holder * CAP + rank, -1)
+    seat = jnp.sum(jnp.where(same & first[None, :], seat_first[None, :] + 1, 0), axis=1) - 1
+    seats = jnp.arange(32 * CAP)
+    request = jnp.sum(
+        jnp.where(seat_first[:, None] == seats[None, :], local_row[:, None], 0), axis=0
+    )
+    message = jnp.concatenate(
+        [
+            request.reshape(32, CAP),
+            jnp.broadcast_to(spill.astype(jnp.int32), (32, MSG - CAP)),
+        ],
+        axis=1,
+    )
+    message = lax.all_to_all(message, SHARD_AXES, 0, 0, tiled=True)
+    any_spill = jnp.max(message[:, MSG - 1]) > 0
+    asked_rows = message[:, :CAP].reshape(32 * CAP)
+    table_low = tables.astype(jnp.bfloat16).reshape(2 * table_rows, D)
+    give = (asked_rows[:, None] == jnp.arange(2 * table_rows)[None, :]).astype(jnp.bfloat16)
+    given = low(dot_nn(give, table_low))
+    got = lax.all_to_all(given, SHARD_AXES, 0, 0, tiled=True)
+    place = (seat[:, None] == seats[None, :]).astype(jnp.bfloat16)
+    quick = low(dot_nn(place, got))
+    all_targets = jnp.sum(
+        jnp.where(
+            places[None, None, None, :]
+            == (lengths[:, :, None] - CMP + jnp.arange(CMP)[None, None, :])[:, :, :, None],
+            token_ids[:, :, None, :],
+            0,
+        ),
+        axis=-1,
+    )
+
+    def rows_slow():
+        gathered = lax.all_gather(table_low.reshape(2, table_rows, D), ("z", "x"), axis=1, tiled=True)
+        held_rows = gathered.shape[1]
+
+        def find(table, wanted_ids):
+            local = wanted_ids - vocab_index * held_rows
+            inside = (local >= 0) & (local < held_rows)
+            rows = jnp.take(table, jnp.clip(local, 0, held_rows - 1), axis=0)
+            return jnp.where(inside[:, None], rows, 0)
+
+        found = jnp.concatenate(
+            [
+                find(gathered[0], token_ids.reshape(-1)).reshape(-1, TOKENS, D),
+                find(gathered[1], all_targets.reshape(-1)).reshape(-1, PAIR_ROWS, D),
+            ],
+            axis=1,
+        )
+        summed = lax.psum(found.astype(jnp.float32), ("y", "core")).astype(jnp.bfloat16)
+        return lax.dynamic_index_in_dim(summed, vocab_index, 0, keepdims=False)
+
+    rows = lax.cond(any_spill, rows_slow, lambda: quick)
+    x, truth = rows[:TOKENS], rows[TOKENS:]
+    inv_freq = ROPE_BASE ** (-jnp.arange(HDIM // 2).astype(jnp.float32) * 2.0 / HDIM)
+    phase = places.astype(jnp.float32)[:, None] * inv_freq[None, :]
+    phase_pick = pos.reshape(PAIR_ROWS).astype(jnp.float32)[:, None] * inv_freq[None, :]
+
+    def turning(angle, repeat):
+        cosine, sine = jnp.cos(angle), jnp.sin(angle)
+        return (
+            jnp.tile(jnp.concatenate([cosine] * 4, axis=1), (repeat, 1)),
+            jnp.tile(jnp.concatenate([-sine, sine, -sine, sine], axis=1), (repeat, 1)),
+        )
+
+    turns = turning(phase_pick, 1) + turning(phase, seqs)
+    saved = forward_call(owner, coord, lens, x, gains, turns, parts)
+    plane, other = spread(saved[-1])
+    head_rows = jnp.concatenate([plane, other]).reshape(-1, D)
+    wide = -(-table_rows // 128) * 128
+    head_low = jnp.pad(table_low[table_rows:], ((0, wide - table_rows), (0, 0)))
+    ext, kept, stat = head_call(head_rows, head_low, table_rows)
+    half = ext.shape[0] // 2
+    ext = merge_call(ext[:half], hop_core(ext[half:])).reshape(4, 4 * PAIR_ROWS, EXT)
+    one = merge_call(ext[1], hop_two(ext[3]))
+    ext = merge_call(ext[0], hop_one(one), hop_two(ext[2])).reshape(4, PAIR_ROWS, EXT)
+    parts_u = [ext[0]] + [ring(ext[step], -step) for step in range(1, 4)]
+    marks = jnp.stack([wanted.astype(jnp.float32), targets.astype(jnp.float32)], axis=1)
+    marks = jnp.pad(marks, ((0, 0), (0, 126)))
+    act, dx, gain_part, info, loss_part = backward_call(
+        owner, coord, lens, refs, x, gains, turns, saved, truth, marks, parts_u, parts
+    )
+    inverse = jnp.sum(
+        jnp.where(
+            owner[None, :] == jnp.arange(NBLK)[:, None], jnp.arange(NBLK, dtype=jnp.int32)[None, :], 0
+        ),
+        axis=1,
+    )
+    x_at, y_at = block_rows()
+    chosen = (inverse[:, None] == jnp.arange(NBLK)[None, :]).astype(jnp.int32)
+    grads = weight_grad_call(
+        inverse,
+        jnp.sum(chosen * x_at[None, :], axis=1),
+        jnp.sum(chosen * y_at[None, :], axis=1),
+        coord,
+        act,
+        hop_core(act),
+    )
+    share_list, wholes = [], []
+    for slot in range(4):
+        own, one, two, both = grads[4 * slot : 4 * slot + 4]
+        one = low(high(one) + high(hop_two(both)))
+        one = hop_one(one)
+        two = hop_two(two)
+        line = [low(high(own[n]) + high(one[n]) + high(two[n])) for n in range(4)]
+        share = high(line[0])
+        for step in range(1, 4):
+            share = share + high(ring(line[step], -step))
+        share_list.append(share)
+    block_grads = jnp.stack(share_list)
+    near = block_grads.astype(jnp.bfloat16)
+    by_y = hop_y(near)
+    pair = hop_core(jnp.stack([near, by_y]))
+    new_left, new_right, new_blocks = shampoo_call(
+        coord, (near, by_y, pair[0], pair[1]), left_stat, right_stat, left_root, right_root, blocks
+    )
+    told = jnp.concatenate(
+        [
+            info[:, :3].reshape(-1),
+            gain_part.reshape(-1),
+            loss_part[0, :1],
+            jnp.zeros((63,), jnp.float32),
+        ]
+    )
+    heard = lax.all_to_all(
+        jnp.broadcast_to(told[None], (32, told.shape[0])), AXES, 0, 0, tiled=True
+    )
+    summed = jnp.sum(heard[:, 3 * PAIR_ROWS :], axis=0)
+    gain_grad = summed[: 3 * D].reshape(3, D)
+    loss_sum = summed[3 * D]
+    sources = []
+    for other_core in range(2):
+        for rel in range(4):
+            for back in range(4):
+                sources.append(flat_of(*source_of((zi, xi, yi, ci), other_core, rel, back)))
+    sources = jnp.stack(sources)
+    infos = jnp.sum(
+        jnp.where(
+            (sources[:, None] == jnp.arange(32)[None, :])[:, :, None],
+            heard[None, :, : 3 * PAIR_ROWS],
+            0.0,
+        ),
+        axis=1,
+    ).reshape(-1, 3)
+    infos = jnp.concatenate(
+        [infos[:, :2], infos[:, 2:3] - (shard * table_rows).astype(jnp.float32)], axis=1
+    )
+    infos = jnp.pad(infos, ((0, 0), (0, 125)))
+    grad_head = head_grad_call(head_rows, kept, stat, infos)[:table_rows]
+    place_x = place[:TOKENS]
+    sent = low(dot_tn(place_x, dx))
+    back_rows = lax.all_to_all(sent, SHARD_AXES, 0, 0, tiled=True)
+    take_back = (asked_rows[None, :] == jnp.arange(table_rows)[:, None]).astype(jnp.bfloat16)
+
+    def embed_slow():
+        all_dx = lax.all_gather(dx, ("y", "core"), axis=0, tiled=True).astype(jnp.float32)
+        held_rows = table_rows * 8
+        local = token_ids.reshape(-1) - vocab_index * held_rows
+        inside = (local >= 0) & (local < held_rows)
+        grad = (
+            jnp.zeros((held_rows, D), jnp.float32)
+            .at[jnp.clip(local, 0, held_rows - 1)]
+            .add(jnp.where(inside[:, None], all_dx, 0.0))
+        )
+        return lax.psum_scatter(grad, ("z", "x"), scatter_dimension=0, tiled=True)
+
+    grad_embed = lax.cond(any_spill, embed_slow, lambda: dot_nn(take_back, back_rows))
+    new_embed = adam_step(tables[0], grad_embed, table_moment[0], table_second[0], 0.3)
+    new_head = adam_step(tables[1], grad_head, table_moment[1], table_second[1], 0.02)
+    new_tables, new_table_moment, new_table_second = (
+        jnp.stack([e, h]) for e, h in zip(new_embed, new_head)
+    )
+    new_gains, new_gain_moment, new_gain_second = adam_step(
+        gains, gain_grad, gain_moment, gain_second, GAIN_RATE
+    )
+    return (
+        new_blocks,
+        block_grads,
+        new_left,
+        new_right,
+        new_tables,
+        new_table_moment,
+        new_table_second,
+        new_gains,
+        new_gain_moment,
+        new_gain_second,
+        loss_sum,
+    )
+
+
 def solution(mesh):
+    tuned = mesh.shape["dp"] == 8 and mesh.shape["vocab"] == 4
+    if tuned:
+        dp, vocab = ("z", "x"), ("y", "core")
+        where = Mesh(mesh.devices.reshape(4, 2, 2, 2), AXES)
+        body = per_core
+    else:
+        dp, vocab = ("dp",), ("vocab",)
+        where = mesh
+        body = per_device
     placed = (
-        P("dp", None, None),
-        P("dp", None),
-        P("dp", None, None),
-        P("dp", None),
+        P(dp, None, None),
+        P(dp, None),
+        P(dp, None, None),
+        P(dp, None),
         P(),
-        P("dp", "vocab", None),
-        P("dp", None, None),
-        P("dp", None, None),
-        P("dp", None, None),
-        P("dp", None, None),
-        P(None, ("vocab", "dp"), None),
-        P(None, ("vocab", "dp"), None),
-        P(None, ("vocab", "dp"), None),
+        P(dp, vocab, None),
+        P(dp, None, None),
+        P(dp, None, None),
+        P(dp, None, None),
+        P(dp, None, None),
+        P(None, vocab + dp, None),
+        P(None, vocab + dp, None),
+        P(None, vocab + dp, None),
         P(),
         P(),
         P(),
     )
     return jax.shard_map(
-        per_device,
-        mesh=mesh,
+        body,
+        mesh=where,
         in_specs=placed,
         out_specs=(
-            P("dp", "vocab", None),
-            P("dp", "vocab", None),
-            P("dp", None, None),
-            P("dp", None, None),
-            P(None, ("vocab", "dp"), None),
-            P(None, ("vocab", "dp"), None),
-            P(None, ("vocab", "dp"), None),
+            P(dp, vocab, None),
+            P(dp, vocab, None),
+            P(dp, None, None),
+            P(dp, None, None),
+            P(None, vocab + dp, None),
+            P(None, vocab + dp, None),
+            P(None, vocab + dp, None),
             P(),
             P(),
             P(),

time: 2540 us -> 565 us (0.22)
  waiting for transfers between devices: 1820 us -> 187 us
  local copies, waits for them, and re-layouts: 225 us -> 30.9 us
  matrix products: 196 us -> 13.2 us
  starting transfers between devices: 1.09 us -> 124 us
  Pallas kernels: 0 us -> 106 us
  other arithmetic: 175 us -> 69.6 us
  blocking collectives: 87.4 us -> 0 us
    all_gather x5 -> x0, waiting for transfers between devices: 827 us -> none  [the longest x1 459 us: per_device(): lax.all_gather(tables.astype(jnp.bfloat16), 'dp', axis=1, tiled=True)]
    unnamed x13 -> x0, waiting for transfers between devices: 712 us -> none
    reduce_scatter x4 -> x0, waiting for transfers between devices: 285 us -> none  [the longest x1 271 us: per_device(): lax.psum_scatter(slotted.astype(jnp.bfloat16), 'dp', scatter_dimension=0,...]
    dot_general x56 -> x4, matrix products: 196 us -> 13.2 us  [the longest x3 10.6 us: dot_nn(): lax.dot_general(left, right, (((1,), (0,)), ((), ())), preferred_element_...]
    ppermute x0 -> x69, waiting for transfers between devices: none -> 166 us  [the longest x20 86.3 us: hop_two(): lax.ppermute(value, AXES, moves(lambda z, x, y, c: (z, x, 1 - y, c) if c...]
    ppermute x0 -> x69, starting transfers between devices: none -> 107 us  [the longest x30 65.5 us: ring(): lax.ppermute(value, AXES, moves(lambda z, x, y, c: ((z + step) % 4, x, y,...]
    pallas_call x0 -> x9, Pallas kernels: none -> 106 us  [the longest x1 20.3 us: backward_call(): pl.pallas_call(backward_kernel, out_shape=(jax.ShapeDtypeStruct((ACT_ROWS...]
    gather x13 -> x0, local copies, waits for them, and re-layouts: 48.5 us -> none  [the longest x1 14.9 us: per_device(): kept_mats = groups(jnp.take(slots_all, owner, axis=0))]
  transfers between devices with their start and end apart: 11 -> 73, of which waited for: 8 -> 33; matrix products, arithmetic and copies ran while one was open for 10% -> 16% of each run, Pallas kernels for 0% -> 6%
where the time goes in v1:
time: 565 us; the launch traced here: 556 us
  waiting for transfers between devices  187 us (33%)
  starting transfers between devices  124 us (22%)
  Pallas kernels  106 us (19%)
  other arithmetic  69.6 us (12%)
  local copies, waits for them, and re-layouts  30.9 us (5%)
  between operations  16.5 us (3%)
  matrix products  13.2 us (2%)
  loops' own time  8.3 us (1%)
    ppermute x20, waiting for transfers between devices, hop_two(): lax.ppermute(value, AXES, moves(lambda z, x, y, c: (z, x, 1 - y, c) if c...  86.3 us
    ppermute x30, starting transfers between devices, ring(): lax.ppermute(value, AXES, moves(lambda z, x, y, c: ((z + step) % 4, x, y,...  65.5 us
    ppermute x30, waiting for transfers between devices, ring(): lax.ppermute(value, AXES, moves(lambda z, x, y, c: ((z + step) % 4, x, y,...  50.1 us
    ppermute x20, starting transfers between devices, hop_two(): lax.ppermute(value, AXES, moves(lambda z, x, y, c: (z, x, 1 - y, c) if c...  25.2 us
    another operation x4, other arithmetic, per_core(): jnp.stack([e, h])  24.7 us
    ppermute x10, waiting for transfers between devices, hop_one(): lax.ppermute(value, AXES, moves(lambda z, x, y, c: (z, 1 - x, y, c) if c...  23.8 us
    pallas_call x1, Pallas kernels, backward_call(): pl.pallas_call(backward_kernel, out_shape=(jax.ShapeDtypeStruct((ACT_ROWS...  20.3 us
    pallas_call x1, Pallas kernels, weight_grad_call(): pl.pallas_call(weight_grad_kernel, out_shape=tuple([jax.ShapeDtypeStruct(...  19.8 us
  transfers between devices with their start and end apart: 73, of which 33 were waited for; matrix products, arithmetic and copies ran while one was open for 16% of the time, Pallas kernels for 6%

profile of v1, /device:TPU:0, one launch (start us, length us, event | category | flops | bytes accessed | tf_op | source)
XLA Modules:
  0.0 555.8 jit_solution(1159540345786300287)
XLA Ops:
  22.4 7.2 %collective-permute-done.22 = bf16[192,384]{1,0:T(8,128)(2,1)S(1)} collective-permute-done((bf16[192,384]{1,0:T(8,128)(2,1)S(1)}, bf16[192,384]{1,0:T(8,128)(2,1)S(1)}, u32[]{:S(2)}, u32[]{:S(2)}) %collective-permute-start.22) | collective-permute-done | bytes 147488 | tf_op jit(solution)/shard_map/ppermute | solution.py:529
  67.8 5.1 all-to-all-start
  76.0 14.3 %all-to-all-done = s32[32,1,32]{2,1,0:T(1,128)S(1)} async-done(((s32[32,1,32]{2,1,0:T(1,128)}), s32[32,1,32]{2,1,0:T(1,128)S(1)}, u32[]{:S(2)}, u32[]{:S(2)}) %all-to-all-start) | async-done | bytes 4128 | tf_op jit(solution)/shard_map/all_to_all | solution.py:1211
  101.9 5.2 all-to-all-start.1
  111.1 13.3 %collective-permute-done.26 = bf16[4,192,384]{2,1,0:T(8,128)(2,1)} collective-permute-done((bf16[4,192,384]{2,1,0:T(8,128)(2,1)}, bf16[4,192,384]{2,1,0:T(8,128)(2,1)}, u32[]{:S(2)}, u32[]{:S(2)}) %collective-permute-start.26) | collective-permute-done | bytes 589856 | tf_op jit(solution)/shard_map/ppermute | solution.py:513
  146.8 6.3 %collective-permute-done.5 = bf16[4,192,384]{2,1,0:T(8,128)(2,1)S(1)} collective-permute-done((bf16[4,192,384]{2,1,0:T(8,128)(2,1)}, bf16[4,192,384]{2,1,0:T(8,128)(2,1)S(1)}, u32[]{:S(2)}, u32[]{:S(2)}) %collective-permute-start.5) | collective-permute-done | bytes 589856 | tf_op jit(solution)/shard_map/ppermute | solution.py:513
  162.1 8.2 %conditional.2 = (bf16[320,768]{1,0:T(8,128)(2,1)S(1)}, bf16[256,768]{1,0:T(8,128)(2,1)S(1)}, bf16[64,768]{1,0:T(8,128)(2,1)S(1)}) conditional(s32[]{:T(128)} %convert_element_type.513, bf16[320,768]{1,0:T(8,128)(2,1)S(1)} %convolution_convert_fusion.1, (s32[]{:T(128)}, s32[8,2,64]{2,1,0:T(2,128)S(1)}, bf16[2,1000,768]{2,1,0:T(8,128)(2,1)}, ...), branch_computations={%region_10.11_spmd, %region_11.14_spmd} | conditional | flops 6951700 | bytes 154861824 | solution.py:1250
  171.7 15.2 %layer_forward.1 = (bf16[256,768]{1,0:T(8,128)(2,1)}, bf16[64,768]{1,0:T(8,128)(2,1)}, bf16[64,768]{1,0:T(8,128)(2,1)}, bf16[256,768]{1,0:T(8,128)(2,1)}, bf16[2...) custom-call(s32[32]{0:T(128)} %owner.3, ...), custom_call_target="tpu_custom_call" | custom-call | tf_op jit(solution)/shard_map/layer_forward/pallas_call | solution.py:705
  186.9 4.6 collective-permute-start.28
  194.9 4.6 collective-permute-done.29
  202.1 9.8 %collective-permute-done.31 = bf16[4,64,768]{2,1,0:T(8,128)(2,1)S(1)} collective-permute-done((bf16[4,64,768]{2,1,0:T(8,128)(2,1)S(1)}, bf16[4,64,768]{2,1,0:T(8,128)(2,1)S(1)}, u32[]{:S(2)}, u32[]{:S(2)}) %collective-permute-start.31) | collective-permute-done | bytes 393248 | tf_op jit(solution)/shard_map/ppermute | solution.py:505
  213.2 6.6 %collective-permute-done.33 = bf16[4,64,768]{2,1,0:T(8,128)(2,1)S(1)} collective-permute-done((bf16[4,64,768]{2,1,0:T(8,128)(2,1)S(1)}, bf16[4,64,768]{2,1,0:T(8,128)(2,1)S(1)}, u32[]{:S(2)}, u32[]{:S(2)}) %collective-permute-start.33) | collective-permute-done | bytes 393248 | tf_op jit(solution)/shard_map/ppermute | solution.py:513
  225.2 14.6 %head_forward.1 = (bf16[2048,896]{1,0:T(8,128)(2,1)}, bf16[2048,1024]{1,0:T(8,128)(2,1)}, f32[2048,128]{1,0:T(8,128)}) custom-call(bf16[2048,768]{1,0:T(8,128)(2,1)} %bitcast.275, bf16[1024,768]{1,0:T(8,128)(2,1)} %pad.15.head), custom_call_target="tpu_custom_call" | custom-call | tf_op jit(solution)/shard_map/head_forward/pallas_call | solution.py:802
  248.4 5.1 merge_parts.3
  258.1 6.5 %collective-permute-done.36.refs_1_ = bf16[256,896]{1,0:T(8,128)(2,1)S(1)} collective-permute-done((bf16[256,896]{1,0:T(8,128)(2,1)S(1)}, bf16[256,896]{1,0:T(8,128)(2,1)S(1)}, u32[]{:S(2)}, u32[]{:S(2)}) %collective-permute-start.36) | collective-permute-done | bytes 458784 | tf_op jit(solution)/shard_map/ppermute | solution.py:513
  269.6 6.9 %collective-permute-done.37.refs_1_ = bf16[256,896]{1,0:T(8,128)(2,1)S(1)} collective-permute-done((bf16[256,896]{1,0:T(8,128)(2,1)}, bf16[256,896]{1,0:T(8,128)(2,1)S(1)}, u32[]{:S(2)}, u32[]{:S(2)}) %collective-permute-start.37) | collective-permute-done | bytes 458784 | tf_op jit(solution)/shard_map/ppermute | solution.py:505
  289.7 5.6 %collective-permute-done.40.rest_17_ = bf16[64,896]{1,0:T(8,128)(2,1)S(1)} collective-permute-done((bf16[64,896]{1,0:T(8,128)(2,1)S(1)}, bf16[64,896]{1,0:T(8,128)(2,1)S(1)}, u32[]{:S(2)}, u32[]{:S(2)}) %collective-permute-start.40) | collective-permute-done | bytes 114720 | tf_op jit(solution)/shard_map/ppermute | solution.py:529
  296.0 20.3 %layer_backward.1 = (bf16[1920,768]{1,0:T(8,128)(2,1)}, bf16[256,768]{1,0:T(8,128)(2,1)}, f32[3,768]{1,0:T(4,128)}, f32[64,128]{1,0:T(8,128)}, f32[1,128]{1,0:T(1,128)}) custom-call(s32[32]{0:T(128)} %owner.3, s32[4]{0:T(128)} %pad_add_fusion.coord, s32[4]{0:T(128)} %copy-done.55, f32[4]{0:T(128)} %reshape.677.refs, ...), custom_call_target="tpu_custom_call" | custom-call | tf_op jit(solution)/shard_map/layer_backward/pallas_call | solution.py:963
  329.3 7.0 %all-to-all-done.3 = f32[32,1,2560]{2,1,0:T(1,128)} async-done(((f32[32,1,2560]{2,1,0:T(1,128)}), f32[32,1,2560]{2,1,0:T(1,128)}, u32[]{:S(2)}, u32[]{:S(2)}) %all-to-all-start.3) | async-done | bytes 327712 | tf_op jit(solution)/shard_map/all_to_all | solution.py:1322
  343.2 19.8 %weight_grads.1 = (bf16[4,192,384]{2,1,0:T(8,128)(2,1)}, bf16[4,192,384]{2,1,0:T(8,128)(2,1)}, bf16[4,192,384]{2,1,0:T(8,128)(2,1)}, bf16[4,192,384]{2,1,0:T(8,1...) custom-call(s32[32]{0:T(128)} %copy-done.56, ...), custom_call_target="tpu_custom_call" | custom-call | tf_op jit(solution)/shard_map/weight_grads/pallas_call | solution.py:1065
  382.6 7.1 %collective-permute-done.55 = bf16[4,192,384]{2,1,0:T(8,128)(2,1)S(1)} collective-permute-done((bf16[4,192,384]{2,1,0:T(8,128)(2,1)}, bf16[4,192,384]{2,1,0:T(8,128)(2,1)S(1)}, u32[]{:S(2)}, u32[]{:S(2)}) %collective-permute-start.55) | collective-permute-done | bytes 589856 | tf_op jit(solution)/shard_map/ppermute | solution.py:513
  392.6 9.8 %collective-permute-done.45 = bf16[4,192,384]{2,1,0:T(8,128)(2,1)S(1)} collective-permute-done((bf16[4,192,384]{2,1,0:T(8,128)(2,1)}, bf16[4,192,384]{2,1,0:T(8,128)(2,1)S(1)}, u32[]{:S(2)}, u32[]{:S(2)}) %collective-permute-start.45) | collective-permute-done | bytes 589856 | tf_op jit(solution)/shard_map/ppermute | solution.py:513
  404.4 13.4 %collective-permute-done.61 = bf16[4,192,384]{2,1,0:T(8,128)(2,1)S(1)} collective-permute-done((bf16[4,192,384]{2,1,0:T(8,128)(2,1)}, bf16[4,192,384]{2,1,0:T(8,128)(2,1)S(1)}, u32[]{:S(2)}, u32[]{:S(2)}) %collective-permute-start.61) | collective-permute-done | bytes 589856 | tf_op jit(solution)/shard_map/ppermute | solution.py:513
  449.7 5.5 collective-permute-start.60
  455.2 8.9 %collective-permute-done.53 = bf16[192,384]{1,0:T(8,128)(2,1)S(1)} collective-permute-done((bf16[192,384]{1,0:T(8,128)(2,1)S(1)}, bf16[192,384]{1,0:T(8,128)(2,1)S(1)}, u32[]{:S(2)}, u32[]{:S(2)}) %collective-permute-start.53) | collective-permute-done | bytes 147488 | tf_op jit(solution)/shard_map/ppermute | solution.py:529
  470.3 7.0 %collective-permute-done.59 = bf16[192,384]{1,0:T(8,128)(2,1)S(1)} collective-permute-done((bf16[192,384]{1,0:T(8,128)(2,1)S(1)}, bf16[192,384]{1,0:T(8,128)(2,1)S(1)}, u32[]{:S(2)}, u32[]{:S(2)}) %collective-permute-start.59) | collective-permute-done | bytes 147488 | tf_op jit(solution)/shard_map/ppermute | solution.py:529
  487.6 12.1 %head_grad.1 = f32[1024,768]{1,0:T(8,128)} custom-call(bf16[2048,768]{1,0:T(8,128)(2,1)} %bitcast.276, bf16[2048,1024]{1,0:T(8,128)(2,1)} %get-tuple-element.147.kept, f32[2048,128]{1,0:T(8,128)} %get-tuple-element.148.stat, f32[2048,128]{1,0:T(8,128)} %select_maximum_fusion.info), custom_call_target="tpu_custom_call" | custom-call | tf_op jit(solution)/shard_map/head_grad/pallas_call | solution.py:840
  500.4 5.0 conditional.3
  500.4 4.9 fusion.74
  507.9 12.3 %fusion.15 = (f32[1,1000,768]{2,1,0:T(8,128)S(1)}, f32[1,1000,768]{2,1,0:T(8,128)S(1)}, f32[1,1000,768]{2,1,0:T(8,128)}, f32[1,1000,768]{2,1,0:T(8,128)S(1)}, f3...) fusion(f32[2,1000,768]{2,1,0:T(8,128)} %param.32, f32[1000,768]{1,0:T(8,128)} %get-tuple-element.244, ...), kind=kLoop, calls=%fused_computation.56 | loop fusion | flops 23040000 | bytes 43008000 | tf_op jit(solution)/shard_map/stack | solution.py:1368
  520.2 6.0 %pad_maximum_fusion.2 = f32[2,1000,768]{2,1,0:T(8,128)} fusion(f32[1,1000,768]{2,1,0:T(8,128)} %get-tuple-element.167, f32[1,1000,768]{2,1,0:T(8,128)} %get-tuple-element.169), kind=kLoop, calls=%fused_computation.39 | loop fusion | flops 1536000 | bytes 12288000 | tf_op jit(solution)/shard_map/stack | solution.py:1368
  535.0 13.8 %shampoo.1 = (f32[4,768,768]{2,1,0:T(8,128)}, f32[4,384,384]{2,1,0:T(8,128)}, f32[4,192,384]{2,1,0:T(8,128)}) custom-call(s32[4]{0:T(128)} %pad_add_fusion.coord, bf16[4,192,384]{2,1,0:T(8,128)(2,1)} %get-tuple-element.157.own, bf16[4,192,384]{2,1,0:T(8,128)(2,1)} %collective-permute-done.67.by_y, bf16[4,192,384]{2,1,0:T(8,128)(2,1)} %get-tuple-element.198.by_core, ...), custom_call_target="tpu_custom_call" | custom-call | tf_op jit(solution)/shard_map/shampoo/pallas_call | solution.py:1098
  (359 shorter events, 252.3 us)
Async XLA Ops:
  16.4 25.7 %collective-permute-start.15 = (bf16[192,384]{1,0:T(8,128)(2,1)S(1)}, bf16[192,384]{1,0:T(8,128)(2,1)S(1)}, u32[]{:S(2)}, u32[]{:S(2)}) collective-permute-start(bf16[192,384]{1,0:T(8,128)(2,1)S(1)} %get-tuple-element.204), channel_id=1, source_target_pairs={{0,16},{1,17},{2,18},{3,19},{4,20},{5,21},{6,22},{7,23},{8,24},{9,... | collective-permute-start | bytes 442376 | tf_op jit(solution)/shard_map/ppermute | solution.py:529
  19.6 26.6 %collective-permute-start.16 = (bf16[192,384]{1,0:T(8,128)(2,1)S(1)}, bf16[192,384]{1,0:T(8,128)(2,1)S(1)}, u32[]{:S(2)}, u32[]{:S(2)}) collective-permute-start(bf16[192,384]{1,0:T(8,128)(2,1)S(1)} %get-tuple-element.204), channel_id=1, source_target_pairs={{0,24},{1,25},{2,26},{3,27},{4,28},{5,29},{6,30},{7,31},{8,0},{9,1... | collective-permute-start | bytes 442376 | tf_op jit(solution)/shard_map/ppermute | solution.py:529
  54.7 37.8 %collective-permute-start.24 = (bf16[4,192,384]{2,1,0:T(8,128)(2,1)}, bf16[4,192,384]{2,1,0:T(8,128)(2,1)}, u32[]{:S(2)}, u32[]{:S(2)}) collective-permute-start(bf16[4,192,384]{2,1,0:T(8,128)(2,1)} %get-tuple-element.200), channel_id=1, source_target_pairs={{0,4},{1,3},{2,6},{3,1},{4,0},{5,7},{6,2},{7,5},{8,12},{9,11},{10,... | collective-permute-start | bytes 1769480 | tf_op jit(solution)/shard_map/ppermute | solution.py:505
  56.2 37.6 %collective-permute-start.25 = (bf16[4,192,384]{2,1,0:T(8,128)(2,1)}, bf16[4,192,384]{2,1,0:T(8,128)(2,1)}, u32[]{:S(2)}, u32[]{:S(2)}) collective-permute-start(bf16[4,192,384]{2,1,0:T(8,128)(2,1)} %get-tuple-element.200), channel_id=1, source_target_pairs={{0,2},{1,5},{2,0},{3,7},{4,6},{5,1},{6,4},{7,3},{8,10},{9,13},{10,... | collective-permute-start | bytes 1769480 | tf_op jit(solution)/shard_map/ppermute | solution.py:513
  58.8 36.5 %collective-permute-start.17 = (bf16[4,192,384]{2,1,0:T(8,128)(2,1)}, bf16[4,192,384]{2,1,0:T(8,128)(2,1)}, u32[]{:S(2)}, u32[]{:S(2)}) collective-permute-start(bf16[4,192,384]{2,1,0:T(8,128)(2,1)} %get-tuple-element.210), channel_id=1, source_target_pairs={{0,4},{1,3},{2,6},{3,1},{4,0},{5,7},{6,2},{7,5},{8,12},{9,11},{10,... | collective-permute-start | bytes 1769480 | tf_op jit(solution)/shard_map/ppermute | solution.py:505
  62.1 33.9 %collective-permute-start.18 = (bf16[4,192,384]{2,1,0:T(8,128)(2,1)}, bf16[4,192,384]{2,1,0:T(8,128)(2,1)}, u32[]{:S(2)}, u32[]{:S(2)}) collective-permute-start(bf16[4,192,384]{2,1,0:T(8,128)(2,1)} %get-tuple-element.210), channel_id=1, source_target_pairs={{0,2},{1,5},{2,0},{3,7},{4,6},{5,1},{6,4},{7,3},{8,10},{9,13},{10,... | collective-permute-start | bytes 1769480 | tf_op jit(solution)/shard_map/ppermute | solution.py:513
  63.6 33.8 %collective-permute-start.10 = (bf16[4,192,384]{2,1,0:T(8,128)(2,1)}, bf16[4,192,384]{2,1,0:T(8,128)(2,1)}, u32[]{:S(2)}, u32[]{:S(2)}) collective-permute-start(bf16[4,192,384]{2,1,0:T(8,128)(2,1)} %get-tuple-element.212), channel_id=1, source_target_pairs={{0,4},{1,3},{2,6},{3,1},{4,0},{5,7},{6,2},{7,5},{8,12},{9,11},{10,... | collective-permute-start | bytes 1769480 | tf_op jit(solution)/shard_map/ppermute | solution.py:505
  67.8 22.5 %all-to-all-start = ((s32[32,1,32]{2,1,0:T(1,128)}), s32[32,1,32]{2,1,0:T(1,128)S(1)}, u32[]{:S(2)}, u32[]{:S(2)}) async-start(s32[32,1,32]{2,1,0:T(1,128)} %bitcast.18), calls=%async_computation.1 | async-start | bytes 32768 | tf_op jit(solution)/shard_map/all_to_all | solution.py:1211
  92.5 43.0 %collective-permute-start.11 = (bf16[4,192,384]{2,1,0:T(8,128)(2,1)}, bf16[4,192,384]{2,1,0:T(8,128)(2,1)}, u32[]{:S(2)}, u32[]{:S(2)}) collective-permute-start(bf16[4,192,384]{2,1,0:T(8,128)(2,1)} %get-tuple-element.212), channel_id=1, source_target_pairs={{0,2},{1,5},{2,0},{3,7},{4,6},{5,1},{6,4},{7,3},{8,10},{9,13},{10,... | collective-permute-start | bytes 1769480 | tf_op jit(solution)/shard_map/ppermute | solution.py:513
  95.3 29.1 %collective-permute-start.26 = (bf16[4,192,384]{2,1,0:T(8,128)(2,1)}, bf16[4,192,384]{2,1,0:T(8,128)(2,1)}, u32[]{:S(2)}, u32[]{:S(2)}) collective-permute-start(bf16[4,192,384]{2,1,0:T(8,128)(2,1)} %collective-permute-done.24), channel_id=1, source_target_pairs={{0,2},{1,5},{2,0},{3,7},{4,6},{5,1},{6,4},{7,3},{8,10},{9,13},{10,... | collective-permute-start | bytes 1769480 | tf_op jit(solution)/shard_map/ppermute | solution.py:513
  96.0 36.3 %collective-permute-start.19 = (bf16[4,192,384]{2,1,0:T(8,128)(2,1)}, bf16[4,192,384]{2,1,0:T(8,128)(2,1)}, u32[]{:S(2)}, u32[]{:S(2)}) collective-permute-start(bf16[4,192,384]{2,1,0:T(8,128)(2,1)} %collective-permute-done.17), channel_id=1, source_target_pairs={{0,2},{1,5},{2,0},{3,7},{4,6},{5,1},{6,4},{7,3},{8,10},{9,13},{10,... | collective-permute-start | bytes 1769480 | tf_op jit(solution)/shard_map/ppermute | solution.py:513
  97.4 42.4 %collective-permute-start.12 = (bf16[4,192,384]{2,1,0:T(8,128)(2,1)}, bf16[4,192,384]{2,1,0:T(8,128)(2,1)}, u32[]{:S(2)}, u32[]{:S(2)}) collective-permute-start(bf16[4,192,384]{2,1,0:T(8,128)(2,1)} %collective-permute-done.10), channel_id=1, source_target_pairs={{0,2},{1,5},{2,0},{3,7},{4,6},{5,1},{6,4},{7,3},{8,10},{9,13},{10,... | collective-permute-start | bytes 1769480 | tf_op jit(solution)/shard_map/ppermute | solution.py:513
  101.9 58.3 %all-to-all-start.1 = ((bf16[32,24,768]{2,1,0:T(8,128)(2,1)}), bf16[32,24,768]{2,1,0:T(8,128)(2,1)}, u32[]{:S(2)}, u32[]{:S(2)}) async-start(bf16[32,24,768]{2,1,0:T(8,128)(2,1)} %bitcast.289), calls=%async_computation.2 | async-start | bytes 2359296 | tf_op jit(solution)/shard_map/all_to_all | solution.py:1217
  110.4 36.4 %collective-permute-start.4 = (bf16[4,192,384]{2,1,0:T(8,128)(2,1)}, bf16[4,192,384]{2,1,0:T(8,128)(2,1)S(1)}, u32[]{:S(2)}, u32[]{:S(2)}) collective-permute-start(bf16[4,192,384]{2,1,0:T(8,128)(2,1)} %get-tuple-element.214), channel_id=1, source_target_pairs={{0,2},{1,5},{2,0},{3,7},{4,6},{5,1},{6,4},{7,3},{8,10},{9,13},{10,... | collective-permute-start | bytes 1769480 | tf_op jit(solution)/shard_map/ppermute | solution.py:513
  124.4 28.7 %collective-permute-start.5 = (bf16[4,192,384]{2,1,0:T(8,128)(2,1)}, bf16[4,192,384]{2,1,0:T(8,128)(2,1)S(1)}, u32[]{:S(2)}, u32[]{:S(2)}) collective-permute-start(bf16[4,192,384]{2,1,0:T(8,128)(2,1)} %collective-permute-done.3), channel_id=1, source_target_pairs={{0,2},{1,5},{2,0},{3,7},{4,6},{5,1},{6,4},{7,3},{8,10},{9,13},{10,... | collective-permute-start | bytes 1769480 | tf_op jit(solution)/shard_map/ppermute | solution.py:513
  132.3 38.0 %collective-permute-start.27 = (bf16[4,4,192,384]{3,2,1,0:T(8,128)(2,1)S(1)}, bf16[4,4,192,384]{3,2,1,0:T(8,128)(2,1)}, u32[]{:S(2)}, u32[]{:S(2)}) collective-permute-start(bf16[4,4,192,384]{3,2,1,0:T(8,128)(2,1)S(1)} %pad_maximum_fusion.6.rest_6_.rest_25_), channel_id=1, source_target_pairs={{0,1},{1,0},{2,3},{3,2},{4,5},{5,4},{6,7},{7,6},{8,9},{9,8},{10,11... | collective-permute-start | bytes 7077896 | tf_op jit(solution)/shard_map/ppermute | solution.py:521
  135.5 34.9 %collective-permute-start.20 = (bf16[4,4,192,384]{3,2,1,0:T(8,128)(2,1)}, bf16[4,4,192,384]{3,2,1,0:T(8,128)(2,1)}, u32[]{:S(2)}, u32[]{:S(2)}) collective-permute-start(bf16[4,4,192,384]{3,2,1,0:T(8,128)(2,1)} %pad_maximum_fusion.5.rest_4_.rest_23_), channel_id=1, source_target_pairs={{0,1},{1,0},{2,3},{3,2},{4,5},{5,4},{6,7},{7,6},{8,9},{9,8},{10,11... | collective-permute-start | bytes 7077896 | tf_op jit(solution)/shard_map/ppermute | solution.py:521
  143.0 27.3 %collective-permute-start.13 = (bf16[4,4,192,384]{3,2,1,0:T(8,128)(2,1)}, bf16[4,4,192,384]{3,2,1,0:T(8,128)(2,1)}, u32[]{:S(2)}, u32[]{:S(2)}) collective-permute-start(bf16[4,4,192,384]{3,2,1,0:T(8,128)(2,1)} %pad_maximum_fusion.4.rest_2_.rest_21_), channel_id=1, source_target_pairs={{0,1},{1,0},{2,3},{3,2},{4,5},{5,4},{6,7},{7,6},{8,9},{9,8},{10,11... | collective-permute-start | bytes 7077896 | tf_op jit(solution)/shard_map/ppermute | solution.py:521
  316.3 24.6 %collective-permute-start.42 = (bf16[1920,768]{1,0:T(8,128)(2,1)}, bf16[1920,768]{1,0:T(8,128)(2,1)S(1)}, u32[]{:S(2)}, u32[]{:S(2)}) collective-permute-start(bf16[1920,768]{1,0:T(8,128)(2,1)} %get-tuple-element.126.mine), channel_id=1, source_target_pairs={{0,1},{1,0},{2,3},{3,2},{4,5},{5,4},{6,7},{7,6},{8,9},{9,8},{10,11... | collective-permute-start | bytes 8847368 | tf_op jit(solution)/shard_map/ppermute | solution.py:521
  336.3 164.1 %all-to-all-start.2 = ((bf16[32,24,768]{2,1,0:T(8,128)(2,1)}), bf16[32,24,768]{2,1,0:T(8,128)(2,1)}, u32[]{:S(2)}, u32[]{:S(2)}) async-start(bf16[32,24,768]{2,1,0:T(8,128)(2,1)} %bitcast.96), calls=%async_computation.3 | async-start | bytes 2359296 | tf_op jit(solution)/shard_map/all_to_all | solution.py:1349
  366.4 23.3 %collective-permute-start.55 = (bf16[4,192,384]{2,1,0:T(8,128)(2,1)}, bf16[4,192,384]{2,1,0:T(8,128)(2,1)S(1)}, u32[]{:S(2)}, u32[]{:S(2)}) collective-permute-start(bf16[4,192,384]{2,1,0:T(8,128)(2,1)} %get-tuple-element.137), channel_id=1, source_target_pairs={{0,2},{1,5},{2,0},{3,7},{4,6},{5,1},{6,4},{7,3},{8,10},{9,13},{10,... | collective-permute-start | bytes 1769480 | tf_op jit(solution)/shard_map/ppermute | solution.py:513
  368.6 33.8 %collective-permute-start.45 = (bf16[4,192,384]{2,1,0:T(8,128)(2,1)}, bf16[4,192,384]{2,1,0:T(8,128)(2,1)S(1)}, u32[]{:S(2)}, u32[]{:S(2)}) collective-permute-start(bf16[4,192,384]{2,1,0:T(8,128)(2,1)} %get-tuple-element.130), channel_id=1, source_target_pairs={{0,2},{1,5},{2,0},{3,7},{4,6},{5,1},{6,4},{7,3},{8,10},{9,13},{10,... | collective-permute-start | bytes 1769480 | tf_op jit(solution)/shard_map/ppermute | solution.py:513
  368.9 51.6 %collective-permute-start.51 = (bf16[4,192,384]{2,1,0:T(8,128)(2,1)}, bf16[4,192,384]{2,1,0:T(8,128)(2,1)S(1)}, u32[]{:S(2)}, u32[]{:S(2)}) collective-permute-start(bf16[4,192,384]{2,1,0:T(8,128)(2,1)} %get-tuple-element.134), channel_id=1, source_target_pairs={{0,2},{1,5},{2,0},{3,7},{4,6},{5,1},{6,4},{7,3},{8,10},{9,13},{10,... | collective-permute-start | bytes 1769480 | tf_op jit(solution)/shard_map/ppermute | solution.py:513
  373.6 44.1 %collective-permute-start.61 = (bf16[4,192,384]{2,1,0:T(8,128)(2,1)}, bf16[4,192,384]{2,1,0:T(8,128)(2,1)S(1)}, u32[]{:S(2)}, u32[]{:S(2)}) collective-permute-start(bf16[4,192,384]{2,1,0:T(8,128)(2,1)} %get-tuple-element.141), channel_id=1, source_target_pairs={{0,2},{1,5},{2,0},{3,7},{4,6},{5,1},{6,4},{7,3},{8,10},{9,13},{10,... | collective-permute-start | bytes 1769480 | tf_op jit(solution)/shard_map/ppermute | solution.py:513
  379.9 42.0 %collective-permute-start.44 = (bf16[4,192,384]{2,1,0:T(8,128)(2,1)S(1)}, bf16[4,192,384]{2,1,0:T(8,128)(2,1)S(1)}, u32[]{:S(2)}, u32[]{:S(2)}) collective-permute-start(bf16[4,192,384]{2,1,0:T(8,128)(2,1)S(1)} %add_convert_fusion.3), channel_id=1, source_target_pairs={{0,4},{1,3},{2,6},{3,1},{4,0},{5,7},{6,2},{7,5},{8,12},{9,11},{10,... | collective-permute-start | bytes 1769480 | tf_op jit(solution)/shard_map/ppermute | solution.py:505
  389.7 32.4 %collective-permute-start.50 = (bf16[4,192,384]{2,1,0:T(8,128)(2,1)S(1)}, bf16[4,192,384]{2,1,0:T(8,128)(2,1)S(1)}, u32[]{:S(2)}, u32[]{:S(2)}) collective-permute-start(bf16[4,192,384]{2,1,0:T(8,128)(2,1)S(1)} %add_convert_fusion.2), channel_id=1, source_target_pairs={{0,4},{1,3},{2,6},{3,1},{4,0},{5,7},{6,2},{7,5},{8,12},{9,11},{10,... | collective-permute-start | bytes 1769480 | tf_op jit(solution)/shard_map/ppermute | solution.py:505
  402.3 25.3 %collective-permute-start.57 = (bf16[4,192,384]{2,1,0:T(8,128)(2,1)S(1)}, bf16[4,192,384]{2,1,0:T(8,128)(2,1)S(1)}, u32[]{:S(2)}, u32[]{:S(2)}) collective-permute-start(bf16[4,192,384]{2,1,0:T(8,128)(2,1)S(1)} %copy-done.60), channel_id=1, source_target_pairs={{0,2},{1,5},{2,0},{3,7},{4,6},{5,1},{6,4},{7,3},{8,10},{9,13},{10,... | collective-permute-start | bytes 1769480 | tf_op jit(solution)/shard_map/ppermute | solution.py:513
  421.9 21.8 %collective-permute-start.62 = (bf16[4,192,384]{2,1,0:T(8,128)(2,1)S(1)}, bf16[4,192,384]{2,1,0:T(8,128)(2,1)S(1)}, u32[]{:S(2)}, u32[]{:S(2)}) collective-permute-start(bf16[4,192,384]{2,1,0:T(8,128)(2,1)S(1)} %add_convert_fusion), channel_id=1, source_target_pairs={{0,4},{1,3},{2,6},{3,1},{4,0},{5,7},{6,2},{7,5},{8,12},{9,11},{10,... | collective-permute-start | bytes 1769480 | tf_op jit(solution)/shard_map/ppermute | solution.py:505
  422.1 22.7 %collective-permute-start.46 = (bf16[192,384]{1,0:T(8,128)(2,1)S(1)}, bf16[192,384]{1,0:T(8,128)(2,1)S(1)}, u32[]{:S(2)}, u32[]{:S(2)}) collective-permute-start(bf16[192,384]{1,0:T(8,128)(2,1)S(1)} %get-tuple-element.185), channel_id=1, source_target_pairs={{0,24},{1,25},{2,26},{3,27},{4,28},{5,29},{6,30},{7,31},{8,0},{9,1... | collective-permute-start | bytes 442376 | tf_op jit(solution)/shard_map/ppermute | solution.py:529
  448.7 28.6 %collective-permute-start.59 = (bf16[192,384]{1,0:T(8,128)(2,1)S(1)}, bf16[192,384]{1,0:T(8,128)(2,1)S(1)}, u32[]{:S(2)}, u32[]{:S(2)}) collective-permute-start(bf16[192,384]{1,0:T(8,128)(2,1)S(1)} %get-tuple-element.193), channel_id=1, source_target_pairs={{0,16},{1,17},{2,18},{3,19},{4,20},{5,21},{6,22},{7,23},{8,24},{9,... | collective-permute-start | bytes 442376 | tf_op jit(solution)/shard_map/ppermute | solution.py:529
  449.7 27.6 %collective-permute-start.60 = (bf16[192,384]{1,0:T(8,128)(2,1)S(1)}, bf16[192,384]{1,0:T(8,128)(2,1)S(1)}, u32[]{:S(2)}, u32[]{:S(2)}) collective-permute-start(bf16[192,384]{1,0:T(8,128)(2,1)S(1)} %get-tuple-element.192), channel_id=1, source_target_pairs={{0,8},{1,9},{2,10},{3,11},{4,12},{5,13},{6,14},{7,15},{8,16},{9,17... | collective-permute-start | bytes 442376 | tf_op jit(solution)/shard_map/ppermute | solution.py:529
  507.9 24.7 %collective-permute-start.68 = (bf16[2,4,192,384]{3,2,1,0:T(8,128)(2,1)}, bf16[2,4,192,384]{3,2,1,0:T(8,128)(2,1)}, u32[]{:S(2)}, u32[]{:S(2)}) collective-permute-start(bf16[2,4,192,384]{3,2,1,0:T(8,128)(2,1)} %pad_maximum_fusion.9), channel_id=1, source_target_pairs={{0,1},{1,0},{2,3},{3,2},{4,5},{5,4},{6,7},{7,6},{8,9},{9,8},{10,11... | collective-permute-start | bytes 3538952 | tf_op jit(solution)/shard_map/ppermute | solution.py:521
  (99 other events, 1822.3 us)

commit v2 on v1

--- a/solution.py
+++ b/solution.py
@@ -5,6 +5,7 @@
 import jax.numpy as jnp
 from jax import lax
 from jax.experimental import pallas as pl
+from jax.experimental.layout import Layout, with_layout_constraint
 from jax.experimental.pallas import tpu as pltpu
 from jax.sharding import Mesh
 from jax.sharding import PartitionSpec as P
@@ -302,6 +303,8 @@
 
 
 def per_device(
+    dp,
+    vocab,
     token_ids,
     lengths,
     comp_mask,
@@ -319,11 +322,11 @@
     gain_moment,
     gain_second,
 ):
-    vocab_count = lax.axis_size("vocab")
-    vocab_index = lax.axis_index("vocab")
+    vocab_count = lax.axis_size(vocab)
+    vocab_index = lax.axis_index(vocab)
     row_share = blocks.shape[1]
     cosine, sine = angles()
-    tables_low = lax.all_gather(tables.astype(jnp.bfloat16), "dp", axis=1, tiled=True)
+    tables_low = lax.all_gather(tables.astype(jnp.bfloat16), dp, axis=1, tiled=True)
     vocab_rows = tables_low.shape[1]
     local_ids = token_ids.reshape(-1) - vocab_index * vocab_rows
     inside = (local_ids >= 0) & (local_ids < vocab_rows)
@@ -332,10 +335,10 @@
         jnp.float32
     )
     embedded = lax.psum_scatter(
-        looked.astype(jnp.bfloat16), "vocab", scatter_dimension=0, tiled=True
+        looked.astype(jnp.bfloat16), vocab, scatter_dimension=0, tiled=True
     ).astype(jnp.float32)
-    rows_all = lax.all_gather(blocks.astype(jnp.bfloat16), "vocab", axis=1, tiled=True)
-    slots_all = lax.all_gather(rows_all, "dp", axis=0, tiled=True)
+    rows_all = lax.all_gather(blocks.astype(jnp.bfloat16), vocab, axis=1, tiled=True)
+    slots_all = lax.all_gather(rows_all, dp, axis=0, tiled=True)
     kept_mats = groups(jnp.take(slots_all, owner, axis=0))
     gain_total = jnp.zeros((3, D), jnp.float32)
     loss_own = jnp.zeros((), jnp.float32)
@@ -353,7 +356,7 @@
             h_out.reshape(2, SLOT, D), pos_own[:, :, None], axis=1
         ).reshape(2 * CMP, D)
         c_low = rms_forward(picked_rows, gains[2]).astype(jnp.bfloat16)
-        all_rows = lax.all_gather(c_low, "vocab", axis=0, tiled=True)
+        all_rows = lax.all_gather(c_low, vocab, axis=0, tiled=True)
         ids_sel = token_ids[micro::MB]
         lens_sel = lengths[micro::MB]
         mask_sel = comp_mask[micro::MB].astype(jnp.float32)
@@ -367,7 +370,7 @@
         row_max = jnp.max(logits, axis=1)
         row_sum = jnp.sum(jnp.exp(logits - row_max[:, None]), axis=1)
         row_pick = jnp.sum(jnp.where(one_hot, logits, 0.0), axis=1)
-        full_max, full_sum, full_pick = joined((row_max, row_sum, row_pick), "vocab", combine_parts)
+        full_max, full_sum, full_pick = joined((row_max, row_sum, row_pick), vocab, combine_parts)
         log_norm = full_max + jnp.log(full_sum)
         seq_logp = jnp.sum((full_pick - log_norm).reshape(vocab_count, 2, CMP) * mask_sel, axis=2)
         margin = DPO_BETA * (seq_logp[:, 0] - ref_sel[:, 0] - (seq_logp[:, 1] - ref_sel[:, 1]))
@@ -382,7 +385,7 @@
         logit_grads.append(grad_logits)
         head_inputs.append(all_rows)
         grad_c = lax.psum_scatter(
-            mult(grad_logits, tables_low[1]), "vocab", scatter_dimension=0, tiled=True
+            mult(grad_logits, tables_low[1]), vocab, scatter_dimension=0, tiled=True
         )
         back_rows, gain_head = rms_backward(picked_rows, gains[2], grad_c)
         seq_index = jnp.arange(2)[:, None]
@@ -406,7 +409,7 @@
     block_order = weight_grads(joined_ops)
     grad_head = mult_t(jnp.concatenate(logit_grads, axis=0), jnp.concatenate(head_inputs, axis=0))
     grad_rows = lax.all_gather(
-        jnp.concatenate(grad_inputs, axis=0).astype(jnp.bfloat16), "vocab", axis=0, tiled=True
+        jnp.concatenate(grad_inputs, axis=0).astype(jnp.bfloat16), vocab, axis=0, tiled=True
     ).astype(jnp.float32)
     grad_embed = (
         jnp.zeros((vocab_rows, D), jnp.float32)
@@ -415,17 +418,17 @@
     )
     table_grad = lax.psum_scatter(
         jnp.stack([grad_embed, grad_head]).astype(jnp.bfloat16),
-        "dp",
+        dp,
         scatter_dimension=1,
         tiled=True,
     ).astype(jnp.float32)
     inverse = jnp.zeros((NBLK,), jnp.int32).at[owner].set(jnp.arange(NBLK, dtype=jnp.int32))
     slotted = jnp.take(block_order, inverse, axis=0)
-    summed = lax.psum_scatter(slotted.astype(jnp.bfloat16), "dp", scatter_dimension=0, tiled=True)
-    share_part = lax.psum_scatter(summed, "vocab", scatter_dimension=1, tiled=True).astype(
+    summed = lax.psum_scatter(slotted.astype(jnp.bfloat16), dp, scatter_dimension=0, tiled=True)
+    share_part = lax.psum_scatter(summed, vocab, scatter_dimension=1, tiled=True).astype(
         jnp.float32
     )
-    whole = lax.all_gather(share_part.astype(jnp.bfloat16), "vocab", axis=1, tiled=True).astype(
+    whole = lax.all_gather(share_part.astype(jnp.bfloat16), vocab, axis=1, tiled=True).astype(
         share_part.dtype
     )
     highest = lax.Precision.HIGHEST
@@ -440,7 +443,7 @@
     new_blocks = blocks - SHAMPOO_RATE * lax.dynamic_slice_in_dim(
         direction, vocab_index * row_share, row_share, 1
     )
-    loss_sum, gain_grad = lax.psum((loss_own, gain_total), ("dp", "vocab"))
+    loss_sum, gain_grad = lax.psum((loss_own, gain_total), dp + vocab)
     rates = jnp.array([0.3, 0.02], jnp.float32)[:, None, None]
     new_tables, new_table_moment, new_table_second = adam_step(
         tables, table_grad, table_moment, table_second, rates
@@ -473,18 +476,20 @@
 VMEM_LIMIT = 60 * 1024 * 1024
 
 AT_A = 0
-AT_DK = AT_A + TOKENS
+AT_AP = AT_A + TOKENS
+AT_O = AT_AP + PAIR_ROWS
+AT_B = AT_O + PAIR_ROWS
+AT_Z = AT_B + PAIR_ROWS
+LEFT_ROWS = AT_Z + (FF // D) * PAIR_ROWS
+LEFT_KINDS = (LEFT_ROWS - AT_AP) // PAIR_ROWS
+AT_DK = 0
 AT_DV = AT_DK + TOKENS
-AT_AP = AT_DV + TOKENS
-AT_DQ = AT_AP + PAIR_ROWS
-AT_O = AT_DQ + PAIR_ROWS
-AT_DO = AT_O + PAIR_ROWS
-AT_B = AT_DO + PAIR_ROWS
-AT_Z = AT_B + PAIR_ROWS
-AT_DGATE = AT_Z + (FF // D) * PAIR_ROWS
+AT_DQ = AT_DV + TOKENS
+AT_DO = AT_DQ + PAIR_ROWS
+AT_DGATE = AT_DO + PAIR_ROWS
 AT_DUP = AT_DGATE + (FF // D) * PAIR_ROWS
 AT_DH = AT_DUP + (FF // D) * PAIR_ROWS
-ACT_ROWS = AT_DH + PAIR_ROWS
+RIGHT_ROWS = AT_DH + PAIR_ROWS
 
 
 def flat_of(z, x, y, c):
@@ -529,13 +534,27 @@
     return lax.ppermute(value, AXES, moves(lambda z, x, y, c: ((z + step) % 4, x, y, c)))
 
 
-def spread(chunk):
-    line = jnp.stack([chunk] + [ring(chunk, step) for step in range(1, 4)])
+def after(value, *others):
+    return lax.optimization_barrier((value,) + others)[0]
+
+
+def together(*values):
+    return lax.optimization_barrier(values)
+
+
+def all_round(chunk):
+    return jnp.stack([chunk] + [ring(chunk, step) for step in range(1, 4)])
+
+
+def spread(chunk, wait=()):
+    if wait:
+        chunk = after(chunk, *wait)
+    around = [ring(chunk, step) for step in range(1, 4)]
+    line = jnp.stack([chunk] + around)
     one = hop_one(line)
     two = hop_two(line)
     both = hop_two(one)
-    plane = jnp.stack([line, one, two, both])
-    return plane, hop_core(plane)
+    return jnp.stack([line, one, two, both]), around
 
 
 def dot_nn(left, right):
@@ -558,33 +577,39 @@
     return value.astype(jnp.float32)
 
 
-def source_of(coord, other_core, rel, back):
+def place_of(coord, other_core, rel):
     core = coord[3] + other_core * (1 - 2 * coord[3])
     first = rel & 1
     second = rel >> 1
     x_flip = first + core * (second - first)
     y_flip = second + core * (first - second)
-    z = (coord[0] + 4 - back) & 3
     x = coord[1] + x_flip * (1 - 2 * coord[1])
     y = coord[2] + y_flip * (1 - 2 * coord[2])
-    return z, x, y, core
+    return x, y, core
 
 
 def start_weights(coord, parts, held, sem):
-    for index in range(8):
-        slot_low, other_core = index // 2, index % 2
-
-        def one(i, carry):
-            rel, back = i >> 2, i & 3
-            z, x, y, core = source_of(coord, other_core, rel, back)
-            slot = 8 * z + 4 * x + slot_low
-            row = pl.multiple_of(192 * (2 * y + core), 64)
-            pltpu.make_async_copy(
-                parts[index].at[rel, back], held.at[slot, pl.ds(row, 192)], sem
-            ).start()
-            return carry
-
-        lax.fori_loop(0, 16, one, 0)
+    def start(source, slots, y, core):
+        row = pl.multiple_of(192 * (2 * y + core), 64)
+        pltpu.make_async_copy(source, held.at[slots, pl.ds(row, 192)], sem).start()
+
+    for other_core in range(2):
+        for rel in range(4):
+            x, y, core = place_of(coord, other_core, rel)
+            pair, third, fourth = (
+                parts[2 * rel + other_core],
+                parts[8 + 2 * rel + other_core],
+                parts[16 + 2 * rel + other_core],
+            )
+
+            def one(n, carry):
+                back = (coord[0] + 4 - n) & 3
+                start(pair.at[n], pl.ds(8 * n + 4 * x, 2), y, core)
+                start(third.at[n], 8 * back + 4 * x + 2, y, core)
+                start(fourth.at[n], 8 * back + 4 * x + 3, y, core)
+                return carry
+
+            lax.fori_loop(0, 4, one, 0)
 
 
 def wait_weights(held, sem):
@@ -630,17 +655,17 @@
 
 
 def forward_kernel(owner, coord, lens, x, gains, cos_q, sin_q, cos_k, sin_k, *rest):
-    parts, rest = rest[:8], rest[8:]
-    a_out, ap_out, q_out, k_out, v_out, o_out, h1_out, b_out, gate_out, up_out, z_out, h2_out, c_out = rest[:13]
-    held, sem = rest[13:]
+    parts, rest = rest[:24], rest[24:]
+    left, q_out, k_out, v_out, h1_out, gate_out, up_out, h2_out, c_out = rest[:9]
+    held, sem = rest[9:]
     start_weights(coord, parts, held, sem)
     values = high(x[...])
     a_low = low(values * scale_of(values) * gains[0:1, :])
-    a_out[...] = a_low
+    left[AT_A:AT_AP] = a_low
     valid, chosen = masks(lens)
     select = jnp.where(chosen, 1.0, 0.0).astype(jnp.bfloat16)
     a_pick = low(dot_nn(select, a_low))
-    ap_out[...] = a_pick
+    left[AT_AP:AT_O] = a_pick
     x_pick = dot_nn(select, x[...])
     wait_weights(held, sem)
     for j in range(2):
@@ -663,24 +688,28 @@
             e = jnp.exp(s - jnp.max(s, axis=-1, keepdims=True))
             prob = low(e / jnp.sum(e, axis=-1, keepdims=True))
             total = total + dot_nn(prob, jnp.where(mine, v_out[:, at], zero))
-        o_out[:, at] = low(total)
+        left[AT_O:AT_B, at] = low(total)
     for j in range(2):
         at = slice(j * BC, (j + 1) * BC)
-        h1_out[:, at] = x_pick[:, at] + dot_nn(o_out[...], held[owner[6 + j]])
+        h1_out[:, at] = x_pick[:, at] + dot_nn(left[AT_O:AT_B], held[owner[6 + j]])
     h1 = h1_out[...]
     b_low = low(h1 * scale_of(h1) * gains[1:2, :])
-    b_out[...] = b_low
+    left[AT_B:AT_Z] = b_low
     for j in range(FF // BC):
         at = slice(j * BC, (j + 1) * BC)
         gate = dot_nn(b_low, held[owner[8 + j]])
         up = dot_nn(b_low, held[owner[16 + j]])
         gate_out[:, at] = gate
         up_out[:, at] = up
-        z_out[:, at] = low(gate * jax.nn.sigmoid(gate) * up)
+        row = AT_Z + j // 2 * PAIR_ROWS
+        left[row : row + PAIR_ROWS, j % 2 * BC : (j % 2 + 1) * BC] = low(
+            gate * jax.nn.sigmoid(gate) * up
+        )
     for j in range(2):
         total = h1[:, j * BC : (j + 1) * BC]
         for r in range(FF // D):
-            total = total + dot_nn(z_out[:, r * D : (r + 1) * D], held[owner[24 + 2 * r + j]])
+            row = AT_Z + r * PAIR_ROWS
+            total = total + dot_nn(left[row : row + PAIR_ROWS], held[owner[24 + 2 * r + j]])
         h2_out[:, j * BC : (j + 1) * BC] = total
     h2 = h2_out[...]
     c_out[...] = low(h2 * scale_of(h2) * gains[2:3, :])
@@ -705,22 +734,18 @@
     return pl.pallas_call(
         forward_kernel,
         out_shape=(
-            made(TOKENS, D, jnp.bfloat16),
-            made(PAIR_ROWS, D, jnp.bfloat16),
+            made(LEFT_ROWS, D, jnp.bfloat16),
             made(PAIR_ROWS, D, jnp.bfloat16),
             made(TOKENS, D, jnp.bfloat16),
             made(TOKENS, D, jnp.bfloat16),
-            made(PAIR_ROWS, D, jnp.bfloat16),
+            made(PAIR_ROWS, D, jnp.float32),
+            made(PAIR_ROWS, FF, jnp.float32),
+            made(PAIR_ROWS, FF, jnp.float32),
             made(PAIR_ROWS, D, jnp.float32),
             made(PAIR_ROWS, D, jnp.bfloat16),
-            made(PAIR_ROWS, FF, jnp.float32),
-            made(PAIR_ROWS, FF, jnp.float32),
-            made(PAIR_ROWS, FF, jnp.bfloat16),
-            made(PAIR_ROWS, D, jnp.float32),
-            made(PAIR_ROWS, D, jnp.bfloat16),
-        ),
-        in_specs=smem(3) + vmem(6) + anywhere(8),
-        out_specs=tuple(vmem(13)),
+        ),
+        in_specs=smem(3) + vmem(6) + anywhere(24),
+        out_specs=tuple(vmem(9)),
         scratch_shapes=[
             pltpu.VMEM((NBLK, D, BC), jnp.bfloat16),
             pltpu.SemaphoreType.DMA,
@@ -761,26 +786,32 @@
     return top, total, mixed
 
 
-def merge_kernel(*refs):
-    out = refs[-1]
-    top, total, mixed = merge([unpack(ref[...]) for ref in refs[:-1]])
-    out[:, :D] = low(mixed)
-    out[:, D:EXT] = pack_stat(top, total)
-
-
-def merge_call(*parts):
-    rows = parts[0].shape[0]
-    block = min(rows, 256)
-    spec = pl.BlockSpec((block, EXT), lambda i: (i, 0))
+def merge_kernel(number, *refs):
+    top, total, mixed = merge([unpack(ref[...]) for ref in refs[:number]])
+    mixed = low(mixed)
+    stat = pack_stat(top, total)
+    outs = refs[number:]
+    rows = outs[0].shape[0]
+    for n, out in enumerate(outs):
+        out[:, :D] = mixed[n * rows : (n + 1) * rows]
+        out[:, D:EXT] = stat[n * rows : (n + 1) * rows]
+
+
+def merge_call(parts, pieces=1):
+    rows = 4 * PAIR_ROWS
+    made = jax.ShapeDtypeStruct((rows // pieces, EXT), jnp.bfloat16)
     return pl.pallas_call(
-        merge_kernel,
-        grid=(rows // block,),
-        out_shape=jax.ShapeDtypeStruct((rows, EXT), jnp.bfloat16),
-        in_specs=[spec] * len(parts),
-        out_specs=spec,
+        functools.partial(merge_kernel, len(parts)),
+        grid=(1,),
+        out_shape=(made,) * pieces,
+        in_specs=[pl.BlockSpec((rows, EXT), lambda i, at=at: (at, 0)) for _, at in parts],
+        out_specs=(pl.BlockSpec(made.shape, lambda i: (0, 0)),) * pieces,
         compiler_params=pltpu.CompilerParams(vmem_limit_bytes=VMEM_LIMIT),
+        cost_estimate=pl.CostEstimate(
+            flops=8 * rows * D, bytes_accessed=4 * rows * EXT, transcendentals=rows
+        ),
         name="merge_parts",
-    )(*parts)
+    )(*[array for array, _ in parts])
 
 
 def head_kernel(real, rows, head, ext, kept, stat):
@@ -817,57 +848,70 @@
             pl.BlockSpec((256, 128), lambda i: (i, 0)),
         ),
         compiler_params=pltpu.CompilerParams(vmem_limit_bytes=VMEM_LIMIT),
+        cost_estimate=pl.CostEstimate(
+            flops=4 * number * wide * D, bytes_accessed=2 * number * wide, transcendentals=number * wide
+        ),
         name="head_forward",
     )(rows, head)
 
 
-def head_grad_kernel(rows, kept, stat, info, out):
-    weight = info[:, 0:1]
-    factor = weight * jnp.exp(stat[:, 0:1] - info[:, 1:2])
-    col = iota(kept.shape, 1)
-    hit = col == info[:, 2:3].astype(jnp.int32)
-    grad = low(jnp.where(hit, weight, 0.0) - high(kept[...]) * factor)
-
-    @pl.when(pl.program_id(0) == 0)
+def head_grad_kernel(steps, rows_a, rows_b, kept_a, kept_b, stat_a, stat_b, info, out):
+    def add(rows, kept, stat):
+        weight = info[:, 0:1]
+        factor = weight * jnp.exp(stat[:, 0:1] - info[:, 1:2])
+        col = iota(kept.shape, 1)
+        hit = col == info[:, 2:3].astype(jnp.int32)
+        grad = low(jnp.where(hit, weight, 0.0) - high(kept[...]) * factor)
+        return dot_tn(grad, rows[...])
+
+    i = pl.program_id(0)
+
+    @pl.when(i == 0)
     def _():
-        out[...] = jnp.zeros(out.shape, jnp.float32)
-
-    out[...] += dot_tn(grad, rows[...])
+        out[...] = add(rows_a, kept_a, stat_a)
+
+    @pl.when((i > 0) & (i < steps))
+    def _():
+        out[...] += add(rows_a, kept_a, stat_a)
+
+    @pl.when(i >= steps)
+    def _():
+        out[...] += add(rows_b, kept_b, stat_b)
 
 
 def head_grad_call(rows, kept, stat, info):
-    number, wide = kept.shape
+    number, wide = kept[0].shape
+    steps = number // 256
+
+    def pair(columns):
+        return [
+            pl.BlockSpec((256, columns), lambda i: (jnp.minimum(i, steps - 1), 0)),
+            pl.BlockSpec((256, columns), lambda i: (jnp.maximum(i - steps, 0), 0)),
+        ]
+
     return pl.pallas_call(
-        head_grad_kernel,
-        grid=(number // 256,),
+        functools.partial(head_grad_kernel, steps),
+        grid=(2 * steps,),
         out_shape=jax.ShapeDtypeStruct((wide, D), jnp.float32),
-        in_specs=[
-            pl.BlockSpec((256, D), lambda i: (i, 0)),
-            pl.BlockSpec((256, wide), lambda i: (i, 0)),
-            pl.BlockSpec((256, 128), lambda i: (i, 0)),
-            pl.BlockSpec((256, 128), lambda i: (i, 0)),
-        ],
+        in_specs=pair(D) + pair(wide) + pair(128) + [pl.BlockSpec((256, 128), lambda i: (i, 0))],
         out_specs=pl.BlockSpec((wide, D), lambda i: (0, 0)),
         compiler_params=pltpu.CompilerParams(vmem_limit_bytes=VMEM_LIMIT),
+        cost_estimate=pl.CostEstimate(
+            flops=4 * number * wide * D, bytes_accessed=4 * number * wide, transcendentals=number
+        ),
         name="head_grad",
-    )(rows, kept, stat, info)
+    )(*rows, *kept, *stat, info)
 
 
 def backward_kernel(owner, coord, lens, refs, x, gains, cos_q, sin_q, cos_k, sin_k, *rest):
-    a, ap, q, k, v, o, h1, b, gate, up, z, h2, c = rest[:13]
-    truth, wanted, u0, u1, u2, u3 = rest[13:19]
-    parts = rest[19:27]
-    act, dx_out, gain_out, info_out, loss_out = rest[27:32]
-    held, sem, dk_acc = rest[32:]
+    q, k, v, h1, gate, up, h2, c = rest[:8]
+    truth, wanted, u0, u1, u2, u3 = rest[8:14]
+    parts = rest[14:38]
+    act, dx_out, gain_out, info_out, loss_out = rest[38:43]
+    held, sem = rest[43:]
     start_weights(coord, parts, held, sem)
     valid, chosen = masks(lens)
     select = jnp.where(chosen, 1.0, 0.0).astype(jnp.bfloat16)
-    act[AT_A:AT_DK] = a[...]
-    act[AT_AP:AT_DQ] = ap[...]
-    act[AT_O:AT_DO] = o[...]
-    act[AT_B:AT_Z] = b[...]
-    for r in range(FF // D):
-        act[AT_Z + r * PAIR_ROWS : AT_Z + (r + 1) * PAIR_ROWS] = z[:, r * D : (r + 1) * D]
     top, total, mixed = merge([unpack(part[...]) for part in (u0, u1, u2, u3)])
     norm = top + jnp.log(total)
     target = high(truth[...])
@@ -893,7 +937,7 @@
     d2, gain_top = rms_back(h2[...], gains[2:3, :], grad_c)
     gain_out[2:3, :] = gain_top
     d2_low = low(d2)
-    act[AT_DH:ACT_ROWS] = d2_low
+    act[AT_DH:RIGHT_ROWS] = d2_low
     wait_weights(held, sem)
     grad_b = jnp.zeros((PAIR_ROWS, D), jnp.float32)
     for r in range(FF // D):
@@ -915,7 +959,7 @@
     gain_out[1:2, :] = gain_mid
     d1 = d2 + back
     d1_low = low(d1)
-    act[AT_DO:AT_B] = d1_low
+    act[AT_DO:AT_DGATE] = d1_low
     d_att = low(
         dot_nt(d1_low[:, :BC], held[owner[6]]) + dot_nt(d1_low[:, BC:], held[owner[7]])
     )
@@ -943,16 +987,16 @@
             d_q = d_q + dot_nn(d_s, k_one)
             d_k = d_k + dot_tn(d_s, q_one)
             d_v = d_v + dot_tn(low(prob), do_one)
-        act[AT_DQ:AT_O, at] = low(turn(d_q * root, cos_q[...], sin_q[...], -1.0))
+        act[AT_DQ:AT_DO, at] = low(turn(d_q * root, cos_q[...], sin_q[...], -1.0))
         act[AT_DK:AT_DV, at] = low(turn(d_k * root, cos_k[...], sin_k[...], -1.0))
-        act[AT_DV:AT_AP, at] = low(d_v)
-    d_q_all = low(dot_tn(select, act[AT_DQ:AT_O]))
+        act[AT_DV:AT_DQ, at] = low(d_v)
+    d_q_all = low(dot_tn(select, act[AT_DQ:AT_DO]))
     grad_a = jnp.zeros((TOKENS, D), jnp.float32)
     for j in range(2):
         cut = slice(j * BC, (j + 1) * BC)
         grad_a = grad_a + dot_nt(d_q_all[:, cut], held[owner[j]])
         grad_a = grad_a + dot_nt(act[AT_DK:AT_DV, cut], held[owner[2 + j]])
-        grad_a = grad_a + dot_nt(act[AT_DV:AT_AP, cut], held[owner[4 + j]])
+        grad_a = grad_a + dot_nt(act[AT_DV:AT_DQ, cut], held[owner[4 + j]])
     back_in, gain_in = rms_back(high(x[...]), gains[0:1, :], grad_a)
     gain_out[0:1, :] = gain_in
     rest_low = low(d1 - high(d1_low))
@@ -963,116 +1007,139 @@
     return pl.pallas_call(
         backward_kernel,
         out_shape=(
-            jax.ShapeDtypeStruct((ACT_ROWS, D), jnp.bfloat16),
+            jax.ShapeDtypeStruct((RIGHT_ROWS, D), jnp.bfloat16),
             jax.ShapeDtypeStruct((TOKENS, D), jnp.bfloat16),
             jax.ShapeDtypeStruct((3, D), jnp.float32),
             jax.ShapeDtypeStruct((PAIR_ROWS, 128), jnp.float32),
             jax.ShapeDtypeStruct((1, 128), jnp.float32),
         ),
-        in_specs=smem(4) + vmem(6 + 13 + 2 + 4) + anywhere(8),
+        in_specs=smem(4) + vmem(6 + 8 + 2 + 4) + anywhere(24),
         out_specs=tuple(vmem(5)),
         scratch_shapes=[
             pltpu.VMEM((NBLK, D, BC), jnp.bfloat16),
             pltpu.SemaphoreType.DMA,
-            pltpu.VMEM((8, 128), jnp.float32),
         ],
         compiler_params=pltpu.CompilerParams(vmem_limit_bytes=VMEM_LIMIT),
         name="layer_backward",
     )(owner, coord, lens, refs, x, gains, *turns, *saved, truth, wanted, *parts_u, *parts)
 
 
-def weight_grad_kernel(block_of, x_at, y_at, coord, mine, theirs, *outs):
-    core = coord[3]
-    for k in range(4):
-        own, one, two, both = outs[4 * k : 4 * k + 4]
-        for x_flip in range(2):
-
-            def step(back, carry):
-                z = (coord[0] + 4 - back) & 3
-                x = coord[1] + x_flip * (1 - 2 * coord[1])
-                slot = 8 * z + 4 * x + k
-                block = block_of[slot]
-                cut = pl.ds(pl.multiple_of((block & 1) * BC, 128), BC)
-                x_row = pl.multiple_of(x_at[slot], 64)
-                y_row = pl.multiple_of(y_at[slot], 64)
-
-                def put(grad):
-                    grad_low = low(grad)
-                    quarter = [grad_low[192 * n : 192 * (n + 1)] for n in range(4)]
-                    even = coord[2] == 0
-                    first = core == 0
-                    near = jnp.where(
-                        even,
-                        jnp.where(first, quarter[0], quarter[1]),
-                        jnp.where(first, quarter[2], quarter[3]),
-                    )
-                    far = jnp.where(
-                        even,
-                        jnp.where(first, quarter[2], quarter[3]),
-                        jnp.where(first, quarter[0], quarter[1]),
-                    )
-                    if x_flip == 0:
-                        own[back] = near
-
-                        @pl.when(first)
-                        def _():
-                            two[back] = far
-
-                        @pl.when(jnp.logical_not(first))
-                        def _():
-                            one[back] = far
-                    else:
-                        both[back] = far
-
-                        @pl.when(first)
-                        def _():
-                            one[back] = near
-
-                        @pl.when(jnp.logical_not(first))
-                        def _():
-                            two[back] = near
-
-                wide = (block >= 2) & (block < 6)
-
-                @pl.when(wide)
-                def _():
-                    left = jnp.concatenate(
-                        [mine[pl.ds(x_row, TOKENS), :], theirs[pl.ds(x_row, TOKENS), :]], axis=0
-                    )
-                    right = jnp.concatenate(
-                        [mine[pl.ds(y_row, TOKENS), cut], theirs[pl.ds(y_row, TOKENS), cut]], axis=0
-                    )
-                    put(dot_tn(left, right))
-
-                @pl.when(jnp.logical_not(wide))
-                def _():
-                    left = jnp.concatenate(
-                        [mine[pl.ds(x_row, PAIR_ROWS), :], theirs[pl.ds(x_row, PAIR_ROWS), :]],
-                        axis=0,
-                    )
-                    right = jnp.concatenate(
-                        [mine[pl.ds(y_row, PAIR_ROWS), cut], theirs[pl.ds(y_row, PAIR_ROWS), cut]],
-                        axis=0,
-                    )
-                    put(dot_tn(left, right))
-
-                return carry
-
-            lax.fori_loop(0, 4, step, 0)
-
-
-def weight_grad_call(block_of, x_at, y_at, coord, mine, theirs):
+def transpose_kernel(coord, mine, theirs, picked, tokens, turned_a, turned_b):
+    near_row = pl.multiple_of(192 * (2 * coord[2] + coord[3]), 64)
+    far_row = pl.multiple_of(192 * (2 * (1 - coord[2]) + coord[3]), 64)
+    for n in range(LEFT_KINDS):
+        at = slice(AT_AP + n * PAIR_ROWS, AT_AP + (n + 1) * PAIR_ROWS)
+        turned_a[...] = jnp.concatenate([mine[at], theirs[at]], axis=0).T
+        picked[n, :192] = turned_a[pl.ds(near_row, 192), :]
+        picked[n, 192:] = turned_a[pl.ds(far_row, 192), :]
+    turned_b[:, :TOKENS] = mine[AT_A:AT_AP].T
+    turned_b[:, TOKENS:] = theirs[AT_A:AT_AP].T
+    tokens[:192] = turned_b[pl.ds(near_row, 192), :]
+    tokens[192:] = turned_b[pl.ds(far_row, 192), :]
+
+
+def transpose_call(coord, mine, theirs):
+    return pl.pallas_call(
+        transpose_kernel,
+        out_shape=(
+            jax.ShapeDtypeStruct((LEFT_KINDS, 384, 2 * PAIR_ROWS), jnp.bfloat16),
+            jax.ShapeDtypeStruct((384, 2 * TOKENS), jnp.bfloat16),
+        ),
+        in_specs=smem(1) + vmem(2),
+        out_specs=tuple(vmem(2)),
+        scratch_shapes=[
+            pltpu.VMEM((D, 2 * PAIR_ROWS), jnp.bfloat16),
+            pltpu.VMEM((D, 2 * TOKENS), jnp.bfloat16),
+        ],
+        compiler_params=pltpu.CompilerParams(vmem_limit_bytes=VMEM_LIMIT),
+        cost_estimate=pl.CostEstimate(
+            flops=0, bytes_accessed=8 * LEFT_ROWS * D, transcendentals=0
+        ),
+        name="left_transposed",
+    )(coord, mine, theirs)
+
+
+def weight_grad_kernel(block_of, x_at, y_at, coord, picked, tokens, mine, theirs, *rest):
+    pair, singles = rest[:4], (rest[4:8], rest[8:12])
+    near_held, far_held, sem = rest[12:]
+    first = coord[3] == 0
+    for group, (k, x_flip) in enumerate((k, x_flip) for k in range(4) for x_flip in range(2)):
+        x = coord[1] + x_flip * (1 - 2 * coord[1])
+
+        def step(n, carry):
+            z = n if k < 2 else (coord[0] + 4 - n) & 3
+            slot = 8 * z + 4 * x + k
+            block = block_of[slot]
+            cut = pl.ds(pl.multiple_of((block & 1) * BC, 128), BC)
+            y_row = pl.multiple_of(y_at[slot], 64)
+
+            def put(left, rows):
+                right = jnp.concatenate(
+                    [mine[pl.ds(y_row, rows), cut], theirs[pl.ds(y_row, rows), cut]], axis=0
+                )
+                grad = low(dot_nn(left, right))
+                near_held[group, n] = grad[:192]
+                far_held[group, n] = grad[192:]
+
+            wide = (block >= 2) & (block < 6)
+
+            @pl.when(wide)
+            def _():
+                put(tokens[...], TOKENS)
+
+            @pl.when(jnp.logical_not(wide))
+            def _():
+                put(picked[x_at[slot]], PAIR_ROWS)
+
+            return carry
+
+        lax.fori_loop(0, 4, step, 0)
+
+        def send(held, rel):
+            target = pair[rel].at[:, k] if k < 2 else singles[k - 2][rel]
+            pltpu.make_async_copy(held.at[group], target, sem).start()
+
+        if x_flip == 0:
+            send(near_held, 0)
+            side = far_held
+        else:
+            send(far_held, 3)
+            side = near_held
+
+        @pl.when(first == (x_flip == 1))
+        def _():
+            send(side, 1)
+
+        @pl.when(first == (x_flip == 0))
+        def _():
+            send(side, 2)
+
+    pltpu.make_async_copy(near_held, near_held, sem).wait()
+    pltpu.make_async_copy(far_held, far_held, sem).wait()
+
+
+def weight_grad_call(block_of, x_at, y_at, coord, picked, tokens, mine, theirs):
     return pl.pallas_call(
         weight_grad_kernel,
-        out_shape=tuple([jax.ShapeDtypeStruct((4, 192, BC), jnp.bfloat16)] * 16),
-        in_specs=smem(4) + vmem(2),
-        out_specs=tuple(vmem(16)),
+        out_shape=tuple(
+            [jax.ShapeDtypeStruct((4, 2, 192, BC), jnp.bfloat16)] * 4
+            + [jax.ShapeDtypeStruct((4, 192, BC), jnp.bfloat16)] * 8
+        ),
+        in_specs=smem(4) + vmem(4),
+        out_specs=tuple(anywhere(12)),
+        scratch_shapes=[
+            pltpu.VMEM((8, 4, 192, BC), jnp.bfloat16),
+            pltpu.VMEM((8, 4, 192, BC), jnp.bfloat16),
+            pltpu.SemaphoreType.DMA,
+        ],
         compiler_params=pltpu.CompilerParams(vmem_limit_bytes=VMEM_LIMIT),
         name="weight_grads",
-    )(block_of, x_at, y_at, coord, mine, theirs)
-
-
-def shampoo_kernel(coord, own, by_y, by_core, by_both, lstat, rstat, lroot, rroot, blk, new_l, new_r, new_b, whole):
+    )(block_of, x_at, y_at, coord, picked, tokens, mine, theirs)
+
+
+def shampoo_kernel(coord, *refs):
+    own, by_y, by_core, by_both, lstat, rstat, lroot, rroot, blk = refs[:9]
+    new_b, grad_out, new_l, new_r, whole = refs[-5:]
     y, core = coord[2], coord[3]
     for piece, y_at, core_at in (
         (own, y, core),
@@ -1082,6 +1149,7 @@
     ):
         row = pl.multiple_of(192 * (2 * y_at + core_at), 64)
         whole[pl.ds(row, 192), :] = piece[0]
+    grad_out[0] = high(own[0])
     grad = whole[...]
     new_l[0] = STAT_DECAY * lstat[0] + (1.0 - STAT_DECAY) * dot_nt(grad, grad)
     new_r[0] = STAT_DECAY * rstat[0] + (1.0 - STAT_DECAY) * dot_tn(grad, grad)
@@ -1089,55 +1157,103 @@
     new_b[0] = blk[0] - SHAMPOO_RATE * dot_nn(low(turned), low(rroot[0]))
 
 
-def shampoo_call(coord, pieces, lstat, rstat, lroot, rroot, blk):
-    slots = lstat.shape[0]
-
+def shampoo_call(start, coord, pieces, lstat, rstat, lroot, rroot, blk, so_far):
     def one(rows, columns):
-        return pl.BlockSpec((1, rows, columns), lambda i, coord: (i, 0, 0))
-
+        return pl.BlockSpec((1, rows, columns), lambda i, coord: (start + i, 0, 0))
+
+    slots = pieces[0].shape[0]
+    in_specs = (
+        [pl.BlockSpec((1, 192, BC), lambda i, coord: (i, 0, 0))] * 4
+        + [
+            one(D, D),
+            one(BC, BC),
+            pl.BlockSpec((1, 192, D), lambda i, coord: (start + i, 2 * coord[2] + coord[3], 0)),
+            one(BC, BC),
+            one(192, BC),
+        ]
+        + anywhere(len(so_far))
+    )
     return pl.pallas_call(
         shampoo_kernel,
         grid_spec=pltpu.PrefetchScalarGridSpec(
             num_scalar_prefetch=1,
             grid=(slots,),
-            in_specs=[one(192, BC)] * 4
-            + [
-                one(D, D),
-                one(BC, BC),
-                pl.BlockSpec((1, 192, D), lambda i, coord: (i, 2 * coord[2] + coord[3], 0)),
-                one(BC, BC),
-                one(192, BC),
-            ],
-            out_specs=(one(D, D), one(BC, BC), one(192, BC)),
+            in_specs=in_specs,
+            out_specs=(one(192, BC), one(192, BC), one(D, D), one(BC, BC)),
             scratch_shapes=[pltpu.VMEM((D, BC), jnp.bfloat16)],
         ),
         out_shape=(
+            jax.ShapeDtypeStruct(blk.shape, jnp.float32),
+            jax.ShapeDtypeStruct(blk.shape, jnp.float32),
             jax.ShapeDtypeStruct(lstat.shape, jnp.float32),
             jax.ShapeDtypeStruct(rstat.shape, jnp.float32),
-            jax.ShapeDtypeStruct(blk.shape, jnp.float32),
-        ),
+        ),
+        input_output_aliases={10 + n: n for n in range(len(so_far))},
         compiler_params=pltpu.CompilerParams(vmem_limit_bytes=VMEM_LIMIT),
+        cost_estimate=pl.CostEstimate(
+            flops=4 * slots * D * D * BC,
+            bytes_accessed=8 * slots * 1024 * 1024,
+            transcendentals=0,
+        ),
         name="shampoo",
-    )(coord, *pieces, lstat, rstat, lroot, rroot, blk)
+    )(coord, *pieces, lstat, rstat, lroot, rroot, blk, *so_far)
+
+
+def adam_kernel(embed, head, w, m, v, new_w, new_m, new_v):
+    def step(grad, rate):
+        new_w[0], new_m[0], new_v[0] = adam_step(w[0], grad, m[0], v[0], rate)
+
+    @pl.when(pl.program_id(0) == 0)
+    def _():
+        step(embed[...], 0.3)
+
+    @pl.when(pl.program_id(0) == 1)
+    def _():
+        step(head[...], 0.02)
+
+
+def adam_call(embed, head, w, m, v):
+    rows = w.shape[1]
+    block = next(n for n in (200, 40, 8) if rows % n == 0)
+    steps = rows // block
+    spec = pl.BlockSpec((1, block, D), lambda i, j: (i, j, 0))
+    return pl.pallas_call(
+        adam_kernel,
+        grid=(2, steps),
+        out_shape=(jax.ShapeDtypeStruct(w.shape, jnp.float32),) * 3,
+        in_specs=[
+            pl.BlockSpec((block, D), lambda i, j: (j * (1 - i) + (steps - 1) * i, 0)),
+            pl.BlockSpec((block, D), lambda i, j: (j * i, 0)),
+            spec,
+            spec,
+            spec,
+        ],
+        out_specs=(spec,) * 3,
+        compiler_params=pltpu.CompilerParams(vmem_limit_bytes=VMEM_LIMIT),
+        cost_estimate=pl.CostEstimate(
+            flops=20 * rows * D, bytes_accessed=64 * rows * D, transcendentals=2 * rows * D
+        ),
+        name="adam",
+    )(embed, head, w, m, v)
 
 
 def block_rows():
     x_at, y_at = [], []
     for b in range(NBLK):
         if b < 2:
-            x_at.append(AT_AP), y_at.append(AT_DQ)
+            x_at.append(0), y_at.append(AT_DQ)
         elif b < 4:
-            x_at.append(AT_A), y_at.append(AT_DK)
+            x_at.append(0), y_at.append(AT_DK)
         elif b < 6:
-            x_at.append(AT_A), y_at.append(AT_DV)
+            x_at.append(0), y_at.append(AT_DV)
         elif b < 8:
-            x_at.append(AT_O), y_at.append(AT_DO)
+            x_at.append(1), y_at.append(AT_DO)
         elif b < 16:
-            x_at.append(AT_B), y_at.append(AT_DGATE + (b - 8) // 2 * PAIR_ROWS)
+            x_at.append(2), y_at.append(AT_DGATE + (b - 8) // 2 * PAIR_ROWS)
         elif b < 24:
-            x_at.append(AT_B), y_at.append(AT_DUP + (b - 16) // 2 * PAIR_ROWS)
+            x_at.append(2), y_at.append(AT_DUP + (b - 16) // 2 * PAIR_ROWS)
         else:
-            x_at.append(AT_Z + (b - 24) // 2 * PAIR_ROWS), y_at.append(AT_DH)
+            x_at.append(3 + (b - 24) // 2), y_at.append(AT_DH)
     return jnp.array(x_at, jnp.int32), jnp.array(y_at, jnp.int32)
 
 
@@ -1167,9 +1283,8 @@
     vocab = table_rows * 32
     seqs = 2 * MB
     shares = blocks.astype(jnp.bfloat16)
-    parts = []
-    for slot in range(4):
-        parts.extend(spread(shares[slot]))
+    with jax.named_scope("weights_fourth"):
+        line4 = all_round(shares[3])
     first_pair = vocab_index * MB
     ids = lax.dynamic_slice_in_dim(token_ids, first_pair, MB, 0).reshape(seqs, SLOT)
     lens = lax.dynamic_slice_in_dim(lengths, first_pair, MB, 0).reshape(seqs)
@@ -1209,45 +1324,36 @@
         axis=1,
     )
     message = lax.all_to_all(message, SHARD_AXES, 0, 0, tiled=True)
+    line4, shares, message = together(line4, shares, message)
     any_spill = jnp.max(message[:, MSG - 1]) > 0
     asked_rows = message[:, :CAP].reshape(32 * CAP)
     table_low = tables.astype(jnp.bfloat16).reshape(2 * table_rows, D)
     give = (asked_rows[:, None] == jnp.arange(2 * table_rows)[None, :]).astype(jnp.bfloat16)
     given = low(dot_nn(give, table_low))
+    with jax.named_scope("weights_fourth"):
+        one4, two4 = hop_one(line4), hop_two(line4)
+    with jax.named_scope("weights_third"):
+        line3 = all_round(shares[2])
+    with jax.named_scope("weights_pair"):
+        line = lax.all_gather(shares[:2], "z")
+    line4, one4, two4, line3, given = together(line4, one4, two4, line3, given)
     got = lax.all_to_all(given, SHARD_AXES, 0, 0, tiled=True)
+    with jax.named_scope("weights_third"):
+        one3, two3 = hop_one(line3), hop_two(line3)
+    with jax.named_scope("weights_fourth"):
+        both4 = hop_two(one4)
+    fourth = [line4, one4, two4, both4]
+    line3, one3, two3, both4, line = together(line3, one3, two3, both4, line)
+    with jax.named_scope("weights_pair"):
+        one, two = hop_one(line), hop_two(line)
+    with jax.named_scope("weights_third"):
+        both3 = hop_two(one3)
+    third = [line3, one3, two3, both3]
+    line, one, two, both3, got = together(line, one, two, both3, got)
+    with jax.named_scope("weights_pair"):
+        pair = [line, one, two, hop_two(one)]
     place = (seat[:, None] == seats[None, :]).astype(jnp.bfloat16)
-    quick = low(dot_nn(place, got))
-    all_targets = jnp.sum(
-        jnp.where(
-            places[None, None, None, :]
-            == (lengths[:, :, None] - CMP + jnp.arange(CMP)[None, None, :])[:, :, :, None],
-            token_ids[:, :, None, :],
-            0,
-        ),
-        axis=-1,
-    )
-
-    def rows_slow():
-        gathered = lax.all_gather(table_low.reshape(2, table_rows, D), ("z", "x"), axis=1, tiled=True)
-        held_rows = gathered.shape[1]
-
-        def find(table, wanted_ids):
-            local = wanted_ids - vocab_index * held_rows
-            inside = (local >= 0) & (local < held_rows)
-            rows = jnp.take(table, jnp.clip(local, 0, held_rows - 1), axis=0)
-            return jnp.where(inside[:, None], rows, 0)
-
-        found = jnp.concatenate(
-            [
-                find(gathered[0], token_ids.reshape(-1)).reshape(-1, TOKENS, D),
-                find(gathered[1], all_targets.reshape(-1)).reshape(-1, PAIR_ROWS, D),
-            ],
-            axis=1,
-        )
-        summed = lax.psum(found.astype(jnp.float32), ("y", "core")).astype(jnp.bfloat16)
-        return lax.dynamic_index_in_dim(summed, vocab_index, 0, keepdims=False)
-
-    rows = lax.cond(any_spill, rows_slow, lambda: quick)
+    rows = low(dot_nn(place, got))
     x, truth = rows[:TOKENS], rows[TOKENS:]
     inv_freq = ROPE_BASE ** (-jnp.arange(HDIM // 2).astype(jnp.float32) * 2.0 / HDIM)
     phase = places.astype(jnp.float32)[:, None] * inv_freq[None, :]
@@ -1261,17 +1367,27 @@
         )
 
     turns = turning(phase_pick, 1) + turning(phase, seqs)
-    saved = forward_call(owner, coord, lens, x, gains, turns, parts)
-    plane, other = spread(saved[-1])
-    head_rows = jnp.concatenate([plane, other]).reshape(-1, D)
+    pair[1] = after(pair[1], x, truth, *turns)
+    parts = []
+    for part in fourth + third + pair:
+        parts.extend([part, hop_core(part)])
+    parts = parts[16:] + parts[8:16] + parts[:8]
+    left, *saved = forward_call(owner, coord, lens, x, gains, turns, parts)
+    plane, _ = spread(saved[-1])
+    plane = plane.reshape(-1, D)
+    other = hop_core(plane)
+    left_t = transpose_call(coord, left, hop_core(left))
     wide = -(-table_rows // 128) * 128
     head_low = jnp.pad(table_low[table_rows:], ((0, wide - table_rows), (0, 0)))
-    ext, kept, stat = head_call(head_rows, head_low, table_rows)
-    half = ext.shape[0] // 2
-    ext = merge_call(ext[:half], hop_core(ext[half:])).reshape(4, 4 * PAIR_ROWS, EXT)
-    one = merge_call(ext[1], hop_two(ext[3]))
-    ext = merge_call(ext[0], hop_one(one), hop_two(ext[2])).reshape(4, PAIR_ROWS, EXT)
-    parts_u = [ext[0]] + [ring(ext[step], -step) for step in range(1, 4)]
+    ext_other, kept_other, stat_other = head_call(other, head_low, table_rows)
+    ext_hop = hop_core(ext_other)
+    ext_own, kept_own, stat_own = head_call(plane, head_low, table_rows)
+    both = merge_call([(ext_own, 3), (ext_hop, 3)])[0]
+    two = merge_call([(ext_own, 2), (ext_hop, 2)])[0]
+    one = merge_call([(ext_own, 1), (ext_hop, 1), (hop_two(both), 0)])[0]
+    pieces = merge_call([(ext_own, 0), (ext_hop, 0), (hop_one(one), 0), (hop_two(two), 0)], 4)
+    pieces = lax.optimization_barrier(tuple(pieces) + tuple(left_t))[:4]
+    parts_u = [pieces[0]] + [ring(pieces[step], -step) for step in range(1, 4)]
     marks = jnp.stack([wanted.astype(jnp.float32), targets.astype(jnp.float32)], axis=1)
     marks = jnp.pad(marks, ((0, 0), (0, 126)))
     act, dx, gain_part, info, loss_part = backward_call(
@@ -1290,27 +1406,27 @@
         jnp.sum(chosen * x_at[None, :], axis=1),
         jnp.sum(chosen * y_at[None, :], axis=1),
         coord,
+        *left_t,
         act,
         hop_core(act),
     )
-    share_list, wholes = [], []
-    for slot in range(4):
-        own, one, two, both = grads[4 * slot : 4 * slot + 4]
-        one = low(high(one) + high(hop_two(both)))
-        one = hop_one(one)
-        two = hop_two(two)
-        line = [low(high(own[n]) + high(one[n]) + high(two[n])) for n in range(4)]
-        share = high(line[0])
-        for step in range(1, 4):
-            share = share + high(ring(line[step], -step))
-        share_list.append(share)
-    block_grads = jnp.stack(share_list)
-    near = block_grads.astype(jnp.bfloat16)
-    by_y = hop_y(near)
-    pair = hop_core(jnp.stack([near, by_y]))
-    new_left, new_right, new_blocks = shampoo_call(
-        coord, (near, by_y, pair[0], pair[1]), left_stat, right_stat, left_root, right_root, blocks
-    )
+    def plus(*values):
+        return low(sum(high(value) for value in values))
+
+    own, one, two, both = grads[:4]
+    own3, one3, two3, both3 = grads[4:8]
+    own4, one4, two4, both4 = grads[8:]
+    info, gain_part, loss_part, dx, both, both3 = together(
+        info, gain_part, loss_part, dx, both, both3
+    )
+    with jax.named_scope("grads_pair"):
+        one = plus(one, hop_two(both))
+    with jax.named_scope("grads_third"):
+        one3 = plus(one3, hop_two(both3))
+    sent = low(dot_tn(place[:TOKENS], dx))
+    one, two, one3, two3, both4, sent = together(one, two, one3, two3, both4, sent)
+    with jax.named_scope("grads_pair"):
+        line = plus(own, hop_one(one), hop_two(two)).reshape(8, 192, BC)
     told = jnp.concatenate(
         [
             info[:, :3].reshape(-1),
@@ -1329,7 +1445,9 @@
     for other_core in range(2):
         for rel in range(4):
             for back in range(4):
-                sources.append(flat_of(*source_of((zi, xi, yi, ci), other_core, rel, back)))
+                sources.append(
+                    flat_of((zi + 4 - back) % 4, *place_of((zi, xi, yi, ci), other_core, rel))
+                )
     sources = jnp.stack(sources)
     infos = jnp.sum(
         jnp.where(
@@ -1343,34 +1461,55 @@
         [infos[:, :2], infos[:, 2:3] - (shard * table_rows).astype(jnp.float32)], axis=1
     )
     infos = jnp.pad(infos, ((0, 0), (0, 125)))
-    grad_head = head_grad_call(head_rows, kept, stat, infos)[:table_rows]
-    place_x = place[:TOKENS]
-    sent = low(dot_tn(place_x, dx))
+    line, one3, two3, both4, infos = together(line, one3, two3, both4, infos)
+    grad_head = head_grad_call(
+        (plane, other), (kept_own, kept_other), (stat_own, stat_other), infos
+    )
+    with jax.named_scope("grads_pair"):
+        pair = lax.psum_scatter(line, "z", scatter_dimension=0, tiled=True)
+    with jax.named_scope("grads_third"):
+        one3, two3 = hop_one(one3), hop_two(two3)
+        line3 = [plus(own3[n], one3[n], two3[n]) for n in range(4)]
+    with jax.named_scope("grads_fourth"):
+        one4 = plus(one4, hop_two(both4))
+    *line3, one4, two4, grad_head = together(*line3, one4, two4, grad_head)
+    with jax.named_scope("grads_third"):
+        third = plus(line3[0], *[ring(line3[step], -step) for step in range(1, 4)])
+    with jax.named_scope("grads_fourth"):
+        one4, two4 = hop_one(one4), hop_two(two4)
+        line4 = [plus(own4[n], one4[n], two4[n]) for n in range(4)]
     back_rows = lax.all_to_all(sent, SHARD_AXES, 0, 0, tiled=True)
     take_back = (asked_rows[None, :] == jnp.arange(table_rows)[:, None]).astype(jnp.bfloat16)
 
-    def embed_slow():
-        all_dx = lax.all_gather(dx, ("y", "core"), axis=0, tiled=True).astype(jnp.float32)
-        held_rows = table_rows * 8
-        local = token_ids.reshape(-1) - vocab_index * held_rows
-        inside = (local >= 0) & (local < held_rows)
-        grad = (
-            jnp.zeros((held_rows, D), jnp.float32)
-            .at[jnp.clip(local, 0, held_rows - 1)]
-            .add(jnp.where(inside[:, None], all_dx, 0.0))
+    grad_embed = dot_nn(take_back, back_rows)
+    new_tables, new_table_moment, new_table_second = adam_call(
+        grad_embed, grad_head, tables, table_moment, table_second
+    )
+    third, new_tables, *line4 = together(third, new_tables, *line4)
+    with jax.named_scope("grads_fourth"):
+        fourth = plus(line4[0], *[ring(line4[step], -step) for step in range(1, 4)])
+    def finish(start, near, so_far):
+        by_y = hop_y(near)
+        return shampoo_call(
+            start,
+            coord,
+            (near, by_y, hop_core(near), hop_core(by_y)),
+            left_stat,
+            right_stat,
+            left_root,
+            right_root,
+            blocks,
+            so_far,
         )
-        return lax.psum_scatter(grad, ("z", "x"), scatter_dimension=0, tiled=True)
-
-    grad_embed = lax.cond(any_spill, embed_slow, lambda: dot_nn(take_back, back_rows))
-    new_embed = adam_step(tables[0], grad_embed, table_moment[0], table_second[0], 0.3)
-    new_head = adam_step(tables[1], grad_head, table_moment[1], table_second[1], 0.02)
-    new_tables, new_table_moment, new_table_second = (
-        jnp.stack([e, h]) for e, h in zip(new_embed, new_head)
+
+    results = finish(0, pair, ())
+    new_blocks, block_grads, new_left, new_right = finish(
+        2, after(jnp.stack([third, fourth]), results[0]), results
     )
     new_gains, new_gain_moment, new_gain_second = adam_step(
         gains, gain_grad, gain_moment, gain_second, GAIN_RATE
     )
-    return (
+    quick = (
         new_blocks,
         block_grads,
         new_left,
@@ -1383,6 +1522,30 @@
         new_gain_second,
         loss_sum,
     )
+    whole = (
+        token_ids,
+        lengths,
+        comp_mask,
+        ref_logp,
+        owner,
+        blocks,
+        left_stat,
+        right_stat,
+        left_root,
+        right_root,
+        tables,
+        table_moment,
+        table_second,
+        gains,
+        gain_moment,
+        gain_second,
+    )
+    def slow(state):
+        outs = list(per_device(("z", "x"), ("y", "core"), *whole))
+        outs[1] = with_layout_constraint(outs[1], Layout((0, 1, 2)))
+        return jnp.zeros((), bool), tuple(outs)
+
+    return lax.while_loop(lambda state: state[0], slow, (any_spill, quick))[1]
 
 
 def solution(mesh):
@@ -1394,7 +1557,7 @@
     else:
         dp, vocab = ("dp",), ("vocab",)
         where = mesh
-        body = per_device
+        body = functools.partial(per_device, ("dp",), ("vocab",))
     placed = (
         P(dp, None, None),
         P(dp, None),

time: 565 us -> 492 us (0.87)
  starting transfers between devices: 124 us -> 72.1 us
  other arithmetic: 69.6 us -> 35.1 us
  Pallas kernels: 106 us -> 123 us
  waiting for transfers between devices: 187 us -> 199 us
  loops' own time: 8.3 us -> 1.17 us
    another operation x19 -> x6, other arithmetic: 48 us -> 6.57 us  [the longest x2 3.67 us: all_round(): return jnp.stack([chunk] + [ring(chunk, step) for step in range(1, 4)])]
    ppermute x30 -> x18, starting transfers between devices: 65.5 us -> 29.3 us  [ring(): lax.ppermute(value, AXES, moves(lambda z, x, y, c: ((z + step) % 4, x, y,...]
    ppermute x10 -> x8, waiting for transfers between devices: 23.8 us -> 49.7 us  [hop_one(): lax.ppermute(value, AXES, moves(lambda z, x, y, c: (z, 1 - x, y, c) if c...]
    pallas_call x6 -> x9, Pallas kernels: 58 us -> 79.4 us  [the longest x1 20.3 us: backward_call(): pl.pallas_call(backward_kernel, out_shape=(jax.ShapeDtypeStruct((RIGHT_RO...]
    ppermute x30 -> x18, waiting for transfers between devices: 50.1 us -> 33.3 us  [ring(): lax.ppermute(value, AXES, moves(lambda z, x, y, c: ((z + step) % 4, x, y,...]
    ppermute x20 -> x16, waiting for transfers between devices: 86.3 us -> 99.5 us  [hop_two(): lax.ppermute(value, AXES, moves(lambda z, x, y, c: (z, x, 1 - y, c) if c...]
    all_to_all x1, waiting for transfers between devices: 14.3 us -> 2.08 us  [per_core(): message = lax.all_to_all(message, SHARD_AXES, 0, 0, tiled=True)]
    convert_element_type x8 -> x7, other arithmetic: 2.54 us -> 12.2 us  [low(): return value.astype(jnp.bfloat16)]
  transfers between devices with their start and end apart: 73 -> 70, of which waited for: 33 -> 29; matrix products, arithmetic and copies ran while one was open for 16% -> 12% of each run, Pallas kernels for 6% -> 10%
where the time goes in v2:
time: 492 us; the launch traced here: 486 us
  waiting for transfers between devices  199 us (40%)
  Pallas kernels  123 us (25%)
  starting transfers between devices  72.1 us (15%)
  other arithmetic  35.1 us (7%)
  local copies, waits for them, and re-layouts  28.3 us (6%)
  between operations  16.7 us (3%)
  matrix products  10.5 us (2%)
    ppermute x16, waiting for transfers between devices, hop_two(): lax.ppermute(value, AXES, moves(lambda z, x, y, c: (z, x, 1 - y, c) if c...  99.5 us
    ppermute x8, waiting for transfers between devices, hop_one(): lax.ppermute(value, AXES, moves(lambda z, x, y, c: (z, 1 - x, y, c) if c...  49.7 us
    ppermute x18, waiting for transfers between devices, ring(): lax.ppermute(value, AXES, moves(lambda z, x, y, c: ((z + step) % 4, x, y,...  33.3 us
    ppermute x18, starting transfers between devices, ring(): lax.ppermute(value, AXES, moves(lambda z, x, y, c: ((z + step) % 4, x, y,...  29.3 us
    pallas_call x1, Pallas kernels, backward_call(): pl.pallas_call(backward_kernel, out_shape=(jax.ShapeDtypeStruct((RIGHT_RO...  20.3 us
    pallas_call x1, Pallas kernels, adam_call(): pl.pallas_call(adam_kernel, grid=(2, steps), out_shape=(jax.ShapeDtypeStr...  18.3 us
    pallas_call x2, Pallas kernels, head_call(): pl.pallas_call(functools.partial(head_kernel, real), grid=(number // 256,...  17 us
    ppermute x16, starting transfers between devices, hop_two(): lax.ppermute(value, AXES, moves(lambda z, x, y, c: (z, x, 1 - y, c) if c...  16.3 us
  transfers between devices with their start and end apart: 70, of which 29 were waited for; matrix products, arithmetic and copies ran while one was open for 12% of the time, Pallas kernels for 10%

profile of v2, /device:TPU:0, one launch (start us, length us, event | category | flops | bytes accessed | tf_op | source)
XLA Modules:
  0.0 485.8 jit_solution(8110726465282163620)
XLA Ops:
  43.2 3.9 fusion.190
  50.9 3.6 collective-permute-done.3.rest_18_.rest_32_
  54.5 3.9 all-to-all-start.1
  62.2 22.4 %collective-permute-done.10.rest_22_.rest_36_ = bf16[4,192,384]{2,1,0:T(8,128)(2,1)} collective-permute-done((bf16[4,192,384]{2,1,0:T(8,128)(2,1)}, bf16[4,192,384]{2,1,0:T(8,128)(2,1)}, u32[]{:S(2)}, u32[]{:S(2)}) %collective-permute-start.10) | collective-permute-done | bytes 589856 | tf_op jit(solution)/shard_map/weights_fourth/ppermute | solution.py:518
  86.2 6.4 %collective-permute-done.9.rest_12_.rest_26_ = bf16[4,192,384]{2,1,0:T(8,128)(2,1)} collective-permute-done((bf16[4,192,384]{2,1,0:T(8,128)(2,1)}, bf16[4,192,384]{2,1,0:T(8,128)(2,1)}, u32[]{:S(2)}, u32[]{:S(2)}) %collective-permute-start.9) | collective-permute-done | bytes 589856 | tf_op jit(solution)/shard_map/weights_third/ppermute | solution.py:518
  95.2 31.8 %collective-permute-done.13.rest_14_.rest_28_ = bf16[4,192,384]{2,1,0:T(8,128)(2,1)} collective-permute-done((bf16[4,192,384]{2,1,0:T(8,128)(2,1)}, bf16[4,192,384]{2,1,0:T(8,128)(2,1)}, u32[]{:S(2)}, u32[]{:S(2)}) %collective-permute-start.13) | collective-permute-done | bytes 589856 | tf_op jit(solution)/shard_map/weights_third/ppermute | solution.py:518
  136.9 6.7 %collective-permute-done.17.rest_6_.rest_20_ = bf16[4,2,192,384]{3,2,1,0:T(8,128)(2,1)} collective-permute-done((bf16[4,2,192,384]{3,2,1,0:T(8,128)(2,1)}, bf16[4,2,192,384]{3,2,1,0:T(8,128)(2,1)}, u32[]{:S(2)}, u32[]{:S(2)}) %collective-permute-start.17) | collective-permute-done | bytes 1179680 | tf_op jit(solution)/shard_map/weights_pair/ppermute | solution.py:518
  147.7 15.2 %layer_forward.1 = (bf16[704,768]{1,0:T(8,128)(2,1)}, bf16[64,768]{1,0:T(8,128)(2,1)}, bf16[256,768]{1,0:T(8,128)(2,1)}, bf16[256,768]{1,0:T(8,128)(2,1)}, f32[6...) custom-call(s32[32]{0:T(128)S(1)} %copy-done.171, ...), custom_call_target="tpu_custom_call" | custom-call | tf_op jit(solution)/shard_map/layer_forward/pallas_call | solution.py:734
  170.4 3.7 collective-permute-done.29
  177.3 9.8 %collective-permute-done.31 = bf16[4,64,768]{2,1,0:T(8,128)(2,1)S(1)} collective-permute-done((bf16[4,64,768]{2,1,0:T(8,128)(2,1)S(1)}, bf16[4,64,768]{2,1,0:T(8,128)(2,1)S(1)}, u32[]{:S(2)}, u32[]{:S(2)}) %collective-permute-start.31) | collective-permute-done | bytes 393248 | tf_op jit(solution)/shard_map/ppermute | solution.py:510
  187.2 7.6 %collective-permute-done.33 = bf16[4,64,768]{2,1,0:T(8,128)(2,1)S(1)} collective-permute-done((bf16[4,64,768]{2,1,0:T(8,128)(2,1)S(1)}, bf16[4,64,768]{2,1,0:T(8,128)(2,1)S(1)}, u32[]{:S(2)}, u32[]{:S(2)}) %collective-permute-start.33) | collective-permute-done | bytes 393248 | tf_op jit(solution)/shard_map/ppermute | solution.py:518
  198.7 8.5 %head_forward.3 = (bf16[1024,896]{1,0:T(8,128)(2,1)}, bf16[1024,1024]{1,0:T(8,128)(2,1)}, f32[1024,128]{1,0:T(8,128)}) custom-call(bf16[1024,768]{1,0:T(8,128)(2,1)} %collective-permute-done.34.rows.rows_b, bf16[1024,768]{1,0:T(8,128)(2,1)} %pad.15.head), custom_call_target="tpu_custom_call" | custom-call | flops 3221225472 | bytes 2097152 | tf_op jit(solution)/shard_map/head_forward/pallas_call | solution.py:833
  207.7 8.5 %head_forward.2 = (bf16[1024,896]{1,0:T(8,128)(2,1)}, bf16[1024,1024]{1,0:T(8,128)(2,1)}, f32[1024,128]{1,0:T(8,128)}) custom-call(bf16[1024,768]{1,0:T(8,128)(2,1)} %bitcast.571, bf16[1024,768]{1,0:T(8,128)(2,1)} %pad.15.head), custom_call_target="tpu_custom_call" | custom-call | flops 3221225472 | bytes 2097152 | tf_op jit(solution)/shard_map/head_forward/pallas_call | solution.py:833
  224.4 4.2 collective-permute-done.36.refs_2_
  237.2 3.6 collective-permute-done.37.refs_2_
  244.7 4.0 collective-permute-start.39
  252.5 5.5 %collective-permute-done.40.rest_12_ = bf16[64,896]{1,0:T(8,128)(2,1)S(1)} collective-permute-done((bf16[64,896]{1,0:T(8,128)(2,1)}, bf16[64,896]{1,0:T(8,128)(2,1)S(1)}, u32[]{:S(2)}, u32[]{:S(2)}) %collective-permute-start.40) | collective-permute-done | bytes 114720 | tf_op jit(solution)/shard_map/ppermute | solution.py:534
  258.7 20.3 %layer_backward.1 = (bf16[1216,768]{1,0:T(8,128)(2,1)}, bf16[256,768]{1,0:T(8,128)(2,1)}, f32[3,768]{1,0:T(4,128)}, f32[64,128]{1,0:T(8,128)}, f32[1,128]{1,0:T(1,128)}) custom-call(s32[32]{0:T(128)S(1)} %copy-done.171, s32[4]{0:T(128)} %pad_add_fusion.coord, s32[4]{0:T(128)} %copy-done.173, f32[4]{0:T(128)} %reshape.1151.refs, bf16[256,768]{1,0:T(8,128)(2,1)} %slice.564.x, ...), custom_call_target="tpu_custom_call" | custom-call | tf_op jit(solution)/shard_map/layer_backward/pallas_call | solution.py:1007
  280.0 3.2 collective-permute-done.42.theirs
  284.4 11.7 %weight_grads.1 = (bf16[4,2,192,384]{3,2,1,0:T(8,128)(2,1)}, bf16[4,2,192,384]{3,2,1,0:T(8,128)(2,1)}, bf16[4,2,192,384]{3,2,1,0:T(8,128)(2,1)}, bf16[4,2,192,38...) custom-call(s32[32]{0:T(128)} %copy-done.174, ...), custom_call_target="tpu_custom_call" | custom-call | tf_op jit(solution)/shard_map/weight_grads/pallas_call | solution.py:1122
  304.2 18.2 %collective-permute-done.44 = bf16[4,192,384]{2,1,0:T(8,128)(2,1)} collective-permute-done((bf16[4,192,384]{2,1,0:T(8,128)(2,1)}, bf16[4,192,384]{2,1,0:T(8,128)(2,1)}, u32[]{:S(2)}, u32[]{:S(2)}) %collective-permute-start.44) | collective-permute-done | bytes 589856 | tf_op jit(solution)/shard_map/grads_third/ppermute | solution.py:518
  331.6 4.6 all-to-all-start.3
  336.2 28.6 %collective-permute-done.45 = bf16[4,2,192,384]{3,2,1,0:T(8,128)(2,1)} collective-permute-done((bf16[4,2,192,384]{3,2,1,0:T(8,128)(2,1)S(1)}, bf16[4,2,192,384]{3,2,1,0:T(8,128)(2,1)}, u32[]{:S(2)}, u32[]{:S(2)}) %collective-permute-start.45) | collective-permute-done | bytes 1179680 | tf_op jit(solution)/shard_map/grads_pair/ppermute | solution.py:510
  364.9 3.5 add_convert_fusion.10
  370.5 11.7 %head_grad.1.head = f32[1024,768]{1,0:T(8,128)} custom-call(bf16[1024,768]{1,0:T(8,128)(2,1)} %bitcast.572, bf16[1024,768]{1,0:T(8,128)(2,1)} %collective-permute-done.34.rows.rows_b, bf16[1024,1024]{1,0:T(8,128)(2,1)} %get-tuple-element.405.kept_a, bf16[1024,1024]{1,0:T(8,128)(2,1)} %get-tuple-element.406.kept_b, f32[1024,128]{1,0:T(8,128)} %get-tuple-element.407.stat_a, ...), custom_call_target="tpu_custom_call" | custom-call | flops 3221225472 | bytes 4194304 | tf_op jit(solution)/shard_map/head_grad/pallas_call | solution.py:892
  396.6 10.5 %collective-permute-done.51 = bf16[192,384]{1,0:T(8,128)(2,1)S(1)} collective-permute-done((bf16[192,384]{1,0:T(8,128)(2,1)S(1)}, bf16[192,384]{1,0:T(8,128)(2,1)S(1)}, u32[]{:S(2)}, u32[]{:S(2)}) %collective-permute-start.51) | collective-permute-done | bytes 147488 | tf_op jit(solution)/shard_map/grads_third/ppermute | solution.py:534
  407.8 3.1 fusion.189.embed
  410.9 18.3 %adam.1 = (f32[2,1000,768]{2,1,0:T(8,128)}, f32[2,1000,768]{2,1,0:T(8,128)}, f32[2,1000,768]{2,1,0:T(8,128)}) custom-call(f32[1000,768]{1,0:T(8,128)} %fusion.189.embed, f32[1024,768]{1,0:T(8,128)} %head_grad.1.head, f32[2,1000,768]{2,1,0:T(8,128)} %w.1, f32[2,1000,768]{2,1,0:T(8,128)} %m.1, f32[2,1000,768]{2,1,0:T(8,128)} %v.1), custom_call_target="tpu_custom_call" | custom-call | flops 15360000 | bytes 49152000 | tf_op jit(solution)/shard_map/adam/pallas_call | solution.py:1220
  439.6 7.2 %collective-permute-done.56 = bf16[192,384]{1,0:T(8,128)(2,1)S(1)} collective-permute-done((bf16[192,384]{1,0:T(8,128)(2,1)S(1)}, bf16[192,384]{1,0:T(8,128)(2,1)S(1)}, u32[]{:S(2)}, u32[]{:S(2)}) %collective-permute-start.56) | collective-permute-done | bytes 147488 | tf_op jit(solution)/shard_map/grads_fourth/ppermute | solution.py:534
  448.5 7.4 %shampoo.2 = (f32[4,192,384]{2,1,0:T(8,128)}, f32[4,192,384]{2,1,0:T(8,128)}, f32[4,768,768]{2,1,0:T(8,128)}, f32[4,384,384]{2,1,0:T(8,128)}) custom-call(s32[4]{0:T(128)} %pad_add_fusion.coord, bf16[2,192,384]{2,1,0:T(8,128)(2,1)} %reduce-scatter.8.cloned.1.call-done.refs_0_, bf16[2,192,384]{2,1,0:T(8,128)(2,1)} %copy-done.119, ...), custom_call_target="tpu_custom_call" | custom-call | flops 1811939328 | bytes 16777216 | tf_op jit(solution)/shard_map/shampoo/pallas_call | solution.py:1176
  461.0 3.7 collective-permute-done.61.refs_1_
  469.7 7.6 %shampoo.3 = (f32[4,192,384]{2,1,0:T(8,128)}, f32[4,192,384]{2,1,0:T(8,128)}, f32[4,768,768]{2,1,0:T(8,128)}, f32[4,384,384]{2,1,0:T(8,128)}) custom-call(s32[4]{0:T(128)} %pad_add_fusion.coord, bf16[2,192,384]{2,1,0:T(8,128)(2,1)} %pad_maximum_fusion.27.refs_0_, ...), custom_call_target="tpu_custom_call", output_to_operand_aliasing={{0}: (10, {}), {1}: (11, {}), {2}: (12, {}), {3}: (13, {})} | custom-call | flops 1811939328 | bytes 16777216 | tf_op jit(solution)/shard_map/shampoo/pallas_call | solution.py:1176
  (308 shorter events, 160.2 us)
Async XLA Ops:
  10.0 19.3 %collective-permute-start = (bf16[192,384]{1,0:T(8,128)(2,1)}, bf16[192,384]{1,0:T(8,128)(2,1)S(1)}, u32[]{:S(2)}, u32[]{:S(2)}) collective-permute-start(bf16[192,384]{1,0:T(8,128)(2,1)} %get-tuple-element.970), channel_id=1, source_target_pairs={{0,8},{1,9},{2,10},{3,11},{4,12},{5,13},{6,14},{7,15},{8,16},{9,17... | collective-permute-start | bytes 442376 | tf_op jit(solution)/shard_map/weights_fourth/ppermute | solution.py:534
  13.0 16.3 %collective-permute-start.1 = (bf16[192,384]{1,0:T(8,128)(2,1)}, bf16[192,384]{1,0:T(8,128)(2,1)S(1)}, u32[]{:S(2)}, u32[]{:S(2)}) collective-permute-start(bf16[192,384]{1,0:T(8,128)(2,1)} %get-tuple-element.970), channel_id=1, source_target_pairs={{0,16},{1,17},{2,18},{3,19},{4,20},{5,21},{6,22},{7,23},{8,24},{9,... | collective-permute-start | bytes 442376 | tf_op jit(solution)/shard_map/weights_fourth/ppermute | solution.py:534
  26.2 66.3 %all-gather.20.cloned.1.call-start = ((), (), s32[]{:S(2)}) async-start(), calls=%async_computation.11 | async-start | bytes 1474560 | tf_op jit(solution)/shard_map/weights_pair/all_gather | solution.py:1338
  38.7 15.7 %collective-permute-start.3 = (bf16[4,192,384]{2,1,0:T(8,128)(2,1)}, bf16[4,192,384]{2,1,0:T(8,128)(2,1)}, u32[]{:S(2)}, u32[]{:S(2)}) collective-permute-start(bf16[4,192,384]{2,1,0:T(8,128)(2,1)} %pad_maximum_fusion.24.rest_16_.rest_30_), channel_id=1, source_target_pairs={{0,4},{1,3},{2,6},{3,1},{4,0},{5,7},{6,2},{7,5},{8,12},{9,11},{10,... | collective-permute-start | bytes 1769480 | tf_op jit(solution)/shard_map/weights_fourth/ppermute | solution.py:510
  39.9 14.6 %collective-permute-start.4 = (bf16[4,192,384]{2,1,0:T(8,128)(2,1)}, bf16[4,192,384]{2,1,0:T(8,128)(2,1)}, u32[]{:S(2)}, u32[]{:S(2)}) collective-permute-start(bf16[4,192,384]{2,1,0:T(8,128)(2,1)} %pad_maximum_fusion.24.rest_16_.rest_30_), channel_id=1, source_target_pairs={{0,2},{1,5},{2,0},{3,7},{4,6},{5,1},{6,4},{7,3},{8,10},{9,13},{10,... | collective-permute-start | bytes 1769480 | tf_op jit(solution)/shard_map/weights_fourth/ppermute | solution.py:518
  54.5 72.6 %all-to-all-start.1 = ((bf16[32,24,768]{2,1,0:T(8,128)(2,1)}), bf16[32,24,768]{2,1,0:T(8,128)(2,1)}, u32[]{:S(2)}, u32[]{:S(2)}) async-start(bf16[32,24,768]{2,1,0:T(8,128)(2,1)} %bitcast.581), calls=%async_computation.6 | async-start | bytes 2359296 | tf_op jit(solution)/shard_map/all_to_all | solution.py:1340
  58.3 26.2 %collective-permute-start.10 = (bf16[4,192,384]{2,1,0:T(8,128)(2,1)}, bf16[4,192,384]{2,1,0:T(8,128)(2,1)}, u32[]{:S(2)}, u32[]{:S(2)}) collective-permute-start(bf16[4,192,384]{2,1,0:T(8,128)(2,1)} %collective-permute-done.3.rest_18_.rest_32_), channel_id=1, source_target_pairs={{0,2},{1,5},{2,0},{3,7},{4,6},{5,1},{6,4},{7,3},{8,10},{9,13},{10,... | collective-permute-start | bytes 1769480 | tf_op jit(solution)/shard_map/weights_fourth/ppermute | solution.py:518
  60.2 26.0 %collective-permute-start.8 = (bf16[4,192,384]{2,1,0:T(8,128)(2,1)}, bf16[4,192,384]{2,1,0:T(8,128)(2,1)}, u32[]{:S(2)}, u32[]{:S(2)}) collective-permute-start(bf16[4,192,384]{2,1,0:T(8,128)(2,1)} %pad_maximum_fusion.25.rest_8_.rest_22_), channel_id=1, source_target_pairs={{0,4},{1,3},{2,6},{3,1},{4,0},{5,7},{6,2},{7,5},{8,12},{9,11},{10,... | collective-permute-start | bytes 1769480 | tf_op jit(solution)/shard_map/weights_third/ppermute | solution.py:510
  61.7 30.9 %collective-permute-start.9 = (bf16[4,192,384]{2,1,0:T(8,128)(2,1)}, bf16[4,192,384]{2,1,0:T(8,128)(2,1)}, u32[]{:S(2)}, u32[]{:S(2)}) collective-permute-start(bf16[4,192,384]{2,1,0:T(8,128)(2,1)} %pad_maximum_fusion.25.rest_8_.rest_22_), channel_id=1, source_target_pairs={{0,2},{1,5},{2,0},{3,7},{4,6},{5,1},{6,4},{7,3},{8,10},{9,13},{10,... | collective-permute-start | bytes 1769480 | tf_op jit(solution)/shard_map/weights_third/ppermute | solution.py:518
  92.6 34.5 %collective-permute-start.11 = (bf16[4,2,192,384]{3,2,1,0:T(8,128)(2,1)}, bf16[4,2,192,384]{3,2,1,0:T(8,128)(2,1)}, u32[]{:S(2)}, u32[]{:S(2)}) collective-permute-start(bf16[4,2,192,384]{3,2,1,0:T(8,128)(2,1)} %bitcast.23.rest_0_.rest_14_), channel_id=1, source_target_pairs={{0,4},{1,3},{2,6},{3,1},{4,0},{5,7},{6,2},{7,5},{8,12},{9,11},{10,... | collective-permute-start | bytes 3538952 | tf_op jit(solution)/shard_map/weights_pair/ppermute | solution.py:510
  92.6 34.5 %collective-permute-start.12 = (bf16[4,2,192,384]{3,2,1,0:T(8,128)(2,1)}, bf16[4,2,192,384]{3,2,1,0:T(8,128)(2,1)}, u32[]{:S(2)}, u32[]{:S(2)}) collective-permute-start(bf16[4,2,192,384]{3,2,1,0:T(8,128)(2,1)} %bitcast.23.rest_0_.rest_14_), channel_id=1, source_target_pairs={{0,2},{1,5},{2,0},{3,7},{4,6},{5,1},{6,4},{7,3},{8,10},{9,13},{10,... | collective-permute-start | bytes 3538952 | tf_op jit(solution)/shard_map/weights_pair/ppermute | solution.py:518
  92.9 34.2 %collective-permute-start.13 = (bf16[4,192,384]{2,1,0:T(8,128)(2,1)}, bf16[4,192,384]{2,1,0:T(8,128)(2,1)}, u32[]{:S(2)}, u32[]{:S(2)}) collective-permute-start(bf16[4,192,384]{2,1,0:T(8,128)(2,1)} %collective-permute-done.8.rest_10_.rest_24_), channel_id=1, source_target_pairs={{0,2},{1,5},{2,0},{3,7},{4,6},{5,1},{6,4},{7,3},{8,10},{9,13},{10,... | collective-permute-start | bytes 1769480 | tf_op jit(solution)/shard_map/weights_third/ppermute | solution.py:518
  94.6 35.8 %collective-permute-start.24 = (bf16[4,192,384]{2,1,0:T(8,128)(2,1)}, bf16[4,192,384]{2,1,0:T(8,128)(2,1)}, u32[]{:S(2)}, u32[]{:S(2)}) collective-permute-start(bf16[4,192,384]{2,1,0:T(8,128)(2,1)} %collective-permute-done.3.rest_18_.rest_32_), channel_id=1, source_target_pairs={{0,1},{1,0},{2,3},{3,2},{4,5},{5,4},{6,7},{7,6},{8,9},{9,8},{10,11... | collective-permute-start | bytes 1769480 | tf_op jit(solution)/shard_map/ppermute | solution.py:526
  94.6 35.4 %collective-permute-start.23 = (bf16[4,192,384]{2,1,0:T(8,128)(2,1)}, bf16[4,192,384]{2,1,0:T(8,128)(2,1)}, u32[]{:S(2)}, u32[]{:S(2)}) collective-permute-start(bf16[4,192,384]{2,1,0:T(8,128)(2,1)} %pad_maximum_fusion.24.rest_16_.rest_30_), channel_id=1, source_target_pairs={{0,1},{1,0},{2,3},{3,2},{4,5},{5,4},{6,7},{7,6},{8,9},{9,8},{10,11... | collective-permute-start | bytes 1769480 | tf_op jit(solution)/shard_map/ppermute | solution.py:526
  127.1 16.6 %collective-permute-start.17 = (bf16[4,2,192,384]{3,2,1,0:T(8,128)(2,1)}, bf16[4,2,192,384]{3,2,1,0:T(8,128)(2,1)}, u32[]{:S(2)}, u32[]{:S(2)}) collective-permute-start(bf16[4,2,192,384]{3,2,1,0:T(8,128)(2,1)} %collective-permute-done.11.rest_2_.rest_16_), channel_id=1, source_target_pairs={{0,2},{1,5},{2,0},{3,7},{4,6},{5,1},{6,4},{7,3},{8,10},{9,13},{10,... | collective-permute-start | bytes 3538952 | tf_op jit(solution)/shard_map/weights_pair/ppermute | solution.py:518
  207.3 26.8 %collective-permute-start.27 = (bf16[704,768]{1,0:T(8,128)(2,1)S(1)}, bf16[704,768]{1,0:T(8,128)(2,1)}, u32[]{:S(2)}, u32[]{:S(2)}) collective-permute-start(bf16[704,768]{1,0:T(8,128)(2,1)S(1)} %copy-done.101), channel_id=1, source_target_pairs={{0,1},{1,0},{2,3},{3,2},{4,5},{5,4},{6,7},{7,6},{8,9},{9,8},{10,11... | collective-permute-start | bytes 3244040 | tf_op jit(solution)/shard_map/ppermute | solution.py:526
  222.5 14.7 %collective-permute-start.38 = (bf16[256,896]{1,0:T(8,128)(2,1)}, bf16[256,896]{1,0:T(8,128)(2,1)S(1)}, u32[]{:S(2)}, u32[]{:S(2)}) collective-permute-start(bf16[256,896]{1,0:T(8,128)(2,1)} %merge_parts.6), channel_id=1, source_target_pairs={{0,2},{1,5},{2,0},{3,7},{4,6},{5,1},{6,4},{7,3},{8,10},{9,13},{10,... | collective-permute-start | bytes 1376264 | tf_op jit(solution)/shard_map/ppermute | solution.py:518
  296.2 28.4 %collective-permute-start.43 = (bf16[4,2,192,384]{3,2,1,0:T(8,128)(2,1)}, bf16[4,2,192,384]{3,2,1,0:T(8,128)(2,1)S(1)}, u32[]{:S(2)}, u32[]{:S(2)}) collective-permute-start(bf16[4,2,192,384]{3,2,1,0:T(8,128)(2,1)} %get-tuple-element.385), channel_id=1, source_target_pairs={{0,2},{1,5},{2,0},{3,7},{4,6},{5,1},{6,4},{7,3},{8,10},{9,13},{10,... | collective-permute-start | bytes 3538952 | tf_op jit(solution)/shard_map/grads_pair/ppermute | solution.py:518
  296.6 25.8 %collective-permute-start.44 = (bf16[4,192,384]{2,1,0:T(8,128)(2,1)}, bf16[4,192,384]{2,1,0:T(8,128)(2,1)}, u32[]{:S(2)}, u32[]{:S(2)}) collective-permute-start(bf16[4,192,384]{2,1,0:T(8,128)(2,1)} %get-tuple-element.388), channel_id=1, source_target_pairs={{0,2},{1,5},{2,0},{3,7},{4,6},{5,1},{6,4},{7,3},{8,10},{9,13},{10,... | collective-permute-start | bytes 1769480 | tf_op jit(solution)/shard_map/grads_third/ppermute | solution.py:518
  299.7 28.2 %all-to-all-start.2 = ((f32[32,1,2560]{2,1,0:T(1,128)}), f32[32,1,2560]{2,1,0:T(1,128)S(1)}, u32[]{:S(2)}, u32[]{:S(2)}) async-start(f32[32,1,2560]{2,1,0:T(1,128)} %broadcast_in_dim.197), calls=%async_computation.7 | async-start | bytes 655360 | tf_op jit(solution)/shard_map/all_to_all | solution.py:1438
  327.2 37.7 %collective-permute-start.45 = (bf16[4,2,192,384]{3,2,1,0:T(8,128)(2,1)S(1)}, bf16[4,2,192,384]{3,2,1,0:T(8,128)(2,1)}, u32[]{:S(2)}, u32[]{:S(2)}) collective-permute-start(bf16[4,2,192,384]{3,2,1,0:T(8,128)(2,1)S(1)} %add_convert_fusion.11), channel_id=1, source_target_pairs={{0,4},{1,3},{2,6},{3,1},{4,0},{5,7},{6,2},{7,5},{8,12},{9,11},{10,... | collective-permute-start | bytes 3538952 | tf_op jit(solution)/shard_map/grads_pair/ppermute | solution.py:510
  327.6 37.2 %collective-permute-start.46 = (bf16[4,2,192,384]{3,2,1,0:T(8,128)(2,1)}, bf16[4,2,192,384]{3,2,1,0:T(8,128)(2,1)}, u32[]{:S(2)}, u32[]{:S(2)}) collective-permute-start(bf16[4,2,192,384]{3,2,1,0:T(8,128)(2,1)} %get-tuple-element.393), channel_id=1, source_target_pairs={{0,2},{1,5},{2,0},{3,7},{4,6},{5,1},{6,4},{7,3},{8,10},{9,13},{10,... | collective-permute-start | bytes 3538952 | tf_op jit(solution)/shard_map/grads_pair/ppermute | solution.py:518
  331.6 76.2 %all-to-all-start.3 = ((bf16[32,24,768]{2,1,0:T(8,128)(2,1)}), bf16[32,24,768]{2,1,0:T(8,128)(2,1)S(1)}, u32[]{:S(2)}, u32[]{:S(2)}) async-start(bf16[32,24,768]{2,1,0:T(8,128)(2,1)} %bitcast.76), calls=%async_computation.8 | async-start | bytes 2359296 | tf_op jit(solution)/shard_map/all_to_all | solution.py:1481
  336.2 93.0 %reduce-scatter.8.cloned.1.call-start = ((), (), s32[]{:S(2)}) async-start(), calls=%async_computation.10 | async-start | bytes 1474560 | tf_op jit(solution)/shard_map/grads_pair/reduce_scatter | solution.py:1469
  368.4 16.3 %collective-permute-start.47 = (bf16[4,192,384]{2,1,0:T(8,128)(2,1)S(1)}, bf16[4,192,384]{2,1,0:T(8,128)(2,1)}, u32[]{:S(2)}, u32[]{:S(2)}) collective-permute-start(bf16[4,192,384]{2,1,0:T(8,128)(2,1)S(1)} %copy-done.106), channel_id=1, source_target_pairs={{0,4},{1,3},{2,6},{3,1},{4,0},{5,7},{6,2},{7,5},{8,12},{9,11},{10,... | collective-permute-start | bytes 1769480 | tf_op jit(solution)/shard_map/grads_third/ppermute | solution.py:510
  368.4 16.3 %collective-permute-start.48 = (bf16[4,192,384]{2,1,0:T(8,128)(2,1)}, bf16[4,192,384]{2,1,0:T(8,128)(2,1)}, u32[]{:S(2)}, u32[]{:S(2)}) collective-permute-start(bf16[4,192,384]{2,1,0:T(8,128)(2,1)} %get-tuple-element.401), channel_id=1, source_target_pairs={{0,2},{1,5},{2,0},{3,7},{4,6},{5,1},{6,4},{7,3},{8,10},{9,13},{10,... | collective-permute-start | bytes 1769480 | tf_op jit(solution)/shard_map/grads_third/ppermute | solution.py:518
  368.9 19.5 %collective-permute-start.49 = (bf16[4,192,384]{2,1,0:T(8,128)(2,1)}, bf16[4,192,384]{2,1,0:T(8,128)(2,1)S(1)}, u32[]{:S(2)}, u32[]{:S(2)}) collective-permute-start(bf16[4,192,384]{2,1,0:T(8,128)(2,1)} %get-tuple-element.403), channel_id=1, source_target_pairs={{0,2},{1,5},{2,0},{3,7},{4,6},{5,1},{6,4},{7,3},{8,10},{9,13},{10,... | collective-permute-start | bytes 1769480 | tf_op jit(solution)/shard_map/grads_fourth/ppermute | solution.py:518
  390.6 16.4 %collective-permute-start.51 = (bf16[192,384]{1,0:T(8,128)(2,1)S(1)}, bf16[192,384]{1,0:T(8,128)(2,1)S(1)}, u32[]{:S(2)}, u32[]{:S(2)}) collective-permute-start(bf16[192,384]{1,0:T(8,128)(2,1)S(1)} %get-tuple-element.412), channel_id=1, source_target_pairs={{0,16},{1,17},{2,18},{3,19},{4,20},{5,21},{6,22},{7,23},{8,24},{9,... | collective-permute-start | bytes 442376 | tf_op jit(solution)/shard_map/grads_third/ppermute | solution.py:534
  391.9 15.2 %collective-permute-start.52 = (bf16[192,384]{1,0:T(8,128)(2,1)S(1)}, bf16[192,384]{1,0:T(8,128)(2,1)S(1)}, u32[]{:S(2)}, u32[]{:S(2)}) collective-permute-start(bf16[192,384]{1,0:T(8,128)(2,1)S(1)} %get-tuple-element.413), channel_id=1, source_target_pairs={{0,8},{1,9},{2,10},{3,11},{4,12},{5,13},{6,14},{7,15},{8,16},{9,17... | collective-permute-start | bytes 442376 | tf_op jit(solution)/shard_map/grads_third/ppermute | solution.py:534
  393.9 37.1 %collective-permute-start.53 = (bf16[4,192,384]{2,1,0:T(8,128)(2,1)}, bf16[4,192,384]{2,1,0:T(8,128)(2,1)}, u32[]{:S(2)}, u32[]{:S(2)}) collective-permute-start(bf16[4,192,384]{2,1,0:T(8,128)(2,1)} %add_convert_fusion.12), channel_id=1, source_target_pairs={{0,4},{1,3},{2,6},{3,1},{4,0},{5,7},{6,2},{7,5},{8,12},{9,11},{10,... | collective-permute-start | bytes 1769480 | tf_op jit(solution)/shard_map/grads_fourth/ppermute | solution.py:510
  393.9 37.1 %collective-permute-start.54 = (bf16[4,192,384]{2,1,0:T(8,128)(2,1)}, bf16[4,192,384]{2,1,0:T(8,128)(2,1)}, u32[]{:S(2)}, u32[]{:S(2)}) collective-permute-start(bf16[4,192,384]{2,1,0:T(8,128)(2,1)} %get-tuple-element.419), channel_id=1, source_target_pairs={{0,2},{1,5},{2,0},{3,7},{4,6},{5,1},{6,4},{7,3},{8,10},{9,13},{10,... | collective-permute-start | bytes 1769480 | tf_op jit(solution)/shard_map/grads_fourth/ppermute | solution.py:518
  432.8 14.0 %collective-permute-start.56 = (bf16[192,384]{1,0:T(8,128)(2,1)S(1)}, bf16[192,384]{1,0:T(8,128)(2,1)S(1)}, u32[]{:S(2)}, u32[]{:S(2)}) collective-permute-start(bf16[192,384]{1,0:T(8,128)(2,1)S(1)} %get-tuple-element.423), channel_id=1, source_target_pairs={{0,16},{1,17},{2,18},{3,19},{4,20},{5,21},{6,22},{7,23},{8,24},{9,... | collective-permute-start | bytes 442376 | tf_op jit(solution)/shard_map/grads_fourth/ppermute | solution.py:534
  (82 other events, 1130.9 us)
Sparse Core Ops, SparseCore 0:
  43.3 39.9 all-gather.19
  368.5 27.4 reduce-scatter.7

commit v3 on v2

--- a/solution.py
+++ b/solution.py
@@ -469,6 +469,7 @@
 PAIR_ROWS = MB * 2 * CMP
 TOKENS = MB * 2 * SLOT
 CAP = 24
+CAP_BACK = 18
 MSG = 32
 EXT = D + 128
 AXES = ("z", "x", "y", "core")
@@ -596,17 +597,17 @@
     for other_core in range(2):
         for rel in range(4):
             x, y, core = place_of(coord, other_core, rel)
-            pair, third, fourth = (
+            pair, third, last = (
                 parts[2 * rel + other_core],
                 parts[8 + 2 * rel + other_core],
-                parts[16 + 2 * rel + other_core],
+                parts[16 + other_core],
             )
 
             def one(n, carry):
                 back = (coord[0] + 4 - n) & 3
                 start(pair.at[n], pl.ds(8 * n + 4 * x, 2), y, core)
                 start(third.at[n], 8 * back + 4 * x + 2, y, core)
-                start(fourth.at[n], 8 * back + 4 * x + 3, y, core)
+                start(last.at[n, rel], 8 * n + 4 * x + 3, y, core)
                 return carry
 
             lax.fori_loop(0, 4, one, 0)
@@ -655,7 +656,7 @@
 
 
 def forward_kernel(owner, coord, lens, x, gains, cos_q, sin_q, cos_k, sin_k, *rest):
-    parts, rest = rest[:24], rest[24:]
+    parts, rest = rest[:18], rest[18:]
     left, q_out, k_out, v_out, h1_out, gate_out, up_out, h2_out, c_out = rest[:9]
     held, sem = rest[9:]
     start_weights(coord, parts, held, sem)
@@ -744,7 +745,7 @@
             made(PAIR_ROWS, D, jnp.float32),
             made(PAIR_ROWS, D, jnp.bfloat16),
         ),
-        in_specs=smem(3) + vmem(6) + anywhere(24),
+        in_specs=smem(3) + vmem(6) + anywhere(18),
         out_specs=tuple(vmem(9)),
         scratch_shapes=[
             pltpu.VMEM((NBLK, D, BC), jnp.bfloat16),
@@ -906,9 +907,9 @@
 def backward_kernel(owner, coord, lens, refs, x, gains, cos_q, sin_q, cos_k, sin_k, *rest):
     q, k, v, h1, gate, up, h2, c = rest[:8]
     truth, wanted, u0, u1, u2, u3 = rest[8:14]
-    parts = rest[14:38]
-    act, dx_out, gain_out, info_out, loss_out = rest[38:43]
-    held, sem = rest[43:]
+    parts = rest[14:32]
+    act, dx_out, gain_out, info_out, loss_out = rest[32:37]
+    held, sem = rest[37:]
     start_weights(coord, parts, held, sem)
     valid, chosen = masks(lens)
     select = jnp.where(chosen, 1.0, 0.0).astype(jnp.bfloat16)
@@ -1013,7 +1014,7 @@
             jax.ShapeDtypeStruct((PAIR_ROWS, 128), jnp.float32),
             jax.ShapeDtypeStruct((1, 128), jnp.float32),
         ),
-        in_specs=smem(4) + vmem(6 + 8 + 2 + 4) + anywhere(24),
+        in_specs=smem(4) + vmem(6 + 8 + 2 + 4) + anywhere(18),
         out_specs=tuple(vmem(5)),
         scratch_shapes=[
             pltpu.VMEM((NBLK, D, BC), jnp.bfloat16),
@@ -1060,14 +1061,14 @@
 
 
 def weight_grad_kernel(block_of, x_at, y_at, coord, picked, tokens, mine, theirs, *rest):
-    pair, singles = rest[:4], (rest[4:8], rest[8:12])
-    near_held, far_held, sem = rest[12:]
+    outs = rest[:-3]
+    near_held, far_held, sem = rest[-3:]
     first = coord[3] == 0
     for group, (k, x_flip) in enumerate((k, x_flip) for k in range(4) for x_flip in range(2)):
         x = coord[1] + x_flip * (1 - 2 * coord[1])
 
         def step(n, carry):
-            z = n if k < 2 else (coord[0] + 4 - n) & 3
+            z = n if k != 2 else (coord[0] + 4 - n) & 3
             slot = 8 * z + 4 * x + k
             block = block_of[slot]
             cut = pl.ds(pl.multiple_of((block & 1) * BC, 128), BC)
@@ -1096,7 +1097,12 @@
         lax.fori_loop(0, 4, step, 0)
 
         def send(held, rel):
-            target = pair[rel].at[:, k] if k < 2 else singles[k - 2][rel]
+            if k == 3:
+                target = outs[8].at[:, rel]
+            elif k == 2:
+                target = outs[4 + rel]
+            else:
+                target = outs[rel].at[:, k]
             pltpu.make_async_copy(held.at[group], target, sem).start()
 
         if x_flip == 0:
@@ -1118,23 +1124,19 @@
     pltpu.make_async_copy(far_held, far_held, sem).wait()
 
 
-def weight_grad_call(block_of, x_at, y_at, coord, picked, tokens, mine, theirs):
+def weight_grad_call(*args):
+    shapes = [(4, 2)] * 4 + [(4,)] * 4 + [(4, 4)]
+    made = [jax.ShapeDtypeStruct(shape + (192, BC), jnp.bfloat16) for shape in shapes]
+    held = pltpu.VMEM((8, 4, 192, BC), jnp.bfloat16)
     return pl.pallas_call(
         weight_grad_kernel,
-        out_shape=tuple(
-            [jax.ShapeDtypeStruct((4, 2, 192, BC), jnp.bfloat16)] * 4
-            + [jax.ShapeDtypeStruct((4, 192, BC), jnp.bfloat16)] * 8
-        ),
+        out_shape=tuple(made),
         in_specs=smem(4) + vmem(4),
-        out_specs=tuple(anywhere(12)),
-        scratch_shapes=[
-            pltpu.VMEM((8, 4, 192, BC), jnp.bfloat16),
-            pltpu.VMEM((8, 4, 192, BC), jnp.bfloat16),
-            pltpu.SemaphoreType.DMA,
-        ],
+        out_specs=tuple(anywhere(len(made))),
+        scratch_shapes=[held, held, pltpu.SemaphoreType.DMA],
         compiler_params=pltpu.CompilerParams(vmem_limit_bytes=VMEM_LIMIT),
         name="weight_grads",
-    )(block_of, x_at, y_at, coord, picked, tokens, mine, theirs)
+    )(*args)
 
 
 def shampoo_kernel(coord, *refs):
@@ -1199,42 +1201,29 @@
     )(coord, *pieces, lstat, rstat, lroot, rroot, blk, *so_far)
 
 
-def adam_kernel(embed, head, w, m, v, new_w, new_m, new_v):
-    def step(grad, rate):
-        new_w[0], new_m[0], new_v[0] = adam_step(w[0], grad, m[0], v[0], rate)
-
-    @pl.when(pl.program_id(0) == 0)
-    def _():
-        step(embed[...], 0.3)
-
-    @pl.when(pl.program_id(0) == 1)
-    def _():
-        step(head[...], 0.02)
-
-
-def adam_call(embed, head, w, m, v):
+def adam_kernel(rate, grad, w, m, v, *rest):
+    new_w, new_m, new_v = rest[-3:]
+    new_w[0], new_m[0], new_v[0] = adam_step(w[0], grad[...], m[0], v[0], rate)
+
+
+def adam_call(table, rate, grad, w, m, v, so_far):
     rows = w.shape[1]
     block = next(n for n in (200, 40, 8) if rows % n == 0)
-    steps = rows // block
-    spec = pl.BlockSpec((1, block, D), lambda i, j: (i, j, 0))
+    spec = pl.BlockSpec((1, block, D), lambda j: (table, j, 0))
     return pl.pallas_call(
-        adam_kernel,
-        grid=(2, steps),
+        functools.partial(adam_kernel, rate),
+        grid=(rows // block,),
         out_shape=(jax.ShapeDtypeStruct(w.shape, jnp.float32),) * 3,
-        in_specs=[
-            pl.BlockSpec((block, D), lambda i, j: (j * (1 - i) + (steps - 1) * i, 0)),
-            pl.BlockSpec((block, D), lambda i, j: (j * i, 0)),
-            spec,
-            spec,
-            spec,
-        ],
+        in_specs=[pl.BlockSpec((block, D), lambda j: (j, 0)), spec, spec, spec]
+        + anywhere(len(so_far)),
         out_specs=(spec,) * 3,
+        input_output_aliases={4 + n: n for n in range(len(so_far))},
         compiler_params=pltpu.CompilerParams(vmem_limit_bytes=VMEM_LIMIT),
         cost_estimate=pl.CostEstimate(
-            flops=20 * rows * D, bytes_accessed=64 * rows * D, transcendentals=2 * rows * D
+            flops=10 * rows * D, bytes_accessed=28 * rows * D, transcendentals=rows * D
         ),
         name="adam",
-    )(embed, head, w, m, v)
+    )(grad, w, m, v, *so_far)
 
 
 def block_rows():
@@ -1283,8 +1272,13 @@
     vocab = table_rows * 32
     seqs = 2 * MB
     shares = blocks.astype(jnp.bfloat16)
-    with jax.named_scope("weights_fourth"):
-        line4 = all_round(shares[3])
+    with jax.named_scope("weights_last"):
+        one, two = hop_one(shares[3]), hop_two(shares[3])
+        last = jnp.stack([shares[3], one, two, hop_two(one)])
+    with jax.named_scope("weights_third"):
+        line3 = all_round(shares[2])
+    with jax.named_scope("weights_pair"):
+        line = lax.all_gather(shares[:2], "z")
     first_pair = vocab_index * MB
     ids = lax.dynamic_slice_in_dim(token_ids, first_pair, MB, 0).reshape(seqs, SLOT)
     lens = lax.dynamic_slice_in_dim(lengths, first_pair, MB, 0).reshape(seqs)
@@ -1309,7 +1303,8 @@
     rank = jnp.sum(
         ((holder[:, None] == holder[None, :]) & earlier & first[None, :]).astype(jnp.int32), axis=1
     )
-    spill = jnp.any(first & (rank >= CAP))
+    most = jnp.where(jnp.arange(total) < TOKENS, CAP_BACK, CAP)
+    spill = jnp.any(first & (rank >= most))
     seat_first = jnp.where(first & (rank < CAP), holder * CAP + rank, -1)
     seat = jnp.sum(jnp.where(same & first[None, :], seat_first[None, :] + 1, 0), axis=1) - 1
     seats = jnp.arange(32 * CAP)
@@ -1324,32 +1319,23 @@
         axis=1,
     )
     message = lax.all_to_all(message, SHARD_AXES, 0, 0, tiled=True)
-    line4, shares, message = together(line4, shares, message)
+    line3, last, message = together(line3, last, message)
     any_spill = jnp.max(message[:, MSG - 1]) > 0
     asked_rows = message[:, :CAP].reshape(32 * CAP)
     table_low = tables.astype(jnp.bfloat16).reshape(2 * table_rows, D)
     give = (asked_rows[:, None] == jnp.arange(2 * table_rows)[None, :]).astype(jnp.bfloat16)
     given = low(dot_nn(give, table_low))
-    with jax.named_scope("weights_fourth"):
-        one4, two4 = hop_one(line4), hop_two(line4)
-    with jax.named_scope("weights_third"):
-        line3 = all_round(shares[2])
-    with jax.named_scope("weights_pair"):
-        line = lax.all_gather(shares[:2], "z")
-    line4, one4, two4, line3, given = together(line4, one4, two4, line3, given)
-    got = lax.all_to_all(given, SHARD_AXES, 0, 0, tiled=True)
     with jax.named_scope("weights_third"):
         one3, two3 = hop_one(line3), hop_two(line3)
-    with jax.named_scope("weights_fourth"):
-        both4 = hop_two(one4)
-    fourth = [line4, one4, two4, both4]
-    line3, one3, two3, both4, line = together(line3, one3, two3, both4, line)
+    one3, two3, given, line, last = together(one3, two3, given, line, last)
+    got = lax.all_to_all(given, SHARD_AXES, 0, 0, tiled=True)
+    with jax.named_scope("weights_last"):
+        last = lax.all_gather(last, "z")
+    with jax.named_scope("weights_third"):
+        third = [line3, one3, two3, hop_two(one3)]
     with jax.named_scope("weights_pair"):
         one, two = hop_one(line), hop_two(line)
-    with jax.named_scope("weights_third"):
-        both3 = hop_two(one3)
-    third = [line3, one3, two3, both3]
-    line, one, two, both3, got = together(line, one, two, both3, got)
+    one, two, third[3] = together(one, two, third[3])
     with jax.named_scope("weights_pair"):
         pair = [line, one, two, hop_two(one)]
     place = (seat[:, None] == seats[None, :]).astype(jnp.bfloat16)
@@ -1367,11 +1353,10 @@
         )
 
     turns = turning(phase_pick, 1) + turning(phase, seqs)
-    pair[1] = after(pair[1], x, truth, *turns)
+    last = after(last, x, truth, *turns)
     parts = []
-    for part in fourth + third + pair:
+    for part in pair + third + [last]:
         parts.extend([part, hop_core(part)])
-    parts = parts[16:] + parts[8:16] + parts[:8]
     left, *saved = forward_call(owner, coord, lens, x, gains, turns, parts)
     plane, _ = spread(saved[-1])
     plane = plane.reshape(-1, D)
@@ -1401,7 +1386,7 @@
     )
     x_at, y_at = block_rows()
     chosen = (inverse[:, None] == jnp.arange(NBLK)[None, :]).astype(jnp.int32)
-    grads = weight_grad_call(
+    grad_args = (
         inverse,
         jnp.sum(chosen * x_at[None, :], axis=1),
         jnp.sum(chosen * y_at[None, :], axis=1),
@@ -1410,37 +1395,36 @@
         act,
         hop_core(act),
     )
+
     def plus(*values):
         return low(sum(high(value) for value in values))
 
+    grads = weight_grad_call(*grad_args)
+    info, gain_part, loss_part, dx, *grads = together(info, gain_part, loss_part, dx, *grads)
     own, one, two, both = grads[:4]
-    own3, one3, two3, both3 = grads[4:8]
-    own4, one4, two4, both4 = grads[8:]
-    info, gain_part, loss_part, dx, both, both3 = together(
-        info, gain_part, loss_part, dx, both, both3
-    )
+    own3, one3, two3, both3, ends = grads[4:]
     with jax.named_scope("grads_pair"):
         one = plus(one, hop_two(both))
+    with jax.named_scope("grads_last"):
+        last = lax.psum_scatter(
+            ends.reshape(16, 192, BC), "z", scatter_dimension=0, tiled=True
+        )
+    back = place[:TOKENS].reshape(TOKENS, 32, CAP)[:, :, :CAP_BACK].reshape(TOKENS, 32 * CAP_BACK)
+    sent = low(dot_tn(back, dx))
+    one, two, both3, sent, info, gain_part, loss_part = together(
+        one, two, both3, sent, info, gain_part, loss_part
+    )
+    told = info[:, :3].reshape(-1)
+    known = told.shape[0]
+    told = jnp.concatenate([told, gain_part.reshape(-1), loss_part[0]])
+    told = jnp.broadcast_to(told[None], (32, told.shape[0]))
+    heard = lax.all_to_all(told, AXES, 0, 0, tiled=True)
+    with jax.named_scope("grads_pair"):
+        line = plus(own, hop_one(one), hop_two(two)).reshape(8, 192, BC)
     with jax.named_scope("grads_third"):
         one3 = plus(one3, hop_two(both3))
-    sent = low(dot_tn(place[:TOKENS], dx))
-    one, two, one3, two3, both4, sent = together(one, two, one3, two3, both4, sent)
-    with jax.named_scope("grads_pair"):
-        line = plus(own, hop_one(one), hop_two(two)).reshape(8, 192, BC)
-    told = jnp.concatenate(
-        [
-            info[:, :3].reshape(-1),
-            gain_part.reshape(-1),
-            loss_part[0, :1],
-            jnp.zeros((63,), jnp.float32),
-        ]
-    )
-    heard = lax.all_to_all(
-        jnp.broadcast_to(told[None], (32, told.shape[0])), AXES, 0, 0, tiled=True
-    )
-    summed = jnp.sum(heard[:, 3 * PAIR_ROWS :], axis=0)
-    gain_grad = summed[: 3 * D].reshape(3, D)
-    loss_sum = summed[3 * D]
+    back_rows = lax.all_to_all(sent, SHARD_AXES, 0, 0, tiled=True)
+    summed = jnp.sum(heard[:, known:], axis=0)
     sources = []
     for other_core in range(2):
         for rel in range(4):
@@ -1452,7 +1436,7 @@
     infos = jnp.sum(
         jnp.where(
             (sources[:, None] == jnp.arange(32)[None, :])[:, :, None],
-            heard[None, :, : 3 * PAIR_ROWS],
+            heard[None, :, :known],
             0.0,
         ),
         axis=1,
@@ -1461,53 +1445,47 @@
         [infos[:, :2], infos[:, 2:3] - (shard * table_rows).astype(jnp.float32)], axis=1
     )
     infos = jnp.pad(infos, ((0, 0), (0, 125)))
-    line, one3, two3, both4, infos = together(line, one3, two3, both4, infos)
     grad_head = head_grad_call(
         (plane, other), (kept_own, kept_other), (stat_own, stat_other), infos
     )
+    adam = adam_call(1, 0.02, grad_head, tables, table_moment, table_second, ())
+    line, one3, two3, last, *adam = together(line, one3, two3, last, *adam)
     with jax.named_scope("grads_pair"):
         pair = lax.psum_scatter(line, "z", scatter_dimension=0, tiled=True)
     with jax.named_scope("grads_third"):
         one3, two3 = hop_one(one3), hop_two(two3)
         line3 = [plus(own3[n], one3[n], two3[n]) for n in range(4)]
-    with jax.named_scope("grads_fourth"):
-        one4 = plus(one4, hop_two(both4))
-    *line3, one4, two4, grad_head = together(*line3, one4, two4, grad_head)
-    with jax.named_scope("grads_third"):
-        third = plus(line3[0], *[ring(line3[step], -step) for step in range(1, 4)])
-    with jax.named_scope("grads_fourth"):
-        one4, two4 = hop_one(one4), hop_two(two4)
-        line4 = [plus(own4[n], one4[n], two4[n]) for n in range(4)]
-    back_rows = lax.all_to_all(sent, SHARD_AXES, 0, 0, tiled=True)
-    take_back = (asked_rows[None, :] == jnp.arange(table_rows)[:, None]).astype(jnp.bfloat16)
-
+    with jax.named_scope("grads_last"):
+        one, two = plus(last[1], hop_two(last[3])), hop_two(last[2])
+    back_at = message[:, :CAP_BACK].reshape(32 * CAP_BACK)
+    take_back = (back_at[None, :] == jnp.arange(table_rows)[:, None]).astype(jnp.bfloat16)
     grad_embed = dot_nn(take_back, back_rows)
     new_tables, new_table_moment, new_table_second = adam_call(
-        grad_embed, grad_head, tables, table_moment, table_second
-    )
-    third, new_tables, *line4 = together(third, new_tables, *line4)
-    with jax.named_scope("grads_fourth"):
-        fourth = plus(line4[0], *[ring(line4[step], -step) for step in range(1, 4)])
-    def finish(start, near, so_far):
-        by_y = hop_y(near)
-        return shampoo_call(
-            start,
-            coord,
-            (near, by_y, hop_core(near), hop_core(by_y)),
-            left_stat,
-            right_stat,
-            left_root,
-            right_root,
-            blocks,
-            so_far,
-        )
-
-    results = finish(0, pair, ())
-    new_blocks, block_grads, new_left, new_right = finish(
-        2, after(jnp.stack([third, fourth]), results[0]), results
+        0, 0.3, grad_embed, tables, table_moment, table_second, adam
     )
     new_gains, new_gain_moment, new_gain_second = adam_step(
-        gains, gain_grad, gain_moment, gain_second, GAIN_RATE
+        gains, summed[: 3 * D].reshape(3, D), gain_moment, gain_second, GAIN_RATE
+    )
+    loss_sum = summed[3 * D]
+    one, two, new_tables, new_gains, new_gain_moment, new_gain_second, *line3 = together(
+        one, two, new_tables, new_gains, new_gain_moment, new_gain_second, *line3
+    )
+    pair_y = hop_y(pair)
+    with jax.named_scope("grads_third"):
+        around = [ring(line3[step], -step) for step in range(1, 4)]
+        third = plus(after(line3[0], pair_y), *around)
+    with jax.named_scope("grads_last"):
+        last = plus(last[0], hop_one(one), two)
+
+    rights = (left_stat, right_stat, left_root, right_root, blocks)
+    late = jnp.stack([third, last])
+    late_y = hop_y(late)
+    results = shampoo_call(
+        0, coord, (pair, pair_y, hop_core(pair), hop_core(pair_y)), *rights, ()
+    )
+    late_y, *results = together(late_y, *results)
+    new_blocks, block_grads, new_left, new_right = shampoo_call(
+        2, coord, (late, late_y, hop_core(late), hop_core(late_y)), *rights, results
     )
     quick = (
         new_blocks,
@@ -1540,6 +1518,7 @@
         gain_moment,
         gain_second,
     )
+
     def slow(state):
         outs = list(per_device(("z", "x"), ("y", "core"), *whole))
         outs[1] = with_layout_constraint(outs[1], Layout((0, 1, 2)))

time: 492 us -> 452 us (0.919)
  waiting for transfers between devices: 199 us -> 167 us
  starting transfers between devices: 72.1 us -> 64.6 us
    ppermute x8, waiting for transfers between devices: 49.7 us -> 20.3 us  [hop_one(): lax.ppermute(value, AXES, moves(lambda z, x, y, c: (z, 1 - x, y, c) if c...]
    ppermute x16, waiting for transfers between devices: 99.5 us -> 71.3 us  [hop_two(): lax.ppermute(value, AXES, moves(lambda z, x, y, c: (z, x, 1 - y, c) if c...]
    ppermute x18 -> x12, waiting for transfers between devices: 33.3 us -> 21.1 us  [ring(): lax.ppermute(value, AXES, moves(lambda z, x, y, c: ((z + step) % 4, x, y,...]
    ppermute x18 -> x12, starting transfers between devices: 29.3 us -> 18.2 us  [ring(): lax.ppermute(value, AXES, moves(lambda z, x, y, c: ((z + step) % 4, x, y,...]
    all_to_all x1, waiting for transfers between devices: 0.01 us -> 10.3 us  [per_core(): heard = lax.all_to_all(told, AXES, 0, 0, tiled=True)]
    ppermute x20 -> x17, waiting for transfers between devices: 7.39 us -> 17.4 us  [hop_core(): return lax.ppermute(value, AXES, moves(lambda z, x, y, c: (z, x, y, 1 - c)))]
    all_to_all x1, waiting for transfers between devices: 0.01 us -> 8.67 us  [per_core(): got = lax.all_to_all(given, SHARD_AXES, 0, 0, tiled=True)]
    all_gather x0 -> x1, waiting for transfers between devices: none -> 8.04 us  [per_core(): last = lax.all_gather(last, 'z')]
  transfers between devices with their start and end apart: 70 -> 63, of which waited for: 29 -> 24; matrix products, arithmetic and copies ran while one was open for 12% -> 12% of each run, Pallas kernels for 10% -> 13%
where the time goes in v3:
time: 452 us; the launch traced here: 446 us
  waiting for transfers between devices  167 us (37%)
  Pallas kernels  125 us (28%)
  starting transfers between devices  64.6 us (14%)
  other arithmetic  34.4 us (8%)
  local copies, waits for them, and re-layouts  26.5 us (6%)
  between operations  16.6 us (4%)
  matrix products  10.2 us (2%)
    ppermute x16, waiting for transfers between devices, hop_two(): lax.ppermute(value, AXES, moves(lambda z, x, y, c: (z, x, 1 - y, c) if c...  71.3 us
    ppermute x12, waiting for transfers between devices, ring(): lax.ppermute(value, AXES, moves(lambda z, x, y, c: ((z + step) % 4, x, y,...  21.1 us
    pallas_call x2, Pallas kernels, adam_call(): pl.pallas_call(functools.partial(adam_kernel, rate), grid=(rows // block,...  20.7 us
    pallas_call x1, Pallas kernels, backward_call(): pl.pallas_call(backward_kernel, out_shape=(jax.ShapeDtypeStruct((RIGHT_RO...  20.4 us
    ppermute x8, waiting for transfers between devices, hop_one(): lax.ppermute(value, AXES, moves(lambda z, x, y, c: (z, 1 - x, y, c) if c...  20.3 us
    ppermute x12, starting transfers between devices, ring(): lax.ppermute(value, AXES, moves(lambda z, x, y, c: ((z + step) % 4, x, y,...  18.2 us
    ppermute x17, waiting for transfers between devices, hop_core(): return lax.ppermute(value, AXES, moves(lambda z, x, y, c: (z, x, y, 1 - c)))  17.4 us
    pallas_call x2, Pallas kernels, head_call(): pl.pallas_call(functools.partial(head_kernel, real), grid=(number // 256,...  16.9 us
  transfers between devices with their start and end apart: 63, of which 24 were waited for; matrix products, arithmetic and copies ran while one was open for 12% of the time, Pallas kernels for 13%

profile of v3, /device:TPU:0, one launch (start us, length us, event | category | flops | bytes accessed | tf_op | source)
XLA Modules:
  0.0 446.0 jit_solution(16412656294066625423)
XLA Ops:
  39.5 3.9 fusion.190
  43.4 8.9 %collective-permute-done.6.rest_10_.rest_24_ = bf16[4,192,384]{2,1,0:T(8,128)(2,1)} collective-permute-done((bf16[4,192,384]{2,1,0:T(8,128)(2,1)}, bf16[4,192,384]{2,1,0:T(8,128)(2,1)}, u32[]{:S(2)}, u32[]{:S(2)}) %collective-permute-start.6) | collective-permute-done | bytes 589856 | tf_op jit(solution)/shard_map/weights_third/ppermute | solution.py:511
  52.3 6.0 %all-to-all-start.1 = ((bf16[32,24,768]{2,1,0:T(8,128)(2,1)}), bf16[32,24,768]{2,1,0:T(8,128)(2,1)}, u32[]{:S(2)}, u32[]{:S(2)}) async-start(bf16[32,24,768]{2,1,0:T(8,128)(2,1)} %bitcast.597), calls=%async_computation.6 | async-start | bytes 2359296 | tf_op jit(solution)/shard_map/all_to_all | solution.py:1331
  64.2 40.8 %collective-permute-done.11.rest_14_.rest_28_ = bf16[4,192,384]{2,1,0:T(8,128)(2,1)S(1)} collective-permute-done((bf16[4,192,384]{2,1,0:T(8,128)(2,1)}, bf16[4,192,384]{2,1,0:T(8,128)(2,1)S(1)}, u32[]{:S(2)}, u32[]{:S(2)}) %collective-permute-start.11) | collective-permute-done | bytes 589856 | tf_op jit(solution)/shard_map/weights_third/ppermute | solution.py:519
  105.4 8.7 %all-to-all-done.1 = bf16[32,24,768]{2,1,0:T(8,128)(2,1)} async-done(((bf16[32,24,768]{2,1,0:T(8,128)(2,1)}), bf16[32,24,768]{2,1,0:T(8,128)(2,1)}, u32[]{:S(2)}, u32[]{:S(2)}) %all-to-all-start.1) | async-done | bytes 1179680 | tf_op jit(solution)/shard_map/all_to_all | solution.py:1331
  117.5 8.0 %all-gather.24.cloned.1.call-done = bf16[16,192,384]{2,1,0:T(8,128)(2,1)} async-done(((bf16[4,192,384]{2,1,0:T(8,128)(2,1)}), bf16[16,192,384]{2,1,0:T(8,128)(2,1)}) %all-gather.24.cloned.1.call-update) | async-done | bytes 2359312 | tf_op jit(solution)/shard_map/weights_last/all_gather | solution.py:1333
  128.2 6.7 %collective-permute-done.17.rest_11_.rest_25_ = bf16[4,192,384]{2,1,0:T(8,128)(2,1)S(1)} collective-permute-done((bf16[4,192,384]{2,1,0:T(8,128)(2,1)}, bf16[4,192,384]{2,1,0:T(8,128)(2,1)S(1)}, u32[]{:S(2)}, u32[]{:S(2)}) %collective-permute-start.17) | collective-permute-done | bytes 589856 | tf_op jit(solution)/shard_map/ppermute | solution.py:527
  137.5 5.7 %collective-permute-done.19.rest_15_.rest_29_ = bf16[4,192,384]{2,1,0:T(8,128)(2,1)} collective-permute-done((bf16[4,192,384]{2,1,0:T(8,128)(2,1)}, bf16[4,192,384]{2,1,0:T(8,128)(2,1)}, u32[]{:S(2)}, u32[]{:S(2)}) %collective-permute-start.19) | collective-permute-done | bytes 589856 | tf_op jit(solution)/shard_map/ppermute | solution.py:527
  145.6 15.1 %layer_forward.1 = (bf16[704,768]{1,0:T(8,128)(2,1)}, bf16[64,768]{1,0:T(8,128)(2,1)}, bf16[256,768]{1,0:T(8,128)(2,1)}, bf16[256,768]{1,0:T(8,128)(2,1)}, f32[6...) custom-call(s32[32]{0:T(128)} %owner.3, ...), custom_call_target="tpu_custom_call" | custom-call | tf_op jit(solution)/shard_map/layer_forward/pallas_call | solution.py:735
  165.1 3.4 collective-permute-done.21
  168.5 3.3 collective-permute-done.22
  175.8 9.1 %collective-permute-done.24 = bf16[4,64,768]{2,1,0:T(8,128)(2,1)S(1)} collective-permute-done((bf16[4,64,768]{2,1,0:T(8,128)(2,1)S(1)}, bf16[4,64,768]{2,1,0:T(8,128)(2,1)S(1)}, u32[]{:S(2)}, u32[]{:S(2)}) %collective-permute-start.24) | collective-permute-done | bytes 393248 | tf_op jit(solution)/shard_map/ppermute | solution.py:511
  185.0 7.7 %collective-permute-done.26 = bf16[4,64,768]{2,1,0:T(8,128)(2,1)S(1)} collective-permute-done((bf16[4,64,768]{2,1,0:T(8,128)(2,1)S(1)}, bf16[4,64,768]{2,1,0:T(8,128)(2,1)S(1)}, u32[]{:S(2)}, u32[]{:S(2)}) %collective-permute-start.26) | collective-permute-done | bytes 393248 | tf_op jit(solution)/shard_map/ppermute | solution.py:519
  197.6 8.5 %head_forward.3 = (bf16[1024,896]{1,0:T(8,128)(2,1)}, bf16[1024,1024]{1,0:T(8,128)(2,1)}, f32[1024,128]{1,0:T(8,128)}) custom-call(bf16[1024,768]{1,0:T(8,128)(2,1)} %copy-done.106, bf16[1024,768]{1,0:T(8,128)(2,1)} %pad.15.head), custom_call_target="tpu_custom_call" | custom-call | flops 3221225472 | bytes 2097152 | tf_op jit(solution)/shard_map/head_forward/pallas_call | solution.py:834
  206.6 8.5 %head_forward.2 = (bf16[1024,896]{1,0:T(8,128)(2,1)}, bf16[1024,1024]{1,0:T(8,128)(2,1)}, f32[1024,128]{1,0:T(8,128)}) custom-call(bf16[1024,768]{1,0:T(8,128)(2,1)} %bitcast.582, bf16[1024,768]{1,0:T(8,128)(2,1)} %pad.15.head), custom_call_target="tpu_custom_call" | custom-call | flops 3221225472 | bytes 2097152 | tf_op jit(solution)/shard_map/head_forward/pallas_call | solution.py:834
  223.3 4.2 collective-permute-done.29.refs_2_
  249.6 6.3 %collective-permute-done.34.rest_12_ = bf16[64,896]{1,0:T(8,128)(2,1)S(1)} collective-permute-done((bf16[64,896]{1,0:T(8,128)(2,1)}, bf16[64,896]{1,0:T(8,128)(2,1)S(1)}, u32[]{:S(2)}, u32[]{:S(2)}) %collective-permute-start.34) | collective-permute-done | bytes 114720 | tf_op jit(solution)/shard_map/ppermute | solution.py:535
  256.6 20.4 %layer_backward.1 = (bf16[1216,768]{1,0:T(8,128)(2,1)}, bf16[256,768]{1,0:T(8,128)(2,1)}, f32[3,768]{1,0:T(4,128)}, f32[64,128]{1,0:T(8,128)}, f32[1,128]{1,0:T(1,128)}) custom-call(s32[32]{0:T(128)S(1)} %copy-done.179, s32[4]{0:T(128)} %pad_add_fusion.coord, s32[4]{0:T(128)} %copy-done.181, f32[4]{0:T(128)} %reshape.1139.refs, bf16[256,768]{1,0:T(8,128)(2,1)} %slice.540.x, ...), custom_call_target="tpu_custom_call" | custom-call | tf_op jit(solution)/shard_map/layer_backward/pallas_call | solution.py:1008
  277.9 3.2 collective-permute-done.36.theirs
  282.4 11.7 %weight_grads.1 = (bf16[4,2,192,384]{3,2,1,0:T(8,128)(2,1)}, bf16[4,2,192,384]{3,2,1,0:T(8,128)(2,1)}, bf16[4,2,192,384]{3,2,1,0:T(8,128)(2,1)}, bf16[4,2,192,38...) custom-call(s32[32]{0:T(128)} %copy-done.182, ...), custom_call_target="tpu_custom_call" | custom-call | tf_op jit(solution)/shard_map/weight_grads/pallas_call | solution.py:1131
  296.2 14.4 %collective-permute-done.37 = bf16[4,2,192,384]{3,2,1,0:T(8,128)(2,1)S(1)} collective-permute-done((bf16[4,2,192,384]{3,2,1,0:T(8,128)(2,1)}, bf16[4,2,192,384]{3,2,1,0:T(8,128)(2,1)S(1)}, u32[]{:S(2)}, u32[]{:S(2)}) %collective-permute-start.37) | collective-permute-done | bytes 1179680 | tf_op jit(solution)/shard_map/grads_pair/ppermute | solution.py:519
  313.4 3.4 all-to-all-start.2
  321.6 4.3 collective-permute-done.40
  327.9 10.3 %all-to-all-done.2 = f32[32,1,2624]{2,1,0:T(1,128)S(1)} async-done(((f32[32,1,2624]{2,1,0:T(1,128)}), f32[32,1,2624]{2,1,0:T(1,128)S(1)}, u32[]{:S(2)}, u32[]{:S(2)}) %all-to-all-start.2) | async-done | bytes 335904 | tf_op jit(solution)/shard_map/all_to_all | solution.py:1421
  344.0 11.6 %head_grad.1.grad = f32[1024,768]{1,0:T(8,128)} custom-call(bf16[1024,768]{1,0:T(8,128)(2,1)} %bitcast.583, bf16[1024,768]{1,0:T(8,128)(2,1)} %copy-done.106, bf16[1024,1024]{1,0:T(8,128)(2,1)} %get-tuple-element.406.kept_a, bf16[1024,1024]{1,0:T(8,128)(2,1)} %get-tuple-element.407.kept_b, f32[1024,128]{1,0:T(8,128)} %get-tuple-element.408.stat_a, ...), custom_call_target="tpu_custom_call" | custom-call | flops 3221225472 | bytes 4194304 | tf_op jit(solution)/shard_map/head_grad/pallas_call | solution.py:893
  355.6 10.4 %adam.2 = (f32[2,1000,768]{2,1,0:T(8,128)}, f32[2,1000,768]{2,1,0:T(8,128)}, f32[2,1000,768]{2,1,0:T(8,128)}) custom-call(f32[1024,768]{1,0:T(8,128)} %head_grad.1.grad, f32[2,1000,768]{2,1,0:T(8,128)} %w.3, f32[2,1000,768]{2,1,0:T(8,128)} %m.3, f32[2,1000,768]{2,1,0:T(8,128)} %v.3), custom_call_target="tpu_custom_call" | custom-call | flops 7680000 | bytes 21504000 | tf_op jit(solution)/shard_map/adam/pallas_call | solution.py:1213
  366.1 3.1 add_convert_fusion.10
  379.8 10.3 %adam.3 = (f32[2,1000,768]{2,1,0:T(8,128)}, f32[2,1000,768]{2,1,0:T(8,128)}, f32[2,1000,768]{2,1,0:T(8,128)}) custom-call(f32[1000,768]{1,0:T(8,128)} %fusion.189.grad, f32[2,1000,768]{2,1,0:T(8,128)} %w.3, f32[2,1000,768]{2,1,0:T(8,128)} %m.3, f32[2,1000,768]{2,1,0:T(8,128)} %v.3, ...), custom_call_target="tpu_custom_call", output_to_operand_aliasing={{0}: (4, {}), {1}: (5, {}), {2}: (6, {})} | custom-call | flops 7680000 | bytes 21504000 | tf_op jit(solution)/shard_map/adam/pallas_call | solution.py:1213
  396.0 3.8 reduce-scatter.11.cloned.1.call-done.refs_0_
  408.6 7.1 %collective-permute-done.47 = bf16[192,384]{1,0:T(8,128)(2,1)S(1)} collective-permute-done((bf16[192,384]{1,0:T(8,128)(2,1)}, bf16[192,384]{1,0:T(8,128)(2,1)S(1)}, u32[]{:S(2)}, u32[]{:S(2)}) %collective-permute-start.47) | collective-permute-done | bytes 147488 | tf_op jit(solution)/shard_map/grads_third/ppermute | solution.py:535
  418.0 7.4 %shampoo.2 = (f32[4,192,384]{2,1,0:T(8,128)}, f32[4,192,384]{2,1,0:T(8,128)}, f32[4,768,768]{2,1,0:T(8,128)}, f32[4,384,384]{2,1,0:T(8,128)}) custom-call(s32[4]{0:T(128)} %pad_add_fusion.coord, bf16[2,192,384]{2,1,0:T(8,128)(2,1)} %reduce-scatter.11.cloned.1.call-done.refs_0_, bf16[2,192,384]{2,1,0:T(8,128)(2,1)} %copy-done.126, ...), custom_call_target="tpu_custom_call" | custom-call | flops 1811939328 | bytes 16777216 | tf_op jit(solution)/shard_map/shampoo/pallas_call | solution.py:1178
  430.2 7.6 %shampoo.3 = (f32[4,192,384]{2,1,0:T(8,128)}, f32[4,192,384]{2,1,0:T(8,128)}, f32[4,768,768]{2,1,0:T(8,128)}, f32[4,384,384]{2,1,0:T(8,128)}) custom-call(s32[4]{0:T(128)} %pad_add_fusion.coord, bf16[2,192,384]{2,1,0:T(8,128)(2,1)} %pad_maximum_fusion.27.refs_0_, ...), custom_call_target="tpu_custom_call", output_to_operand_aliasing={{0}: (10, {}), {1}: (11, {}), {2}: (12, {}), {3}: (13, {})} | custom-call | flops 1811939328 | bytes 16777216 | tf_op jit(solution)/shard_map/shampoo/pallas_call | solution.py:1178
  (312 shorter events, 146.0 us)
Async XLA Ops:
  7.2 45.1 %all-gather.22.cloned.1.call-start = ((), (), s32[]{:S(2)}) async-start(), calls=%async_computation.13 | async-start | bytes 1474560 | tf_op jit(solution)/shard_map/weights_pair/all_gather | solution.py:1281
  9.4 22.5 %collective-permute-start = (bf16[192,384]{1,0:T(8,128)(2,1)}, bf16[192,384]{1,0:T(8,128)(2,1)}, u32[]{:S(2)}, u32[]{:S(2)}) collective-permute-start(bf16[192,384]{1,0:T(8,128)(2,1)} %get-tuple-element.980), channel_id=1, source_target_pairs={{0,8},{1,9},{2,10},{3,11},{4,12},{5,13},{6,14},{7,15},{8,16},{9,17... | collective-permute-start | bytes 442376 | tf_op jit(solution)/shard_map/weights_third/ppermute | solution.py:535
  12.4 19.5 %collective-permute-start.1 = (bf16[192,384]{1,0:T(8,128)(2,1)}, bf16[192,384]{1,0:T(8,128)(2,1)}, u32[]{:S(2)}, u32[]{:S(2)}) collective-permute-start(bf16[192,384]{1,0:T(8,128)(2,1)} %get-tuple-element.980), channel_id=1, source_target_pairs={{0,16},{1,17},{2,18},{3,19},{4,20},{5,21},{6,22},{7,23},{8,24},{9,... | collective-permute-start | bytes 442376 | tf_op jit(solution)/shard_map/weights_third/ppermute | solution.py:535
  15.0 16.9 %collective-permute-start.2 = (bf16[192,384]{1,0:T(8,128)(2,1)}, bf16[192,384]{1,0:T(8,128)(2,1)}, u32[]{:S(2)}, u32[]{:S(2)}) collective-permute-start(bf16[192,384]{1,0:T(8,128)(2,1)} %get-tuple-element.980), channel_id=1, source_target_pairs={{0,24},{1,25},{2,26},{3,27},{4,28},{5,29},{6,30},{7,31},{8,0},{9,1... | collective-permute-start | bytes 442376 | tf_op jit(solution)/shard_map/weights_third/ppermute | solution.py:535
  17.8 16.6 %collective-permute-start.4 = (bf16[192,384]{1,0:T(8,128)(2,1)}, bf16[192,384]{1,0:T(8,128)(2,1)}, u32[]{:S(2)}, u32[]{:S(2)}) collective-permute-start(bf16[192,384]{1,0:T(8,128)(2,1)} %get-tuple-element.981), channel_id=1, source_target_pairs={{0,2},{1,5},{2,0},{3,7},{4,6},{5,1},{6,4},{7,3},{8,10},{9,13},{10,... | collective-permute-start | bytes 442376 | tf_op jit(solution)/shard_map/weights_last/ppermute | solution.py:519
  28.7 96.8 %all-gather.24.cloned.1.call-start = ((), (), s32[]{:S(2)}) async-start(), calls=%async_computation.14 | async-start | bytes 2949120 | tf_op jit(solution)/shard_map/weights_last/all_gather | solution.py:1333
  36.3 16.0 %collective-permute-start.6 = (bf16[4,192,384]{2,1,0:T(8,128)(2,1)}, bf16[4,192,384]{2,1,0:T(8,128)(2,1)}, u32[]{:S(2)}, u32[]{:S(2)}) collective-permute-start(bf16[4,192,384]{2,1,0:T(8,128)(2,1)} %pad_maximum_fusion.24.rest_8_.rest_22_), channel_id=1, source_target_pairs={{0,4},{1,3},{2,6},{3,1},{4,0},{5,7},{6,2},{7,5},{8,12},{9,11},{10,... | collective-permute-start | bytes 1769480 | tf_op jit(solution)/shard_map/weights_third/ppermute | solution.py:511
  37.9 14.3 %collective-permute-start.7 = (bf16[4,192,384]{2,1,0:T(8,128)(2,1)}, bf16[4,192,384]{2,1,0:T(8,128)(2,1)}, u32[]{:S(2)}, u32[]{:S(2)}) collective-permute-start(bf16[4,192,384]{2,1,0:T(8,128)(2,1)} %pad_maximum_fusion.24.rest_8_.rest_22_), channel_id=1, source_target_pairs={{0,2},{1,5},{2,0},{3,7},{4,6},{5,1},{6,4},{7,3},{8,10},{9,13},{10,... | collective-permute-start | bytes 1769480 | tf_op jit(solution)/shard_map/weights_third/ppermute | solution.py:519
  52.3 61.8 %all-to-all-start.1 = ((bf16[32,24,768]{2,1,0:T(8,128)(2,1)}), bf16[32,24,768]{2,1,0:T(8,128)(2,1)}, u32[]{:S(2)}, u32[]{:S(2)}) async-start(bf16[32,24,768]{2,1,0:T(8,128)(2,1)} %bitcast.597), calls=%async_computation.6 | async-start | bytes 2359296 | tf_op jit(solution)/shard_map/all_to_all | solution.py:1331
  58.3 310.9 %reduce-scatter.9.cloned.1.call-start = ((), (), s32[]{:S(2)}) async-start(), calls=%async_computation.11 | async-start | bytes 2949120 | tf_op jit(solution)/shard_map/grads_last/reduce_scatter | solution.py:1409
  58.7 46.3 %collective-permute-start.10 = (bf16[4,2,192,384]{3,2,1,0:T(8,128)(2,1)}, bf16[4,2,192,384]{3,2,1,0:T(8,128)(2,1)S(1)}, u32[]{:S(2)}, u32[]{:S(2)}) collective-permute-start(bf16[4,2,192,384]{3,2,1,0:T(8,128)(2,1)} %bitcast.584), channel_id=1, source_target_pairs={{0,2},{1,5},{2,0},{3,7},{4,6},{5,1},{6,4},{7,3},{8,10},{9,13},{10,... | collective-permute-start | bytes 3538952 | tf_op jit(solution)/shard_map/weights_pair/ppermute | solution.py:519
  60.4 44.6 %collective-permute-start.9 = (bf16[4,2,192,384]{3,2,1,0:T(8,128)(2,1)}, bf16[4,2,192,384]{3,2,1,0:T(8,128)(2,1)}, u32[]{:S(2)}, u32[]{:S(2)}) collective-permute-start(bf16[4,2,192,384]{3,2,1,0:T(8,128)(2,1)} %bitcast.585), channel_id=1, source_target_pairs={{0,4},{1,3},{2,6},{3,1},{4,0},{5,7},{6,2},{7,5},{8,12},{9,11},{10,... | collective-permute-start | bytes 3538952 | tf_op jit(solution)/shard_map/weights_pair/ppermute | solution.py:511
  62.0 43.0 %collective-permute-start.11 = (bf16[4,192,384]{2,1,0:T(8,128)(2,1)}, bf16[4,192,384]{2,1,0:T(8,128)(2,1)S(1)}, u32[]{:S(2)}, u32[]{:S(2)}) collective-permute-start(bf16[4,192,384]{2,1,0:T(8,128)(2,1)} %collective-permute-done.6.rest_10_.rest_24_), channel_id=1, source_target_pairs={{0,2},{1,5},{2,0},{3,7},{4,6},{5,1},{6,4},{7,3},{8,10},{9,13},{10,... | collective-permute-start | bytes 1769480 | tf_op jit(solution)/shard_map/weights_third/ppermute | solution.py:519
  64.1 63.3 %collective-permute-start.16 = (bf16[4,192,384]{2,1,0:T(8,128)(2,1)S(1)}, bf16[4,192,384]{2,1,0:T(8,128)(2,1)S(1)}, u32[]{:S(2)}, u32[]{:S(2)}) collective-permute-start(bf16[4,192,384]{2,1,0:T(8,128)(2,1)S(1)} %copy-done.85), channel_id=1, source_target_pairs={{0,1},{1,0},{2,3},{3,2},{4,5},{5,4},{6,7},{7,6},{8,9},{9,8},{10,11... | collective-permute-start | bytes 1769480 | tf_op jit(solution)/shard_map/ppermute | solution.py:527
  105.0 31.3 %collective-permute-start.14 = (bf16[4,2,192,384]{3,2,1,0:T(8,128)(2,1)}, bf16[4,2,192,384]{3,2,1,0:T(8,128)(2,1)}, u32[]{:S(2)}, u32[]{:S(2)}) collective-permute-start(bf16[4,2,192,384]{3,2,1,0:T(8,128)(2,1)} %collective-permute-done.9.rest_2_.rest_16_), channel_id=1, source_target_pairs={{0,2},{1,5},{2,0},{3,7},{4,6},{5,1},{6,4},{7,3},{8,10},{9,13},{10,... | collective-permute-start | bytes 3538952 | tf_op jit(solution)/shard_map/weights_pair/ppermute | solution.py:519
  126.8 16.4 %collective-permute-start.20 = (bf16[4,4,192,384]{3,2,1,0:T(8,128)(2,1)}, bf16[4,4,192,384]{3,2,1,0:T(8,128)(2,1)S(1)}, u32[]{:S(2)}, u32[]{:S(2)}) collective-permute-start(bf16[4,4,192,384]{3,2,1,0:T(8,128)(2,1)} %bitcast.576), channel_id=1, source_target_pairs={{0,1},{1,0},{2,3},{3,2},{4,5},{5,4},{6,7},{7,6},{8,9},{9,8},{10,11... | collective-permute-start | bytes 7077896 | tf_op jit(solution)/shard_map/ppermute | solution.py:527
  206.3 27.1 %collective-permute-start.32 = (bf16[704,768]{1,0:T(8,128)(2,1)}, bf16[704,768]{1,0:T(8,128)(2,1)S(1)}, u32[]{:S(2)}, u32[]{:S(2)}) collective-permute-start(bf16[704,768]{1,0:T(8,128)(2,1)} %get-tuple-element.370.mine), channel_id=1, source_target_pairs={{0,1},{1,0},{2,3},{3,2},{4,5},{5,4},{6,7},{7,6},{8,9},{9,8},{10,11... | collective-permute-start | bytes 3244040 | tf_op jit(solution)/shard_map/ppermute | solution.py:527
  221.4 16.1 %collective-permute-start.31 = (bf16[256,896]{1,0:T(8,128)(2,1)}, bf16[256,896]{1,0:T(8,128)(2,1)S(1)}, u32[]{:S(2)}, u32[]{:S(2)}) collective-permute-start(bf16[256,896]{1,0:T(8,128)(2,1)} %merge_parts.6), channel_id=1, source_target_pairs={{0,2},{1,5},{2,0},{3,7},{4,6},{5,1},{6,4},{7,3},{8,10},{9,13},{10,... | collective-permute-start | bytes 1376264 | tf_op jit(solution)/shard_map/ppermute | solution.py:519
  294.1 16.5 %collective-permute-start.37 = (bf16[4,2,192,384]{3,2,1,0:T(8,128)(2,1)}, bf16[4,2,192,384]{3,2,1,0:T(8,128)(2,1)S(1)}, u32[]{:S(2)}, u32[]{:S(2)}) collective-permute-start(bf16[4,2,192,384]{3,2,1,0:T(8,128)(2,1)} %get-tuple-element.393), channel_id=1, source_target_pairs={{0,2},{1,5},{2,0},{3,7},{4,6},{5,1},{6,4},{7,3},{8,10},{9,13},{10,... | collective-permute-start | bytes 3538952 | tf_op jit(solution)/shard_map/grads_pair/ppermute | solution.py:519
  311.9 14.0 %collective-permute-start.40 = (bf16[4,192,384]{2,1,0:T(8,128)(2,1)}, bf16[4,192,384]{2,1,0:T(8,128)(2,1)S(1)}, u32[]{:S(2)}, u32[]{:S(2)}) collective-permute-start(bf16[4,192,384]{2,1,0:T(8,128)(2,1)} %get-tuple-element.403), channel_id=1, source_target_pairs={{0,2},{1,5},{2,0},{3,7},{4,6},{5,1},{6,4},{7,3},{8,10},{9,13},{10,... | collective-permute-start | bytes 1769480 | tf_op jit(solution)/shard_map/grads_third/ppermute | solution.py:519
  313.4 24.9 %all-to-all-start.2 = ((f32[32,1,2624]{2,1,0:T(1,128)}), f32[32,1,2624]{2,1,0:T(1,128)S(1)}, u32[]{:S(2)}, u32[]{:S(2)}) async-start(f32[32,1,2624]{2,1,0:T(1,128)} %broadcast_in_dim.199), calls=%async_computation.8 | async-start | bytes 688128 | tf_op jit(solution)/shard_map/all_to_all | solution.py:1421
  317.0 49.0 %collective-permute-start.38 = (bf16[4,2,192,384]{3,2,1,0:T(8,128)(2,1)}, bf16[4,2,192,384]{3,2,1,0:T(8,128)(2,1)}, u32[]{:S(2)}, u32[]{:S(2)}) collective-permute-start(bf16[4,2,192,384]{3,2,1,0:T(8,128)(2,1)} %add_convert_fusion.11), channel_id=1, source_target_pairs={{0,4},{1,3},{2,6},{3,1},{4,0},{5,7},{6,2},{7,5},{8,12},{9,11},{10,... | collective-permute-start | bytes 3538952 | tf_op jit(solution)/shard_map/grads_pair/ppermute | solution.py:511
  318.8 47.2 %collective-permute-start.39 = (bf16[4,2,192,384]{3,2,1,0:T(8,128)(2,1)}, bf16[4,2,192,384]{3,2,1,0:T(8,128)(2,1)}, u32[]{:S(2)}, u32[]{:S(2)}) collective-permute-start(bf16[4,2,192,384]{3,2,1,0:T(8,128)(2,1)} %get-tuple-element.401), channel_id=1, source_target_pairs={{0,2},{1,5},{2,0},{3,7},{4,6},{5,1},{6,4},{7,3},{8,10},{9,13},{10,... | collective-permute-start | bytes 3538952 | tf_op jit(solution)/shard_map/grads_pair/ppermute | solution.py:519
  338.2 35.0 %all-to-all-start.3 = ((bf16[32,18,768]{2,1,0:T(8,128)(2,1)}), bf16[32,18,768]{2,1,0:T(8,128)(2,1)S(1)}, u32[]{:S(2)}, u32[]{:S(2)}) async-start(bf16[32,18,768]{2,1,0:T(8,128)(2,1)} %all_to_all.38), calls=%async_computation.9 | async-start | bytes 2359296 | tf_op jit(solution)/shard_map/all_to_all | solution.py:1426
  341.0 58.8 %reduce-scatter.11.cloned.1.call-start = ((), (), s32[]{:S(2)}) async-start(), calls=%async_computation.12 | async-start | bytes 1474560 | tf_op jit(solution)/shard_map/grads_pair/reduce_scatter | solution.py:1454
  373.4 18.5 %collective-permute-start.43 = (bf16[4,192,384]{2,1,0:T(8,128)(2,1)}, bf16[4,192,384]{2,1,0:T(8,128)(2,1)}, u32[]{:S(2)}, u32[]{:S(2)}) collective-permute-start(bf16[4,192,384]{2,1,0:T(8,128)(2,1)} %add_convert_fusion.12), channel_id=1, source_target_pairs={{0,4},{1,3},{2,6},{3,1},{4,0},{5,7},{6,2},{7,5},{8,12},{9,11},{10,... | collective-permute-start | bytes 1769480 | tf_op jit(solution)/shard_map/grads_third/ppermute | solution.py:511
  373.5 18.4 %collective-permute-start.44 = (bf16[4,192,384]{2,1,0:T(8,128)(2,1)}, bf16[4,192,384]{2,1,0:T(8,128)(2,1)}, u32[]{:S(2)}, u32[]{:S(2)}) collective-permute-start(bf16[4,192,384]{2,1,0:T(8,128)(2,1)} %get-tuple-element.424), channel_id=1, source_target_pairs={{0,2},{1,5},{2,0},{3,7},{4,6},{5,1},{6,4},{7,3},{8,10},{9,13},{10,... | collective-permute-start | bytes 1769480 | tf_op jit(solution)/shard_map/grads_third/ppermute | solution.py:519
  374.7 15.5 %collective-permute-start.41 = (bf16[192,384]{1,0:T(8,128)(2,1)S(1)}, bf16[192,384]{1,0:T(8,128)(2,1)S(1)}, u32[]{:S(2)}, u32[]{:S(2)}) collective-permute-start(bf16[192,384]{1,0:T(8,128)(2,1)S(1)} %get-tuple-element.978), channel_id=1, source_target_pairs={{0,2},{1,5},{2,0},{3,7},{4,6},{5,1},{6,4},{7,3},{8,10},{9,13},{10,... | collective-permute-start | bytes 442376 | tf_op jit(solution)/shard_map/grads_last/ppermute | solution.py:519
  378.8 15.7 %collective-permute-start.42 = (bf16[192,384]{1,0:T(8,128)(2,1)S(1)}, bf16[192,384]{1,0:T(8,128)(2,1)}, u32[]{:S(2)}, u32[]{:S(2)}) collective-permute-start(bf16[192,384]{1,0:T(8,128)(2,1)S(1)} %get-tuple-element.977), channel_id=1, source_target_pairs={{0,2},{1,5},{2,0},{3,7},{4,6},{5,1},{6,4},{7,3},{8,10},{9,13},{10,... | collective-permute-start | bytes 442376 | tf_op jit(solution)/shard_map/grads_last/ppermute | solution.py:519
  402.3 13.3 %collective-permute-start.47 = (bf16[192,384]{1,0:T(8,128)(2,1)}, bf16[192,384]{1,0:T(8,128)(2,1)S(1)}, u32[]{:S(2)}, u32[]{:S(2)}) collective-permute-start(bf16[192,384]{1,0:T(8,128)(2,1)} %get-tuple-element.429), channel_id=1, source_target_pairs={{0,16},{1,17},{2,18},{3,19},{4,20},{5,21},{6,22},{7,23},{8,24},{9,... | collective-permute-start | bytes 442376 | tf_op jit(solution)/shard_map/grads_third/ppermute | solution.py:535
  402.4 13.3 %collective-permute-start.48 = (bf16[192,384]{1,0:T(8,128)(2,1)}, bf16[192,384]{1,0:T(8,128)(2,1)S(1)}, u32[]{:S(2)}, u32[]{:S(2)}) collective-permute-start(bf16[192,384]{1,0:T(8,128)(2,1)} %get-tuple-element.430), channel_id=1, source_target_pairs={{0,8},{1,9},{2,10},{3,11},{4,12},{5,13},{6,14},{7,15},{8,16},{9,17... | collective-permute-start | bytes 442376 | tf_op jit(solution)/shard_map/grads_third/ppermute | solution.py:535
  405.7 12.3 %collective-permute-start.51 = (bf16[2,192,384]{2,1,0:T(8,128)(2,1)}, bf16[2,192,384]{2,1,0:T(8,128)(2,1)}, u32[]{:S(2)}, u32[]{:S(2)}) collective-permute-start(bf16[2,192,384]{2,1,0:T(8,128)(2,1)} %reduce-scatter.11.cloned.1.call-done.refs_0_), channel_id=1, source_target_pairs={{0,1},{1,0},{2,3},{3,2},{4,5},{5,4},{6,7},{7,6},{8,9},{9,8},{10,11... | collective-permute-start | bytes 884744 | tf_op jit(solution)/shard_map/ppermute | solution.py:527
  (81 other events, 799.6 us)
Sparse Core Ops, SparseCore 0:
  20.2 27.3 all-gather.21
  52.4 73.0 all-gather.23
  294.2 51.2 reduce-scatter.8
  369.3 30.3 reduce-scatter.10

commit v4 on v3

--- a/solution.py
+++ b/solution.py
@@ -1335,7 +1335,8 @@
         third = [line3, one3, two3, hop_two(one3)]
     with jax.named_scope("weights_pair"):
         one, two = hop_one(line), hop_two(line)
-    one, two, third[3] = together(one, two, third[3])
+    early = [hop_core(part) for part in third[:3] + [line]]
+    one, two, third[3], *early = together(one, two, third[3], *early)
     with jax.named_scope("weights_pair"):
         pair = [line, one, two, hop_two(one)]
     place = (seat[:, None] == seats[None, :]).astype(jnp.bfloat16)
@@ -1353,10 +1354,14 @@
         )
 
     turns = turning(phase_pick, 1) + turning(phase, seqs)
-    last = after(last, x, truth, *turns)
+    middle = [hop_core(part) for part in (one, two, third[3])]
+    last, *middle = together(last, *middle, x, truth, *turns)[:4]
     parts = []
-    for part in pair + third + [last]:
-        parts.extend([part, hop_core(part)])
+    early += middle
+    for n, part in enumerate(pair + third + [last]):
+        place_of_early = {0: 3, 4: 0, 5: 1, 6: 2, 1: 4, 2: 5, 7: 6}.get(n)
+        parts.append(part)
+        parts.append(hop_core(part) if place_of_early is None else early[place_of_early])
     left, *saved = forward_call(owner, coord, lens, x, gains, turns, parts)
     plane, _ = spread(saved[-1])
     plane = plane.reshape(-1, D)
@@ -1411,16 +1416,16 @@
         )
     back = place[:TOKENS].reshape(TOKENS, 32, CAP)[:, :, :CAP_BACK].reshape(TOKENS, 32 * CAP_BACK)
     sent = low(dot_tn(back, dx))
-    one, two, both3, sent, info, gain_part, loss_part = together(
-        one, two, both3, sent, info, gain_part, loss_part
-    )
     told = info[:, :3].reshape(-1)
     known = told.shape[0]
     told = jnp.concatenate([told, gain_part.reshape(-1), loss_part[0]])
     told = jnp.broadcast_to(told[None], (32, told.shape[0]))
     heard = lax.all_to_all(told, AXES, 0, 0, tiled=True)
     with jax.named_scope("grads_pair"):
-        line = plus(own, hop_one(one), hop_two(two)).reshape(8, 192, BC)
+        two = hop_two(two)
+    one, two, both3, sent, heard = together(one, two, both3, sent, heard)
+    with jax.named_scope("grads_pair"):
+        line = plus(own, hop_one(one), two).reshape(8, 192, BC)
     with jax.named_scope("grads_third"):
         one3 = plus(one3, hop_two(both3))
     back_rows = lax.all_to_all(sent, SHARD_AXES, 0, 0, tiled=True)

time: 452 us -> 440 us (0.973)
  waiting for transfers between devices: 167 us -> 152 us
    ppermute x16, waiting for transfers between devices: 71.3 us -> 40.7 us  [hop_two(): lax.ppermute(value, AXES, moves(lambda z, x, y, c: (z, x, 1 - y, c) if c...]
    all_to_all x1, waiting for transfers between devices: 10.3 us -> 25.6 us  [per_core(): heard = lax.all_to_all(told, AXES, 0, 0, tiled=True)]
    ppermute x8, waiting for transfers between devices: 20.3 us -> 32.1 us  [hop_one(): lax.ppermute(value, AXES, moves(lambda z, x, y, c: (z, 1 - x, y, c) if c...]
    ppermute x17, waiting for transfers between devices: 17.4 us -> 11.2 us  [hop_core(): return lax.ppermute(value, AXES, moves(lambda z, x, y, c: (z, x, y, 1 - c)))]
    all_to_all x1, waiting for transfers between devices: 8.67 us -> 3.85 us  [per_core(): got = lax.all_to_all(given, SHARD_AXES, 0, 0, tiled=True)]
    unnamed x104 -> x100, local copies, waits for them, and re-layouts: 12.3 us -> 10.1 us
  transfers between devices with their start and end apart: 63 -> 63, of which waited for: 24 -> 26; matrix products, arithmetic and copies ran while one was open for 12% -> 14% of each run, Pallas kernels for 13% -> 14%
where the time goes in v4:
time: 440 us; the launch traced here: 434 us
  waiting for transfers between devices  152 us (35%)
  Pallas kernels  125 us (28%)
  starting transfers between devices  64.1 us (15%)
  other arithmetic  38.6 us (9%)
  local copies, waits for them, and re-layouts  27.1 us (6%)
  between operations  16.4 us (4%)
  matrix products  9.22 us (2%)
    ppermute x16, waiting for transfers between devices, hop_two(): lax.ppermute(value, AXES, moves(lambda z, x, y, c: (z, x, 1 - y, c) if c...  40.7 us
    ppermute x8, waiting for transfers between devices, hop_one(): lax.ppermute(value, AXES, moves(lambda z, x, y, c: (z, 1 - x, y, c) if c...  32.1 us
    all_to_all x1, waiting for transfers between devices, per_core(): heard = lax.all_to_all(told, AXES, 0, 0, tiled=True)  25.6 us
    pallas_call x2, Pallas kernels, adam_call(): pl.pallas_call(functools.partial(adam_kernel, rate), grid=(rows // block,...  20.8 us
    ppermute x12, waiting for transfers between devices, ring(): lax.ppermute(value, AXES, moves(lambda z, x, y, c: ((z + step) % 4, x, y,...  20.6 us
    pallas_call x1, Pallas kernels, backward_call(): pl.pallas_call(backward_kernel, out_shape=(jax.ShapeDtypeStruct((RIGHT_RO...  20.4 us
    ppermute x12, starting transfers between devices, ring(): lax.ppermute(value, AXES, moves(lambda z, x, y, c: ((z + step) % 4, x, y,...  18.1 us
    pallas_call x2, Pallas kernels, head_call(): pl.pallas_call(functools.partial(head_kernel, real), grid=(number // 256,...  17 us
  transfers between devices with their start and end apart: 63, of which 26 were waited for; matrix products, arithmetic and copies ran while one was open for 14% of the time, Pallas kernels for 14%

profile of v4, /device:TPU:0, one launch (start us, length us, event | category | flops | bytes accessed | tf_op | source)
XLA Modules:
  0.0 434.2 jit_solution(931381767701051823)
XLA Ops:
  40.1 3.9 fusion.190
  44.0 8.9 %collective-permute-done.6.rest_10_.rest_24_ = bf16[4,192,384]{2,1,0:T(8,128)(2,1)} collective-permute-done((bf16[4,192,384]{2,1,0:T(8,128)(2,1)}, bf16[4,192,384]{2,1,0:T(8,128)(2,1)}, u32[]{:S(2)}, u32[]{:S(2)}) %collective-permute-start.6) | collective-permute-done | bytes 589856 | tf_op jit(solution)/shard_map/weights_third/ppermute | solution.py:511
  53.0 5.9 %all-to-all-start.1 = ((bf16[32,24,768]{2,1,0:T(8,128)(2,1)}), bf16[32,24,768]{2,1,0:T(8,128)(2,1)}, u32[]{:S(2)}, u32[]{:S(2)}) async-start(bf16[32,24,768]{2,1,0:T(8,128)(2,1)} %bitcast.597), calls=%async_computation.6 | async-start | bytes 2359296 | tf_op jit(solution)/shard_map/all_to_all | solution.py:1331
  63.2 22.4 %collective-permute-done.10.rest_14_.rest_28_ = bf16[4,192,384]{2,1,0:T(8,128)(2,1)S(1)} collective-permute-done((bf16[4,192,384]{2,1,0:T(8,128)(2,1)}, bf16[4,192,384]{2,1,0:T(8,128)(2,1)S(1)}, u32[]{:S(2)}, u32[]{:S(2)}) %collective-permute-start.10) | collective-permute-done | bytes 589856 | tf_op jit(solution)/shard_map/weights_third/ppermute | solution.py:519
  88.0 11.2 %collective-permute-done.8.rest_2_.rest_16_ = bf16[4,2,192,384]{3,2,1,0:T(8,128)(2,1)} collective-permute-done((bf16[4,2,192,384]{3,2,1,0:T(8,128)(2,1)}, bf16[4,2,192,384]{3,2,1,0:T(8,128)(2,1)}, u32[]{:S(2)}, u32[]{:S(2)}) %collective-permute-start.8) | collective-permute-done | bytes 1179680 | tf_op jit(solution)/shard_map/weights_pair/ppermute | solution.py:511
  99.3 6.2 %collective-permute-done.9.rest_4_.rest_18_ = bf16[4,2,192,384]{3,2,1,0:T(8,128)(2,1)S(1)} collective-permute-done((bf16[4,2,192,384]{3,2,1,0:T(8,128)(2,1)}, bf16[4,2,192,384]{3,2,1,0:T(8,128)(2,1)S(1)}, u32[]{:S(2)}, u32[]{:S(2)}) %collective-permute-start.9) | collective-permute-done | bytes 1179680 | tf_op jit(solution)/shard_map/weights_pair/ppermute | solution.py:519
  110.8 3.8 all-to-all-done.1
  118.0 8.0 %all-gather.24.cloned.1.call-done = bf16[16,192,384]{2,1,0:T(8,128)(2,1)} async-done(((bf16[4,192,384]{2,1,0:T(8,128)(2,1)}), bf16[16,192,384]{2,1,0:T(8,128)(2,1)}) %all-gather.24.cloned.1.call-update) | async-done | bytes 2359312 | tf_op jit(solution)/shard_map/weights_last/all_gather | solution.py:1333
  130.0 5.1 %collective-permute-done.19.rest_7_.rest_21_ = bf16[4,2,192,384]{3,2,1,0:T(8,128)(2,1)} collective-permute-done((bf16[4,2,192,384]{3,2,1,0:T(8,128)(2,1)}, bf16[4,2,192,384]{3,2,1,0:T(8,128)(2,1)}, u32[]{:S(2)}, u32[]{:S(2)}) %collective-permute-start.19) | collective-permute-done | bytes 1179680 | tf_op jit(solution)/shard_map/ppermute | solution.py:527
  136.7 15.0 %layer_forward.1 = (bf16[704,768]{1,0:T(8,128)(2,1)}, bf16[64,768]{1,0:T(8,128)(2,1)}, bf16[256,768]{1,0:T(8,128)(2,1)}, bf16[256,768]{1,0:T(8,128)(2,1)}, f32[6...) custom-call(s32[32]{0:T(128)} %owner.3, ...), custom_call_target="tpu_custom_call" | custom-call | tf_op jit(solution)/shard_map/layer_forward/pallas_call | solution.py:735
  156.2 3.4 collective-permute-done.21
  159.6 3.3 collective-permute-done.22
  166.9 9.1 %collective-permute-done.24 = bf16[4,64,768]{2,1,0:T(8,128)(2,1)S(1)} collective-permute-done((bf16[4,64,768]{2,1,0:T(8,128)(2,1)S(1)}, bf16[4,64,768]{2,1,0:T(8,128)(2,1)S(1)}, u32[]{:S(2)}, u32[]{:S(2)}) %collective-permute-start.24) | collective-permute-done | bytes 393248 | tf_op jit(solution)/shard_map/ppermute | solution.py:511
  176.0 7.8 %collective-permute-done.26 = bf16[4,64,768]{2,1,0:T(8,128)(2,1)S(1)} collective-permute-done((bf16[4,64,768]{2,1,0:T(8,128)(2,1)S(1)}, bf16[4,64,768]{2,1,0:T(8,128)(2,1)S(1)}, u32[]{:S(2)}, u32[]{:S(2)}) %collective-permute-start.26) | collective-permute-done | bytes 393248 | tf_op jit(solution)/shard_map/ppermute | solution.py:519
  188.7 8.5 %head_forward.3 = (bf16[1024,896]{1,0:T(8,128)(2,1)}, bf16[1024,1024]{1,0:T(8,128)(2,1)}, f32[1024,128]{1,0:T(8,128)}) custom-call(bf16[1024,768]{1,0:T(8,128)(2,1)} %copy-done.105, bf16[1024,768]{1,0:T(8,128)(2,1)} %pad.15.head), custom_call_target="tpu_custom_call" | custom-call | flops 3221225472 | bytes 2097152 | tf_op jit(solution)/shard_map/head_forward/pallas_call | solution.py:834
  197.7 8.5 %head_forward.2 = (bf16[1024,896]{1,0:T(8,128)(2,1)}, bf16[1024,1024]{1,0:T(8,128)(2,1)}, f32[1024,128]{1,0:T(8,128)}) custom-call(bf16[1024,768]{1,0:T(8,128)(2,1)} %bitcast.582, bf16[1024,768]{1,0:T(8,128)(2,1)} %pad.15.head), custom_call_target="tpu_custom_call" | custom-call | flops 3221225472 | bytes 2097152 | tf_op jit(solution)/shard_map/head_forward/pallas_call | solution.py:834
  214.4 4.2 collective-permute-done.29.refs_2_
  231.7 3.1 merge_parts.7
  240.8 6.3 %collective-permute-done.34.rest_12_ = bf16[64,896]{1,0:T(8,128)(2,1)S(1)} collective-permute-done((bf16[64,896]{1,0:T(8,128)(2,1)}, bf16[64,896]{1,0:T(8,128)(2,1)S(1)}, u32[]{:S(2)}, u32[]{:S(2)}) %collective-permute-start.34) | collective-permute-done | bytes 114720 | tf_op jit(solution)/shard_map/ppermute | solution.py:535
  247.7 20.4 %layer_backward.1 = (bf16[1216,768]{1,0:T(8,128)(2,1)}, bf16[256,768]{1,0:T(8,128)(2,1)}, f32[3,768]{1,0:T(4,128)}, f32[64,128]{1,0:T(8,128)}, f32[1,128]{1,0:T(1,128)}) custom-call(s32[32]{0:T(128)S(1)} %copy-done.177, s32[4]{0:T(128)} %pad_add_fusion.coord, s32[4]{0:T(128)} %copy-done.179, f32[4]{0:T(128)} %reshape.1139.refs, bf16[256,768]{1,0:T(8,128)(2,1)} %slice.540.x, ...), custom_call_target="tpu_custom_call" | custom-call | tf_op jit(solution)/shard_map/layer_backward/pallas_call | solution.py:1008
  269.1 3.2 collective-permute-done.36.theirs
  273.5 11.7 %weight_grads.1 = (bf16[4,2,192,384]{3,2,1,0:T(8,128)(2,1)}, bf16[4,2,192,384]{3,2,1,0:T(8,128)(2,1)}, bf16[4,2,192,384]{3,2,1,0:T(8,128)(2,1)}, bf16[4,2,192,38...) custom-call(s32[32]{0:T(128)} %copy-done.180, ...), custom_call_target="tpu_custom_call" | custom-call | tf_op jit(solution)/shard_map/weight_grads/pallas_call | solution.py:1131
  292.3 25.6 %all-to-all-done.2 = f32[32,1,2624]{2,1,0:T(1,128)S(1)} async-done(((f32[32,1,2624]{2,1,0:T(1,128)}), f32[32,1,2624]{2,1,0:T(1,128)S(1)}, u32[]{:S(2)}, u32[]{:S(2)}) %all-to-all-start.2) | async-done | bytes 335904 | tf_op jit(solution)/shard_map/all_to_all | solution.py:1423
  330.1 11.6 %head_grad.1.grad = f32[1024,768]{1,0:T(8,128)} custom-call(bf16[1024,768]{1,0:T(8,128)(2,1)} %bitcast.583, bf16[1024,768]{1,0:T(8,128)(2,1)} %copy-done.105, bf16[1024,1024]{1,0:T(8,128)(2,1)} %get-tuple-element.418.kept_a, bf16[1024,1024]{1,0:T(8,128)(2,1)} %get-tuple-element.419.kept_b, f32[1024,128]{1,0:T(8,128)} %get-tuple-element.420.stat_a, ...), custom_call_target="tpu_custom_call" | custom-call | flops 3221225472 | bytes 4194304 | tf_op jit(solution)/shard_map/head_grad/pallas_call | solution.py:893
  341.7 10.4 %adam.2 = (f32[2,1000,768]{2,1,0:T(8,128)}, f32[2,1000,768]{2,1,0:T(8,128)}, f32[2,1000,768]{2,1,0:T(8,128)}) custom-call(f32[1024,768]{1,0:T(8,128)} %head_grad.1.grad, f32[2,1000,768]{2,1,0:T(8,128)} %w.3, f32[2,1000,768]{2,1,0:T(8,128)} %m.3, f32[2,1000,768]{2,1,0:T(8,128)} %v.3), custom_call_target="tpu_custom_call" | custom-call | flops 7680000 | bytes 21504000 | tf_op jit(solution)/shard_map/adam/pallas_call | solution.py:1213
  354.7 3.1 add_convert_fusion.10
  358.8 5.6 %all-to-all-done.3 = bf16[32,18,768]{2,1,0:T(8,128)(2,1)S(1)} async-done(((bf16[32,18,768]{2,1,0:T(8,128)(2,1)}), bf16[32,18,768]{2,1,0:T(8,128)(2,1)S(1)}, u32[]{:S(2)}, u32[]{:S(2)}) %all-to-all-start.3) | async-done | bytes 884768 | tf_op jit(solution)/shard_map/all_to_all | solution.py:1431
  371.1 10.4 %adam.3 = (f32[2,1000,768]{2,1,0:T(8,128)}, f32[2,1000,768]{2,1,0:T(8,128)}, f32[2,1000,768]{2,1,0:T(8,128)}) custom-call(f32[1000,768]{1,0:T(8,128)} %fusion.189.grad, f32[2,1000,768]{2,1,0:T(8,128)} %w.3, f32[2,1000,768]{2,1,0:T(8,128)} %m.3, f32[2,1000,768]{2,1,0:T(8,128)} %v.3, ...), custom_call_target="tpu_custom_call", output_to_operand_aliasing={{0}: (4, {}), {1}: (5, {}), {2}: (6, {})} | custom-call | flops 7680000 | bytes 21504000 | tf_op jit(solution)/shard_map/adam/pallas_call | solution.py:1213
  394.0 3.3 collective-permute-done.45.refs_1_
  397.3 6.5 %collective-permute-done.47 = bf16[192,384]{1,0:T(8,128)(2,1)S(1)} collective-permute-done((bf16[192,384]{1,0:T(8,128)(2,1)}, bf16[192,384]{1,0:T(8,128)(2,1)S(1)}, u32[]{:S(2)}, u32[]{:S(2)}) %collective-permute-start.47) | collective-permute-done | bytes 147488 | tf_op jit(solution)/shard_map/grads_third/ppermute | solution.py:535
  406.2 7.4 %shampoo.2 = (f32[4,192,384]{2,1,0:T(8,128)}, f32[4,192,384]{2,1,0:T(8,128)}, f32[4,768,768]{2,1,0:T(8,128)}, f32[4,384,384]{2,1,0:T(8,128)}) custom-call(s32[4]{0:T(128)} %pad_add_fusion.coord, bf16[2,192,384]{2,1,0:T(8,128)(2,1)} %reduce-scatter.11.cloned.1.call-done.refs_0_, bf16[2,192,384]{2,1,0:T(8,128)(2,1)} %copy-done.126, ...), custom_call_target="tpu_custom_call" | custom-call | flops 1811939328 | bytes 16777216 | tf_op jit(solution)/shard_map/shampoo/pallas_call | solution.py:1178
  418.3 7.6 %shampoo.3 = (f32[4,192,384]{2,1,0:T(8,128)}, f32[4,192,384]{2,1,0:T(8,128)}, f32[4,768,768]{2,1,0:T(8,128)}, f32[4,384,384]{2,1,0:T(8,128)}) custom-call(s32[4]{0:T(128)} %pad_add_fusion.coord, bf16[2,192,384]{2,1,0:T(8,128)(2,1)} %pad_maximum_fusion.27.refs_0_, ...), custom_call_target="tpu_custom_call", output_to_operand_aliasing={{0}: (10, {}), {1}: (11, {}), {2}: (12, {}), {3}: (13, {})} | custom-call | flops 1811939328 | bytes 16777216 | tf_op jit(solution)/shard_map/shampoo/pallas_call | solution.py:1178
  (308 shorter events, 146.3 us)
Async XLA Ops:
  7.2 45.7 %all-gather.22.cloned.1.call-start = ((), (), s32[]{:S(2)}) async-start(), calls=%async_computation.13 | async-start | bytes 1474560 | tf_op jit(solution)/shard_map/weights_pair/all_gather | solution.py:1281
  9.4 23.1 %collective-permute-start = (bf16[192,384]{1,0:T(8,128)(2,1)}, bf16[192,384]{1,0:T(8,128)(2,1)}, u32[]{:S(2)}, u32[]{:S(2)}) collective-permute-start(bf16[192,384]{1,0:T(8,128)(2,1)} %get-tuple-element.1018), channel_id=1, source_target_pairs={{0,8},{1,9},{2,10},{3,11},{4,12},{5,13},{6,14},{7,15},{8,16},{9,17... | collective-permute-start | bytes 442376 | tf_op jit(solution)/shard_map/weights_third/ppermute | solution.py:535
  12.4 20.1 %collective-permute-start.1 = (bf16[192,384]{1,0:T(8,128)(2,1)}, bf16[192,384]{1,0:T(8,128)(2,1)}, u32[]{:S(2)}, u32[]{:S(2)}) collective-permute-start(bf16[192,384]{1,0:T(8,128)(2,1)} %get-tuple-element.1018), channel_id=1, source_target_pairs={{0,16},{1,17},{2,18},{3,19},{4,20},{5,21},{6,22},{7,23},{8,24},{9,... | collective-permute-start | bytes 442376 | tf_op jit(solution)/shard_map/weights_third/ppermute | solution.py:535
  15.0 17.5 %collective-permute-start.2 = (bf16[192,384]{1,0:T(8,128)(2,1)}, bf16[192,384]{1,0:T(8,128)(2,1)}, u32[]{:S(2)}, u32[]{:S(2)}) collective-permute-start(bf16[192,384]{1,0:T(8,128)(2,1)} %get-tuple-element.1018), channel_id=1, source_target_pairs={{0,24},{1,25},{2,26},{3,27},{4,28},{5,29},{6,30},{7,31},{8,0},{9,1... | collective-permute-start | bytes 442376 | tf_op jit(solution)/shard_map/weights_third/ppermute | solution.py:535
  17.8 17.2 %collective-permute-start.4 = (bf16[192,384]{1,0:T(8,128)(2,1)}, bf16[192,384]{1,0:T(8,128)(2,1)}, u32[]{:S(2)}, u32[]{:S(2)}) collective-permute-start(bf16[192,384]{1,0:T(8,128)(2,1)} %get-tuple-element.1019), channel_id=1, source_target_pairs={{0,2},{1,5},{2,0},{3,7},{4,6},{5,1},{6,4},{7,3},{8,10},{9,13},{10,... | collective-permute-start | bytes 442376 | tf_op jit(solution)/shard_map/weights_last/ppermute | solution.py:519
  29.3 96.7 %all-gather.24.cloned.1.call-start = ((), (), s32[]{:S(2)}) async-start(), calls=%async_computation.14 | async-start | bytes 2949120 | tf_op jit(solution)/shard_map/weights_last/all_gather | solution.py:1333
  36.9 16.0 %collective-permute-start.6 = (bf16[4,192,384]{2,1,0:T(8,128)(2,1)}, bf16[4,192,384]{2,1,0:T(8,128)(2,1)}, u32[]{:S(2)}, u32[]{:S(2)}) collective-permute-start(bf16[4,192,384]{2,1,0:T(8,128)(2,1)} %pad_maximum_fusion.24.rest_8_.rest_22_), channel_id=1, source_target_pairs={{0,4},{1,3},{2,6},{3,1},{4,0},{5,7},{6,2},{7,5},{8,12},{9,11},{10,... | collective-permute-start | bytes 1769480 | tf_op jit(solution)/shard_map/weights_third/ppermute | solution.py:511
  38.5 14.4 %collective-permute-start.7 = (bf16[4,192,384]{2,1,0:T(8,128)(2,1)}, bf16[4,192,384]{2,1,0:T(8,128)(2,1)}, u32[]{:S(2)}, u32[]{:S(2)}) collective-permute-start(bf16[4,192,384]{2,1,0:T(8,128)(2,1)} %pad_maximum_fusion.24.rest_8_.rest_22_), channel_id=1, source_target_pairs={{0,2},{1,5},{2,0},{3,7},{4,6},{5,1},{6,4},{7,3},{8,10},{9,13},{10,... | collective-permute-start | bytes 1769480 | tf_op jit(solution)/shard_map/weights_third/ppermute | solution.py:519
  53.0 61.7 %all-to-all-start.1 = ((bf16[32,24,768]{2,1,0:T(8,128)(2,1)}), bf16[32,24,768]{2,1,0:T(8,128)(2,1)}, u32[]{:S(2)}, u32[]{:S(2)}) async-start(bf16[32,24,768]{2,1,0:T(8,128)(2,1)} %bitcast.597), calls=%async_computation.6 | async-start | bytes 2359296 | tf_op jit(solution)/shard_map/all_to_all | solution.py:1331
  58.8 299.0 %reduce-scatter.9.cloned.1.call-start = ((), (), s32[]{:S(2)}) async-start(), calls=%async_computation.11 | async-start | bytes 2949120 | tf_op jit(solution)/shard_map/grads_last/reduce_scatter | solution.py:1414
  59.5 26.2 %collective-permute-start.10 = (bf16[4,192,384]{2,1,0:T(8,128)(2,1)}, bf16[4,192,384]{2,1,0:T(8,128)(2,1)S(1)}, u32[]{:S(2)}, u32[]{:S(2)}) collective-permute-start(bf16[4,192,384]{2,1,0:T(8,128)(2,1)} %collective-permute-done.6.rest_10_.rest_24_), channel_id=1, source_target_pairs={{0,2},{1,5},{2,0},{3,7},{4,6},{5,1},{6,4},{7,3},{8,10},{9,13},{10,... | collective-permute-start | bytes 1769480 | tf_op jit(solution)/shard_map/weights_third/ppermute | solution.py:519
  61.1 26.9 %collective-permute-start.14 = (bf16[4,2,192,384]{3,2,1,0:T(8,128)(2,1)}, bf16[4,2,192,384]{3,2,1,0:T(8,128)(2,1)S(1)}, u32[]{:S(2)}, u32[]{:S(2)}) collective-permute-start(bf16[4,2,192,384]{3,2,1,0:T(8,128)(2,1)} %bitcast.584), channel_id=1, source_target_pairs={{0,1},{1,0},{2,3},{3,2},{4,5},{5,4},{6,7},{7,6},{8,9},{9,8},{10,11... | collective-permute-start | bytes 3538952 | tf_op jit(solution)/shard_map/ppermute | solution.py:527
  61.2 38.1 %collective-permute-start.8 = (bf16[4,2,192,384]{3,2,1,0:T(8,128)(2,1)}, bf16[4,2,192,384]{3,2,1,0:T(8,128)(2,1)}, u32[]{:S(2)}, u32[]{:S(2)}) collective-permute-start(bf16[4,2,192,384]{3,2,1,0:T(8,128)(2,1)} %bitcast.585), channel_id=1, source_target_pairs={{0,4},{1,3},{2,6},{3,1},{4,0},{5,7},{6,2},{7,5},{8,12},{9,11},{10,... | collective-permute-start | bytes 3538952 | tf_op jit(solution)/shard_map/weights_pair/ppermute | solution.py:511
  62.6 42.9 %collective-permute-start.9 = (bf16[4,2,192,384]{3,2,1,0:T(8,128)(2,1)}, bf16[4,2,192,384]{3,2,1,0:T(8,128)(2,1)S(1)}, u32[]{:S(2)}, u32[]{:S(2)}) collective-permute-start(bf16[4,2,192,384]{3,2,1,0:T(8,128)(2,1)} %bitcast.586), channel_id=1, source_target_pairs={{0,2},{1,5},{2,0},{3,7},{4,6},{5,1},{6,4},{7,3},{8,10},{9,13},{10,... | collective-permute-start | bytes 3538952 | tf_op jit(solution)/shard_map/weights_pair/ppermute | solution.py:519
  63.2 23.9 %collective-permute-start.12 = (bf16[4,192,384]{2,1,0:T(8,128)(2,1)}, bf16[4,192,384]{2,1,0:T(8,128)(2,1)}, u32[]{:S(2)}, u32[]{:S(2)}) collective-permute-start(bf16[4,192,384]{2,1,0:T(8,128)(2,1)} %collective-permute-done.6.rest_10_.rest_24_), channel_id=1, source_target_pairs={{0,1},{1,0},{2,3},{3,2},{4,5},{5,4},{6,7},{7,6},{8,9},{9,8},{10,11... | collective-permute-start | bytes 1769480 | tf_op jit(solution)/shard_map/ppermute | solution.py:527
  105.5 12.5 %collective-permute-start.16 = (bf16[4,2,192,384]{3,2,1,0:T(8,128)(2,1)S(1)}, bf16[4,2,192,384]{3,2,1,0:T(8,128)(2,1)}, u32[]{:S(2)}, u32[]{:S(2)}) collective-permute-start(bf16[4,2,192,384]{3,2,1,0:T(8,128)(2,1)S(1)} %collective-permute-done.9.rest_4_.rest_18_), channel_id=1, source_target_pairs={{0,1},{1,0},{2,3},{3,2},{4,5},{5,4},{6,7},{7,6},{8,9},{9,8},{10,11... | collective-permute-start | bytes 3538952 | tf_op jit(solution)/shard_map/ppermute | solution.py:527
  109.6 19.3 %collective-permute-start.18 = (bf16[4,2,192,384]{3,2,1,0:T(8,128)(2,1)}, bf16[4,2,192,384]{3,2,1,0:T(8,128)(2,1)}, u32[]{:S(2)}, u32[]{:S(2)}) collective-permute-start(bf16[4,2,192,384]{3,2,1,0:T(8,128)(2,1)} %collective-permute-done.8.rest_2_.rest_16_), channel_id=1, source_target_pairs={{0,2},{1,5},{2,0},{3,7},{4,6},{5,1},{6,4},{7,3},{8,10},{9,13},{10,... | collective-permute-start | bytes 3538952 | tf_op jit(solution)/shard_map/weights_pair/ppermute | solution.py:519
  197.3 27.2 %collective-permute-start.32 = (bf16[704,768]{1,0:T(8,128)(2,1)}, bf16[704,768]{1,0:T(8,128)(2,1)S(1)}, u32[]{:S(2)}, u32[]{:S(2)}) collective-permute-start(bf16[704,768]{1,0:T(8,128)(2,1)} %get-tuple-element.382.mine), channel_id=1, source_target_pairs={{0,1},{1,0},{2,3},{3,2},{4,5},{5,4},{6,7},{7,6},{8,9},{9,8},{10,11... | collective-permute-start | bytes 3244040 | tf_op jit(solution)/shard_map/ppermute | solution.py:527
  212.4 16.2 %collective-permute-start.31 = (bf16[256,896]{1,0:T(8,128)(2,1)}, bf16[256,896]{1,0:T(8,128)(2,1)S(1)}, u32[]{:S(2)}, u32[]{:S(2)}) collective-permute-start(bf16[256,896]{1,0:T(8,128)(2,1)} %merge_parts.6), channel_id=1, source_target_pairs={{0,2},{1,5},{2,0},{3,7},{4,6},{5,1},{6,4},{7,3},{8,10},{9,13},{10,... | collective-permute-start | bytes 1376264 | tf_op jit(solution)/shard_map/ppermute | solution.py:519
  285.2 32.7 %collective-permute-start.37 = (bf16[4,2,192,384]{3,2,1,0:T(8,128)(2,1)}, bf16[4,2,192,384]{3,2,1,0:T(8,128)(2,1)}, u32[]{:S(2)}, u32[]{:S(2)}) collective-permute-start(bf16[4,2,192,384]{3,2,1,0:T(8,128)(2,1)} %get-tuple-element.405), channel_id=1, source_target_pairs={{0,2},{1,5},{2,0},{3,7},{4,6},{5,1},{6,4},{7,3},{8,10},{9,13},{10,... | collective-permute-start | bytes 3538952 | tf_op jit(solution)/shard_map/grads_pair/ppermute | solution.py:519
  285.6 35.3 %collective-permute-start.38 = (bf16[4,2,192,384]{3,2,1,0:T(8,128)(2,1)}, bf16[4,2,192,384]{3,2,1,0:T(8,128)(2,1)}, u32[]{:S(2)}, u32[]{:S(2)}) collective-permute-start(bf16[4,2,192,384]{3,2,1,0:T(8,128)(2,1)} %get-tuple-element.406), channel_id=1, source_target_pairs={{0,2},{1,5},{2,0},{3,7},{4,6},{5,1},{6,4},{7,3},{8,10},{9,13},{10,... | collective-permute-start | bytes 3538952 | tf_op jit(solution)/shard_map/grads_pair/ppermute | solution.py:519
  288.5 29.4 %all-to-all-start.2 = ((f32[32,1,2624]{2,1,0:T(1,128)}), f32[32,1,2624]{2,1,0:T(1,128)S(1)}, u32[]{:S(2)}, u32[]{:S(2)}) async-start(f32[32,1,2624]{2,1,0:T(1,128)} %broadcast_in_dim.197), calls=%async_computation.7 | async-start | bytes 688128 | tf_op jit(solution)/shard_map/all_to_all | solution.py:1423
  322.2 30.0 %collective-permute-start.40 = (bf16[4,192,384]{2,1,0:T(8,128)(2,1)}, bf16[4,192,384]{2,1,0:T(8,128)(2,1)}, u32[]{:S(2)}, u32[]{:S(2)}) collective-permute-start(bf16[4,192,384]{2,1,0:T(8,128)(2,1)} %get-tuple-element.415), channel_id=1, source_target_pairs={{0,2},{1,5},{2,0},{3,7},{4,6},{5,1},{6,4},{7,3},{8,10},{9,13},{10,... | collective-permute-start | bytes 1769480 | tf_op jit(solution)/shard_map/grads_third/ppermute | solution.py:519
  322.7 32.0 %collective-permute-start.39 = (bf16[4,2,192,384]{3,2,1,0:T(8,128)(2,1)}, bf16[4,2,192,384]{3,2,1,0:T(8,128)(2,1)}, u32[]{:S(2)}, u32[]{:S(2)}) collective-permute-start(bf16[4,2,192,384]{3,2,1,0:T(8,128)(2,1)} %add_convert_fusion.11), channel_id=1, source_target_pairs={{0,4},{1,3},{2,6},{3,1},{4,0},{5,7},{6,2},{7,5},{8,12},{9,11},{10,... | collective-permute-start | bytes 3538952 | tf_op jit(solution)/shard_map/grads_pair/ppermute | solution.py:511
  325.7 38.7 %all-to-all-start.3 = ((bf16[32,18,768]{2,1,0:T(8,128)(2,1)}), bf16[32,18,768]{2,1,0:T(8,128)(2,1)S(1)}, u32[]{:S(2)}, u32[]{:S(2)}) async-start(bf16[32,18,768]{2,1,0:T(8,128)(2,1)} %all_to_all.38), calls=%async_computation.9 | async-start | bytes 2359296 | tf_op jit(solution)/shard_map/all_to_all | solution.py:1431
  328.4 59.6 %reduce-scatter.11.cloned.1.call-start = ((), (), s32[]{:S(2)}) async-start(), calls=%async_computation.12 | async-start | bytes 1474560 | tf_op jit(solution)/shard_map/grads_pair/reduce_scatter | solution.py:1459
  364.7 18.5 %collective-permute-start.43 = (bf16[4,192,384]{2,1,0:T(8,128)(2,1)}, bf16[4,192,384]{2,1,0:T(8,128)(2,1)}, u32[]{:S(2)}, u32[]{:S(2)}) collective-permute-start(bf16[4,192,384]{2,1,0:T(8,128)(2,1)} %add_convert_fusion.12), channel_id=1, source_target_pairs={{0,4},{1,3},{2,6},{3,1},{4,0},{5,7},{6,2},{7,5},{8,12},{9,11},{10,... | collective-permute-start | bytes 1769480 | tf_op jit(solution)/shard_map/grads_third/ppermute | solution.py:511
  364.8 18.4 %collective-permute-start.44 = (bf16[4,192,384]{2,1,0:T(8,128)(2,1)}, bf16[4,192,384]{2,1,0:T(8,128)(2,1)}, u32[]{:S(2)}, u32[]{:S(2)}) collective-permute-start(bf16[4,192,384]{2,1,0:T(8,128)(2,1)} %get-tuple-element.434), channel_id=1, source_target_pairs={{0,2},{1,5},{2,0},{3,7},{4,6},{5,1},{6,4},{7,3},{8,10},{9,13},{10,... | collective-permute-start | bytes 1769480 | tf_op jit(solution)/shard_map/grads_third/ppermute | solution.py:519
  365.9 15.5 %collective-permute-start.41 = (bf16[192,384]{1,0:T(8,128)(2,1)S(1)}, bf16[192,384]{1,0:T(8,128)(2,1)S(1)}, u32[]{:S(2)}, u32[]{:S(2)}) collective-permute-start(bf16[192,384]{1,0:T(8,128)(2,1)S(1)} %get-tuple-element.1016), channel_id=1, source_target_pairs={{0,2},{1,5},{2,0},{3,7},{4,6},{5,1},{6,4},{7,3},{8,10},{9,13},{10,... | collective-permute-start | bytes 442376 | tf_op jit(solution)/shard_map/grads_last/ppermute | solution.py:519
  370.0 15.7 %collective-permute-start.42 = (bf16[192,384]{1,0:T(8,128)(2,1)S(1)}, bf16[192,384]{1,0:T(8,128)(2,1)}, u32[]{:S(2)}, u32[]{:S(2)}) collective-permute-start(bf16[192,384]{1,0:T(8,128)(2,1)S(1)} %get-tuple-element.1015), channel_id=1, source_target_pairs={{0,2},{1,5},{2,0},{3,7},{4,6},{5,1},{6,4},{7,3},{8,10},{9,13},{10,... | collective-permute-start | bytes 442376 | tf_op jit(solution)/shard_map/grads_last/ppermute | solution.py:519
  390.5 13.3 %collective-permute-start.47 = (bf16[192,384]{1,0:T(8,128)(2,1)}, bf16[192,384]{1,0:T(8,128)(2,1)S(1)}, u32[]{:S(2)}, u32[]{:S(2)}) collective-permute-start(bf16[192,384]{1,0:T(8,128)(2,1)} %get-tuple-element.439), channel_id=1, source_target_pairs={{0,16},{1,17},{2,18},{3,19},{4,20},{5,21},{6,22},{7,23},{8,24},{9,... | collective-permute-start | bytes 442376 | tf_op jit(solution)/shard_map/grads_third/ppermute | solution.py:535
  390.5 13.3 %collective-permute-start.48 = (bf16[192,384]{1,0:T(8,128)(2,1)}, bf16[192,384]{1,0:T(8,128)(2,1)S(1)}, u32[]{:S(2)}, u32[]{:S(2)}) collective-permute-start(bf16[192,384]{1,0:T(8,128)(2,1)} %get-tuple-element.440), channel_id=1, source_target_pairs={{0,8},{1,9},{2,10},{3,11},{4,12},{5,13},{6,14},{7,15},{8,16},{9,17... | collective-permute-start | bytes 442376 | tf_op jit(solution)/shard_map/grads_third/ppermute | solution.py:535
  (79 other events, 851.1 us)
Sparse Core Ops, SparseCore 0:
  20.2 27.3 all-gather.21
  53.1 72.9 all-gather.23
  285.3 53.4 reduce-scatter.8
  358.0 29.9 reduce-scatter.10

commit v5 on v4

--- a/solution.py
+++ b/solution.py
@@ -638,6 +638,22 @@
     return same & (key <= pos), same & (key == pos)
 
 
+def both_heads(chunk, first):
+    zero = jnp.zeros(chunk.shape, chunk.dtype)
+    return jnp.concatenate([jnp.where(first, chunk, zero), jnp.where(first, zero, chunk)], axis=0)
+
+
+def own_lanes(stacked, first):
+    return jnp.where(first, stacked[:PAIR_ROWS], stacked[PAIR_ROWS:])
+
+
+def probabilities(queries, keys, valid):
+    s = dot_nt(queries, keys) * (1.0 / math.sqrt(HDIM))
+    s = jnp.where(valid, s, MASKED)
+    e = jnp.exp(s - jnp.max(s, axis=-1, keepdims=True))
+    return e / jnp.sum(e, axis=-1, keepdims=True)
+
+
 def turn(chunk, cosine, sine, sign):
     lane = iota(chunk.shape, 1)
     swapped = jnp.where((lane & 63) < 32, pltpu.roll(chunk, 96, 1), pltpu.roll(chunk, 32, 1))
@@ -677,19 +693,12 @@
             at = slice(j * BC + i * 128, j * BC + (i + 1) * 128)
             q_out[:, at] = low(turn(q[:, i * 128 : (i + 1) * 128], cos_q[...], sin_q[...], 1.0))
             k_out[:, at] = low(turn(k[:, i * 128 : (i + 1) * 128], cos_k[...], sin_k[...], 1.0))
-    lane = iota((TOKENS, 128), 1)
-    zero = jnp.zeros((TOKENS, 128), jnp.bfloat16)
+    first = iota((PAIR_ROWS, 128), 1) < HDIM
+    valid = jnp.concatenate([valid, valid], axis=0)
     for p in range(HEADS // 2):
         at = slice(p * 128, (p + 1) * 128)
-        total = jnp.zeros((PAIR_ROWS, 128), jnp.float32)
-        for h in range(2):
-            mine = (lane >> 6) == h
-            s = dot_nt(q_out[:, at], jnp.where(mine, k_out[:, at], zero)) * (1.0 / math.sqrt(HDIM))
-            s = jnp.where(valid, s, MASKED)
-            e = jnp.exp(s - jnp.max(s, axis=-1, keepdims=True))
-            prob = low(e / jnp.sum(e, axis=-1, keepdims=True))
-            total = total + dot_nn(prob, jnp.where(mine, v_out[:, at], zero))
-        left[AT_O:AT_B, at] = low(total)
+        prob = low(probabilities(both_heads(q_out[:, at], first), k_out[:, at], valid))
+        left[AT_O:AT_B, at] = low(own_lanes(dot_nn(prob, v_out[:, at]), first))
     for j in range(2):
         at = slice(j * BC, (j + 1) * BC)
         h1_out[:, at] = x_pick[:, at] + dot_nn(left[AT_O:AT_B], held[owner[6 + j]])
@@ -817,8 +826,10 @@
 
 def head_kernel(real, rows, head, ext, kept, stat):
     logits = dot_nt(rows[...], head[...])
-    col = iota(logits.shape, 1)
-    logits = jnp.where(col < real, logits, MASKED)
+    whole = head.shape[0] - 128
+    end = logits[:, whole:]
+    end = jnp.where(iota(end.shape, 1) < real - whole, end, MASKED)
+    logits = jnp.concatenate([logits[:, :whole], end], axis=1)
     top = jnp.max(logits, axis=-1, keepdims=True)
     e = jnp.exp(logits - top)
     total = jnp.sum(e, axis=-1, keepdims=True)
@@ -831,22 +842,23 @@
 
 def head_call(rows, head, real):
     number, wide = rows.shape[0], head.shape[0]
+    block = number // 2
     return pl.pallas_call(
         functools.partial(head_kernel, real),
-        grid=(number // 256,),
+        grid=(number // block,),
         out_shape=(
             jax.ShapeDtypeStruct((number, EXT), jnp.bfloat16),
             jax.ShapeDtypeStruct((number, wide), jnp.bfloat16),
             jax.ShapeDtypeStruct((number, 128), jnp.float32),
         ),
         in_specs=[
-            pl.BlockSpec((256, D), lambda i: (i, 0)),
+            pl.BlockSpec((block, D), lambda i: (i, 0)),
             pl.BlockSpec((wide, D), lambda i: (0, 0)),
         ],
         out_specs=(
-            pl.BlockSpec((256, EXT), lambda i: (i, 0)),
-            pl.BlockSpec((256, wide), lambda i: (i, 0)),
-            pl.BlockSpec((256, 128), lambda i: (i, 0)),
+            pl.BlockSpec((block, EXT), lambda i: (i, 0)),
+            pl.BlockSpec((block, wide), lambda i: (i, 0)),
+            pl.BlockSpec((block, 128), lambda i: (i, 0)),
         ),
         compiler_params=pltpu.CompilerParams(vmem_limit_bytes=VMEM_LIMIT),
         cost_estimate=pl.CostEstimate(
@@ -964,30 +976,19 @@
     d_att = low(
         dot_nt(d1_low[:, :BC], held[owner[6]]) + dot_nt(d1_low[:, BC:], held[owner[7]])
     )
-    lane_k = iota((TOKENS, 128), 1)
-    zero_k = jnp.zeros((TOKENS, 128), jnp.bfloat16)
-    zero_q = jnp.zeros((PAIR_ROWS, 128), jnp.bfloat16)
     root = 1.0 / math.sqrt(HDIM)
+    first = lane < HDIM
+    valid = jnp.concatenate([valid, valid], axis=0)
     for p in range(HEADS // 2):
         at = slice(p * 128, (p + 1) * 128)
-        d_q = jnp.zeros((PAIR_ROWS, 128), jnp.float32)
-        d_k = jnp.zeros((TOKENS, 128), jnp.float32)
-        d_v = jnp.zeros((TOKENS, 128), jnp.float32)
-        for h in range(2):
-            mine_k = (lane_k >> 6) == h
-            mine_q = (lane >> 6) == h
-            k_one = jnp.where(mine_k, k[:, at], zero_k)
-            q_one = jnp.where(mine_q, q[:, at], zero_q)
-            do_one = jnp.where(mine_q, d_att[:, at], zero_q)
-            s = dot_nt(q_one, k_one) * root
-            s = jnp.where(valid, s, MASKED)
-            e = jnp.exp(s - jnp.max(s, axis=-1, keepdims=True))
-            prob = e / jnp.sum(e, axis=-1, keepdims=True)
-            d_p = dot_nt(do_one, v[:, at])
-            d_s = low(prob * (d_p - jnp.sum(prob * d_p, axis=-1, keepdims=True)))
-            d_q = d_q + dot_nn(d_s, k_one)
-            d_k = d_k + dot_tn(d_s, q_one)
-            d_v = d_v + dot_tn(low(prob), do_one)
+        queries = both_heads(q[:, at], first)
+        grads = both_heads(d_att[:, at], first)
+        prob = probabilities(queries, k[:, at], valid)
+        d_p = dot_nt(grads, v[:, at])
+        d_s = low(prob * (d_p - jnp.sum(prob * d_p, axis=-1, keepdims=True)))
+        d_q = own_lanes(dot_nn(d_s, k[:, at]), first)
+        d_k = dot_tn(d_s, queries)
+        d_v = dot_tn(low(prob), grads)
         act[AT_DQ:AT_DO, at] = low(turn(d_q * root, cos_q[...], sin_q[...], -1.0))
         act[AT_DK:AT_DV, at] = low(turn(d_k * root, cos_k[...], sin_k[...], -1.0))
         act[AT_DV:AT_DQ, at] = low(d_v)

time: 440 us -> 437 us (level)
  no operation moved by 1% of the time
where the time goes in v5:
time: 437 us; the launch traced here: 431 us
  waiting for transfers between devices  152 us (35%)
  Pallas kernels  122 us (28%)
  starting transfers between devices  64.1 us (15%)
  other arithmetic  38.6 us (9%)
  local copies, waits for them, and re-layouts  27.1 us (6%)
  between operations  16.4 us (4%)
  matrix products  9.22 us (2%)
    ppermute x16, waiting for transfers between devices, hop_two(): lax.ppermute(value, AXES, moves(lambda z, x, y, c: (z, x, 1 - y, c) if c...  40.7 us
    ppermute x8, waiting for transfers between devices, hop_one(): lax.ppermute(value, AXES, moves(lambda z, x, y, c: (z, 1 - x, y, c) if c...  32.1 us
    all_to_all x1, waiting for transfers between devices, per_core(): heard = lax.all_to_all(told, AXES, 0, 0, tiled=True)  25.6 us
    pallas_call x2, Pallas kernels, adam_call(): pl.pallas_call(functools.partial(adam_kernel, rate), grid=(rows // block,...  20.8 us
    ppermute x12, waiting for transfers between devices, ring(): lax.ppermute(value, AXES, moves(lambda z, x, y, c: ((z + step) % 4, x, y,...  20.5 us
    pallas_call x1, Pallas kernels, backward_call(): pl.pallas_call(backward_kernel, out_shape=(jax.ShapeDtypeStruct((RIGHT_RO...  19.9 us
    ppermute x12, starting transfers between devices, ring(): lax.ppermute(value, AXES, moves(lambda z, x, y, c: ((z + step) % 4, x, y,...  18.2 us
    ppermute x16, starting transfers between devices, hop_two(): lax.ppermute(value, AXES, moves(lambda z, x, y, c: (z, x, 1 - y, c) if c...  16.3 us
  transfers between devices with their start and end apart: 63, of which 26 were waited for; matrix products, arithmetic and copies ran while one was open for 14% of the time, Pallas kernels for 14%

profile of v5, /device:TPU:0, one launch (start us, length us, event | category | flops | bytes accessed | tf_op | source)
XLA Modules:
  0.0 431.2 jit_solution(8159840510159730881)
XLA Ops:
  40.1 3.9 fusion.190
  44.0 8.9 %collective-permute-done.6.rest_10_.rest_24_ = bf16[4,192,384]{2,1,0:T(8,128)(2,1)} collective-permute-done((bf16[4,192,384]{2,1,0:T(8,128)(2,1)}, bf16[4,192,384]{2,1,0:T(8,128)(2,1)}, u32[]{:S(2)}, u32[]{:S(2)}) %collective-permute-start.6) | collective-permute-done | bytes 589856 | tf_op jit(solution)/shard_map/weights_third/ppermute | solution.py:511
  53.0 5.9 %all-to-all-start.1 = ((bf16[32,24,768]{2,1,0:T(8,128)(2,1)}), bf16[32,24,768]{2,1,0:T(8,128)(2,1)}, u32[]{:S(2)}, u32[]{:S(2)}) async-start(bf16[32,24,768]{2,1,0:T(8,128)(2,1)} %bitcast.597), calls=%async_computation.6 | async-start | bytes 2359296 | tf_op jit(solution)/shard_map/all_to_all | solution.py:1332
  63.2 22.4 %collective-permute-done.10.rest_14_.rest_28_ = bf16[4,192,384]{2,1,0:T(8,128)(2,1)S(1)} collective-permute-done((bf16[4,192,384]{2,1,0:T(8,128)(2,1)}, bf16[4,192,384]{2,1,0:T(8,128)(2,1)S(1)}, u32[]{:S(2)}, u32[]{:S(2)}) %collective-permute-start.10) | collective-permute-done | bytes 589856 | tf_op jit(solution)/shard_map/weights_third/ppermute | solution.py:519
  88.0 11.2 %collective-permute-done.8.rest_2_.rest_16_ = bf16[4,2,192,384]{3,2,1,0:T(8,128)(2,1)} collective-permute-done((bf16[4,2,192,384]{3,2,1,0:T(8,128)(2,1)}, bf16[4,2,192,384]{3,2,1,0:T(8,128)(2,1)}, u32[]{:S(2)}, u32[]{:S(2)}) %collective-permute-start.8) | collective-permute-done | bytes 1179680 | tf_op jit(solution)/shard_map/weights_pair/ppermute | solution.py:511
  99.3 6.2 %collective-permute-done.9.rest_4_.rest_18_ = bf16[4,2,192,384]{3,2,1,0:T(8,128)(2,1)S(1)} collective-permute-done((bf16[4,2,192,384]{3,2,1,0:T(8,128)(2,1)}, bf16[4,2,192,384]{3,2,1,0:T(8,128)(2,1)S(1)}, u32[]{:S(2)}, u32[]{:S(2)}) %collective-permute-start.9) | collective-permute-done | bytes 1179680 | tf_op jit(solution)/shard_map/weights_pair/ppermute | solution.py:519
  110.8 3.8 all-to-all-done.1
  118.0 8.0 %all-gather.24.cloned.1.call-done = bf16[16,192,384]{2,1,0:T(8,128)(2,1)} async-done(((bf16[4,192,384]{2,1,0:T(8,128)(2,1)}), bf16[16,192,384]{2,1,0:T(8,128)(2,1)}) %all-gather.24.cloned.1.call-update) | async-done | bytes 2359312 | tf_op jit(solution)/shard_map/weights_last/all_gather | solution.py:1334
  130.0 5.1 %collective-permute-done.19.rest_7_.rest_21_ = bf16[4,2,192,384]{3,2,1,0:T(8,128)(2,1)} collective-permute-done((bf16[4,2,192,384]{3,2,1,0:T(8,128)(2,1)}, bf16[4,2,192,384]{3,2,1,0:T(8,128)(2,1)}, u32[]{:S(2)}, u32[]{:S(2)}) %collective-permute-start.19) | collective-permute-done | bytes 1179680 | tf_op jit(solution)/shard_map/ppermute | solution.py:527
  136.7 13.2 %layer_forward.1 = (bf16[704,768]{1,0:T(8,128)(2,1)}, bf16[64,768]{1,0:T(8,128)(2,1)}, bf16[256,768]{1,0:T(8,128)(2,1)}, bf16[256,768]{1,0:T(8,128)(2,1)}, f32[6...) custom-call(s32[32]{0:T(128)} %owner.3, ...), custom_call_target="tpu_custom_call" | custom-call | tf_op jit(solution)/shard_map/layer_forward/pallas_call | solution.py:744
  154.4 3.4 collective-permute-done.21
  157.7 3.3 collective-permute-done.22
  165.0 9.1 %collective-permute-done.24 = bf16[4,64,768]{2,1,0:T(8,128)(2,1)S(1)} collective-permute-done((bf16[4,64,768]{2,1,0:T(8,128)(2,1)S(1)}, bf16[4,64,768]{2,1,0:T(8,128)(2,1)S(1)}, u32[]{:S(2)}, u32[]{:S(2)}) %collective-permute-start.24) | collective-permute-done | bytes 393248 | tf_op jit(solution)/shard_map/ppermute | solution.py:511
  174.1 7.8 %collective-permute-done.26 = bf16[4,64,768]{2,1,0:T(8,128)(2,1)S(1)} collective-permute-done((bf16[4,64,768]{2,1,0:T(8,128)(2,1)S(1)}, bf16[4,64,768]{2,1,0:T(8,128)(2,1)S(1)}, u32[]{:S(2)}, u32[]{:S(2)}) %collective-permute-start.26) | collective-permute-done | bytes 393248 | tf_op jit(solution)/shard_map/ppermute | solution.py:519
  186.8 8.2 %head_forward.3 = (bf16[1024,896]{1,0:T(8,128)(2,1)}, bf16[1024,1024]{1,0:T(8,128)(2,1)}, f32[1024,128]{1,0:T(8,128)}) custom-call(bf16[1024,768]{1,0:T(8,128)(2,1)} %copy-done.105, bf16[1024,768]{1,0:T(8,128)(2,1)} %pad.15.head), custom_call_target="tpu_custom_call" | custom-call | flops 3221225472 | bytes 2097152 | tf_op jit(solution)/shard_map/head_forward/pallas_call | solution.py:846
  195.5 8.2 %head_forward.2 = (bf16[1024,896]{1,0:T(8,128)(2,1)}, bf16[1024,1024]{1,0:T(8,128)(2,1)}, f32[1024,128]{1,0:T(8,128)}) custom-call(bf16[1024,768]{1,0:T(8,128)(2,1)} %bitcast.582, bf16[1024,768]{1,0:T(8,128)(2,1)} %pad.15.head), custom_call_target="tpu_custom_call" | custom-call | flops 3221225472 | bytes 2097152 | tf_op jit(solution)/shard_map/head_forward/pallas_call | solution.py:846
  212.0 4.2 collective-permute-done.29.refs_2_
  229.2 3.1 merge_parts.7
  238.2 6.3 %collective-permute-done.34.rest_12_ = bf16[64,896]{1,0:T(8,128)(2,1)S(1)} collective-permute-done((bf16[64,896]{1,0:T(8,128)(2,1)}, bf16[64,896]{1,0:T(8,128)(2,1)S(1)}, u32[]{:S(2)}, u32[]{:S(2)}) %collective-permute-start.34) | collective-permute-done | bytes 114720 | tf_op jit(solution)/shard_map/ppermute | solution.py:535
  245.3 19.9 %layer_backward.1 = (bf16[1216,768]{1,0:T(8,128)(2,1)}, bf16[256,768]{1,0:T(8,128)(2,1)}, f32[3,768]{1,0:T(4,128)}, f32[64,128]{1,0:T(8,128)}, f32[1,128]{1,0:T(1,128)}) custom-call(s32[32]{0:T(128)S(1)} %copy-done.177, s32[4]{0:T(128)} %pad_add_fusion.coord, s32[4]{0:T(128)} %copy-done.179, f32[4]{0:T(128)} %reshape.1139.refs, bf16[256,768]{1,0:T(8,128)(2,1)} %slice.540.x, ...), custom_call_target="tpu_custom_call" | custom-call | tf_op jit(solution)/shard_map/layer_backward/pallas_call | solution.py:1009
  266.1 3.2 collective-permute-done.36.theirs
  270.5 11.7 %weight_grads.1 = (bf16[4,2,192,384]{3,2,1,0:T(8,128)(2,1)}, bf16[4,2,192,384]{3,2,1,0:T(8,128)(2,1)}, bf16[4,2,192,384]{3,2,1,0:T(8,128)(2,1)}, bf16[4,2,192,38...) custom-call(s32[32]{0:T(128)} %copy-done.180, ...), custom_call_target="tpu_custom_call" | custom-call | tf_op jit(solution)/shard_map/weight_grads/pallas_call | solution.py:1132
  289.4 25.6 %all-to-all-done.2 = f32[32,1,2624]{2,1,0:T(1,128)S(1)} async-done(((f32[32,1,2624]{2,1,0:T(1,128)}), f32[32,1,2624]{2,1,0:T(1,128)S(1)}, u32[]{:S(2)}, u32[]{:S(2)}) %all-to-all-start.2) | async-done | bytes 335904 | tf_op jit(solution)/shard_map/all_to_all | solution.py:1424
  327.1 11.6 %head_grad.1.grad = f32[1024,768]{1,0:T(8,128)} custom-call(bf16[1024,768]{1,0:T(8,128)(2,1)} %bitcast.583, bf16[1024,768]{1,0:T(8,128)(2,1)} %copy-done.105, bf16[1024,1024]{1,0:T(8,128)(2,1)} %get-tuple-element.418.kept_a, bf16[1024,1024]{1,0:T(8,128)(2,1)} %get-tuple-element.419.kept_b, f32[1024,128]{1,0:T(8,128)} %get-tuple-element.420.stat_a, ...), custom_call_target="tpu_custom_call" | custom-call | flops 3221225472 | bytes 4194304 | tf_op jit(solution)/shard_map/head_grad/pallas_call | solution.py:905
  338.7 10.4 %adam.2 = (f32[2,1000,768]{2,1,0:T(8,128)}, f32[2,1000,768]{2,1,0:T(8,128)}, f32[2,1000,768]{2,1,0:T(8,128)}) custom-call(f32[1024,768]{1,0:T(8,128)} %head_grad.1.grad, f32[2,1000,768]{2,1,0:T(8,128)} %w.3, f32[2,1000,768]{2,1,0:T(8,128)} %m.3, f32[2,1000,768]{2,1,0:T(8,128)} %v.3), custom_call_target="tpu_custom_call" | custom-call | flops 7680000 | bytes 21504000 | tf_op jit(solution)/shard_map/adam/pallas_call | solution.py:1214
  351.8 3.1 add_convert_fusion.10
  355.9 5.6 %all-to-all-done.3 = bf16[32,18,768]{2,1,0:T(8,128)(2,1)S(1)} async-done(((bf16[32,18,768]{2,1,0:T(8,128)(2,1)}), bf16[32,18,768]{2,1,0:T(8,128)(2,1)S(1)}, u32[]{:S(2)}, u32[]{:S(2)}) %all-to-all-start.3) | async-done | bytes 884768 | tf_op jit(solution)/shard_map/all_to_all | solution.py:1432
  368.1 10.3 %adam.3 = (f32[2,1000,768]{2,1,0:T(8,128)}, f32[2,1000,768]{2,1,0:T(8,128)}, f32[2,1000,768]{2,1,0:T(8,128)}) custom-call(f32[1000,768]{1,0:T(8,128)} %fusion.189.grad, f32[2,1000,768]{2,1,0:T(8,128)} %w.3, f32[2,1000,768]{2,1,0:T(8,128)} %m.3, f32[2,1000,768]{2,1,0:T(8,128)} %v.3, ...), custom_call_target="tpu_custom_call", output_to_operand_aliasing={{0}: (4, {}), {1}: (5, {}), {2}: (6, {})} | custom-call | flops 7680000 | bytes 21504000 | tf_op jit(solution)/shard_map/adam/pallas_call | solution.py:1214
  391.0 3.3 collective-permute-done.45.refs_1_
  394.4 6.5 %collective-permute-done.47 = bf16[192,384]{1,0:T(8,128)(2,1)S(1)} collective-permute-done((bf16[192,384]{1,0:T(8,128)(2,1)}, bf16[192,384]{1,0:T(8,128)(2,1)S(1)}, u32[]{:S(2)}, u32[]{:S(2)}) %collective-permute-start.47) | collective-permute-done | bytes 147488 | tf_op jit(solution)/shard_map/grads_third/ppermute | solution.py:535
  403.2 7.4 %shampoo.2 = (f32[4,192,384]{2,1,0:T(8,128)}, f32[4,192,384]{2,1,0:T(8,128)}, f32[4,768,768]{2,1,0:T(8,128)}, f32[4,384,384]{2,1,0:T(8,128)}) custom-call(s32[4]{0:T(128)} %pad_add_fusion.coord, bf16[2,192,384]{2,1,0:T(8,128)(2,1)} %reduce-scatter.11.cloned.1.call-done.refs_0_, bf16[2,192,384]{2,1,0:T(8,128)(2,1)} %copy-done.126, ...), custom_call_target="tpu_custom_call" | custom-call | flops 1811939328 | bytes 16777216 | tf_op jit(solution)/shard_map/shampoo/pallas_call | solution.py:1179
  415.3 7.6 %shampoo.3 = (f32[4,192,384]{2,1,0:T(8,128)}, f32[4,192,384]{2,1,0:T(8,128)}, f32[4,768,768]{2,1,0:T(8,128)}, f32[4,384,384]{2,1,0:T(8,128)}) custom-call(s32[4]{0:T(128)} %pad_add_fusion.coord, bf16[2,192,384]{2,1,0:T(8,128)(2,1)} %pad_maximum_fusion.27.refs_0_, ...), custom_call_target="tpu_custom_call", output_to_operand_aliasing={{0}: (10, {}), {1}: (11, {}), {2}: (12, {}), {3}: (13, {})} | custom-call | flops 1811939328 | bytes 16777216 | tf_op jit(solution)/shard_map/shampoo/pallas_call | solution.py:1179
  (308 shorter events, 146.3 us)
Async XLA Ops:
  7.2 45.7 %all-gather.22.cloned.1.call-start = ((), (), s32[]{:S(2)}) async-start(), calls=%async_computation.13 | async-start | bytes 1474560 | tf_op jit(solution)/shard_map/weights_pair/all_gather | solution.py:1282
  9.4 23.1 %collective-permute-start = (bf16[192,384]{1,0:T(8,128)(2,1)}, bf16[192,384]{1,0:T(8,128)(2,1)}, u32[]{:S(2)}, u32[]{:S(2)}) collective-permute-start(bf16[192,384]{1,0:T(8,128)(2,1)} %get-tuple-element.1018), channel_id=1, source_target_pairs={{0,8},{1,9},{2,10},{3,11},{4,12},{5,13},{6,14},{7,15},{8,16},{9,17... | collective-permute-start | bytes 442376 | tf_op jit(solution)/shard_map/weights_third/ppermute | solution.py:535
  12.4 20.1 %collective-permute-start.1 = (bf16[192,384]{1,0:T(8,128)(2,1)}, bf16[192,384]{1,0:T(8,128)(2,1)}, u32[]{:S(2)}, u32[]{:S(2)}) collective-permute-start(bf16[192,384]{1,0:T(8,128)(2,1)} %get-tuple-element.1018), channel_id=1, source_target_pairs={{0,16},{1,17},{2,18},{3,19},{4,20},{5,21},{6,22},{7,23},{8,24},{9,... | collective-permute-start | bytes 442376 | tf_op jit(solution)/shard_map/weights_third/ppermute | solution.py:535
  15.0 17.5 %collective-permute-start.2 = (bf16[192,384]{1,0:T(8,128)(2,1)}, bf16[192,384]{1,0:T(8,128)(2,1)}, u32[]{:S(2)}, u32[]{:S(2)}) collective-permute-start(bf16[192,384]{1,0:T(8,128)(2,1)} %get-tuple-element.1018), channel_id=1, source_target_pairs={{0,24},{1,25},{2,26},{3,27},{4,28},{5,29},{6,30},{7,31},{8,0},{9,1... | collective-permute-start | bytes 442376 | tf_op jit(solution)/shard_map/weights_third/ppermute | solution.py:535
  17.8 17.2 %collective-permute-start.4 = (bf16[192,384]{1,0:T(8,128)(2,1)}, bf16[192,384]{1,0:T(8,128)(2,1)}, u32[]{:S(2)}, u32[]{:S(2)}) collective-permute-start(bf16[192,384]{1,0:T(8,128)(2,1)} %get-tuple-element.1019), channel_id=1, source_target_pairs={{0,2},{1,5},{2,0},{3,7},{4,6},{5,1},{6,4},{7,3},{8,10},{9,13},{10,... | collective-permute-start | bytes 442376 | tf_op jit(solution)/shard_map/weights_last/ppermute | solution.py:519
  29.3 96.7 %all-gather.24.cloned.1.call-start = ((), (), s32[]{:S(2)}) async-start(), calls=%async_computation.14 | async-start | bytes 2949120 | tf_op jit(solution)/shard_map/weights_last/all_gather | solution.py:1334
  36.9 16.0 %collective-permute-start.6 = (bf16[4,192,384]{2,1,0:T(8,128)(2,1)}, bf16[4,192,384]{2,1,0:T(8,128)(2,1)}, u32[]{:S(2)}, u32[]{:S(2)}) collective-permute-start(bf16[4,192,384]{2,1,0:T(8,128)(2,1)} %pad_maximum_fusion.24.rest_8_.rest_22_), channel_id=1, source_target_pairs={{0,4},{1,3},{2,6},{3,1},{4,0},{5,7},{6,2},{7,5},{8,12},{9,11},{10,... | collective-permute-start | bytes 1769480 | tf_op jit(solution)/shard_map/weights_third/ppermute | solution.py:511
  38.5 14.4 %collective-permute-start.7 = (bf16[4,192,384]{2,1,0:T(8,128)(2,1)}, bf16[4,192,384]{2,1,0:T(8,128)(2,1)}, u32[]{:S(2)}, u32[]{:S(2)}) collective-permute-start(bf16[4,192,384]{2,1,0:T(8,128)(2,1)} %pad_maximum_fusion.24.rest_8_.rest_22_), channel_id=1, source_target_pairs={{0,2},{1,5},{2,0},{3,7},{4,6},{5,1},{6,4},{7,3},{8,10},{9,13},{10,... | collective-permute-start | bytes 1769480 | tf_op jit(solution)/shard_map/weights_third/ppermute | solution.py:519
  53.0 61.7 %all-to-all-start.1 = ((bf16[32,24,768]{2,1,0:T(8,128)(2,1)}), bf16[32,24,768]{2,1,0:T(8,128)(2,1)}, u32[]{:S(2)}, u32[]{:S(2)}) async-start(bf16[32,24,768]{2,1,0:T(8,128)(2,1)} %bitcast.597), calls=%async_computation.6 | async-start | bytes 2359296 | tf_op jit(solution)/shard_map/all_to_all | solution.py:1332
  58.8 296.1 %reduce-scatter.9.cloned.1.call-start = ((), (), s32[]{:S(2)}) async-start(), calls=%async_computation.11 | async-start | bytes 2949120 | tf_op jit(solution)/shard_map/grads_last/reduce_scatter | solution.py:1415
  59.5 26.2 %collective-permute-start.10 = (bf16[4,192,384]{2,1,0:T(8,128)(2,1)}, bf16[4,192,384]{2,1,0:T(8,128)(2,1)S(1)}, u32[]{:S(2)}, u32[]{:S(2)}) collective-permute-start(bf16[4,192,384]{2,1,0:T(8,128)(2,1)} %collective-permute-done.6.rest_10_.rest_24_), channel_id=1, source_target_pairs={{0,2},{1,5},{2,0},{3,7},{4,6},{5,1},{6,4},{7,3},{8,10},{9,13},{10,... | collective-permute-start | bytes 1769480 | tf_op jit(solution)/shard_map/weights_third/ppermute | solution.py:519
  61.1 26.9 %collective-permute-start.14 = (bf16[4,2,192,384]{3,2,1,0:T(8,128)(2,1)}, bf16[4,2,192,384]{3,2,1,0:T(8,128)(2,1)S(1)}, u32[]{:S(2)}, u32[]{:S(2)}) collective-permute-start(bf16[4,2,192,384]{3,2,1,0:T(8,128)(2,1)} %bitcast.584), channel_id=1, source_target_pairs={{0,1},{1,0},{2,3},{3,2},{4,5},{5,4},{6,7},{7,6},{8,9},{9,8},{10,11... | collective-permute-start | bytes 3538952 | tf_op jit(solution)/shard_map/ppermute | solution.py:527
  61.2 38.1 %collective-permute-start.8 = (bf16[4,2,192,384]{3,2,1,0:T(8,128)(2,1)}, bf16[4,2,192,384]{3,2,1,0:T(8,128)(2,1)}, u32[]{:S(2)}, u32[]{:S(2)}) collective-permute-start(bf16[4,2,192,384]{3,2,1,0:T(8,128)(2,1)} %bitcast.585), channel_id=1, source_target_pairs={{0,4},{1,3},{2,6},{3,1},{4,0},{5,7},{6,2},{7,5},{8,12},{9,11},{10,... | collective-permute-start | bytes 3538952 | tf_op jit(solution)/shard_map/weights_pair/ppermute | solution.py:511
  62.6 42.9 %collective-permute-start.9 = (bf16[4,2,192,384]{3,2,1,0:T(8,128)(2,1)}, bf16[4,2,192,384]{3,2,1,0:T(8,128)(2,1)S(1)}, u32[]{:S(2)}, u32[]{:S(2)}) collective-permute-start(bf16[4,2,192,384]{3,2,1,0:T(8,128)(2,1)} %bitcast.586), channel_id=1, source_target_pairs={{0,2},{1,5},{2,0},{3,7},{4,6},{5,1},{6,4},{7,3},{8,10},{9,13},{10,... | collective-permute-start | bytes 3538952 | tf_op jit(solution)/shard_map/weights_pair/ppermute | solution.py:519
  63.2 23.9 %collective-permute-start.12 = (bf16[4,192,384]{2,1,0:T(8,128)(2,1)}, bf16[4,192,384]{2,1,0:T(8,128)(2,1)}, u32[]{:S(2)}, u32[]{:S(2)}) collective-permute-start(bf16[4,192,384]{2,1,0:T(8,128)(2,1)} %collective-permute-done.6.rest_10_.rest_24_), channel_id=1, source_target_pairs={{0,1},{1,0},{2,3},{3,2},{4,5},{5,4},{6,7},{7,6},{8,9},{9,8},{10,11... | collective-permute-start | bytes 1769480 | tf_op jit(solution)/shard_map/ppermute | solution.py:527
  105.5 12.5 %collective-permute-start.16 = (bf16[4,2,192,384]{3,2,1,0:T(8,128)(2,1)S(1)}, bf16[4,2,192,384]{3,2,1,0:T(8,128)(2,1)}, u32[]{:S(2)}, u32[]{:S(2)}) collective-permute-start(bf16[4,2,192,384]{3,2,1,0:T(8,128)(2,1)S(1)} %collective-permute-done.9.rest_4_.rest_18_), channel_id=1, source_target_pairs={{0,1},{1,0},{2,3},{3,2},{4,5},{5,4},{6,7},{7,6},{8,9},{9,8},{10,11... | collective-permute-start | bytes 3538952 | tf_op jit(solution)/shard_map/ppermute | solution.py:527
  109.6 19.3 %collective-permute-start.18 = (bf16[4,2,192,384]{3,2,1,0:T(8,128)(2,1)}, bf16[4,2,192,384]{3,2,1,0:T(8,128)(2,1)}, u32[]{:S(2)}, u32[]{:S(2)}) collective-permute-start(bf16[4,2,192,384]{3,2,1,0:T(8,128)(2,1)} %collective-permute-done.8.rest_2_.rest_16_), channel_id=1, source_target_pairs={{0,2},{1,5},{2,0},{3,7},{4,6},{5,1},{6,4},{7,3},{8,10},{9,13},{10,... | collective-permute-start | bytes 3538952 | tf_op jit(solution)/shard_map/weights_pair/ppermute | solution.py:519
  195.2 26.9 %collective-permute-start.32 = (bf16[704,768]{1,0:T(8,128)(2,1)}, bf16[704,768]{1,0:T(8,128)(2,1)S(1)}, u32[]{:S(2)}, u32[]{:S(2)}) collective-permute-start(bf16[704,768]{1,0:T(8,128)(2,1)} %get-tuple-element.382.mine), channel_id=1, source_target_pairs={{0,1},{1,0},{2,3},{3,2},{4,5},{5,4},{6,7},{7,6},{8,9},{9,8},{10,11... | collective-permute-start | bytes 3244040 | tf_op jit(solution)/shard_map/ppermute | solution.py:527
  209.9 16.2 %collective-permute-start.31 = (bf16[256,896]{1,0:T(8,128)(2,1)}, bf16[256,896]{1,0:T(8,128)(2,1)S(1)}, u32[]{:S(2)}, u32[]{:S(2)}) collective-permute-start(bf16[256,896]{1,0:T(8,128)(2,1)} %merge_parts.6), channel_id=1, source_target_pairs={{0,2},{1,5},{2,0},{3,7},{4,6},{5,1},{6,4},{7,3},{8,10},{9,13},{10,... | collective-permute-start | bytes 1376264 | tf_op jit(solution)/shard_map/ppermute | solution.py:519
  282.3 32.7 %collective-permute-start.37 = (bf16[4,2,192,384]{3,2,1,0:T(8,128)(2,1)}, bf16[4,2,192,384]{3,2,1,0:T(8,128)(2,1)}, u32[]{:S(2)}, u32[]{:S(2)}) collective-permute-start(bf16[4,2,192,384]{3,2,1,0:T(8,128)(2,1)} %get-tuple-element.405), channel_id=1, source_target_pairs={{0,2},{1,5},{2,0},{3,7},{4,6},{5,1},{6,4},{7,3},{8,10},{9,13},{10,... | collective-permute-start | bytes 3538952 | tf_op jit(solution)/shard_map/grads_pair/ppermute | solution.py:519
  282.6 35.3 %collective-permute-start.38 = (bf16[4,2,192,384]{3,2,1,0:T(8,128)(2,1)}, bf16[4,2,192,384]{3,2,1,0:T(8,128)(2,1)}, u32[]{:S(2)}, u32[]{:S(2)}) collective-permute-start(bf16[4,2,192,384]{3,2,1,0:T(8,128)(2,1)} %get-tuple-element.406), channel_id=1, source_target_pairs={{0,2},{1,5},{2,0},{3,7},{4,6},{5,1},{6,4},{7,3},{8,10},{9,13},{10,... | collective-permute-start | bytes 3538952 | tf_op jit(solution)/shard_map/grads_pair/ppermute | solution.py:519
  285.5 29.4 %all-to-all-start.2 = ((f32[32,1,2624]{2,1,0:T(1,128)}), f32[32,1,2624]{2,1,0:T(1,128)S(1)}, u32[]{:S(2)}, u32[]{:S(2)}) async-start(f32[32,1,2624]{2,1,0:T(1,128)} %broadcast_in_dim.197), calls=%async_computation.7 | async-start | bytes 688128 | tf_op jit(solution)/shard_map/all_to_all | solution.py:1424
  319.2 29.9 %collective-permute-start.40 = (bf16[4,192,384]{2,1,0:T(8,128)(2,1)}, bf16[4,192,384]{2,1,0:T(8,128)(2,1)}, u32[]{:S(2)}, u32[]{:S(2)}) collective-permute-start(bf16[4,192,384]{2,1,0:T(8,128)(2,1)} %get-tuple-element.415), channel_id=1, source_target_pairs={{0,2},{1,5},{2,0},{3,7},{4,6},{5,1},{6,4},{7,3},{8,10},{9,13},{10,... | collective-permute-start | bytes 1769480 | tf_op jit(solution)/shard_map/grads_third/ppermute | solution.py:519
  319.7 32.1 %collective-permute-start.39 = (bf16[4,2,192,384]{3,2,1,0:T(8,128)(2,1)}, bf16[4,2,192,384]{3,2,1,0:T(8,128)(2,1)}, u32[]{:S(2)}, u32[]{:S(2)}) collective-permute-start(bf16[4,2,192,384]{3,2,1,0:T(8,128)(2,1)} %add_convert_fusion.11), channel_id=1, source_target_pairs={{0,4},{1,3},{2,6},{3,1},{4,0},{5,7},{6,2},{7,5},{8,12},{9,11},{10,... | collective-permute-start | bytes 3538952 | tf_op jit(solution)/shard_map/grads_pair/ppermute | solution.py:511
  322.7 38.8 %all-to-all-start.3 = ((bf16[32,18,768]{2,1,0:T(8,128)(2,1)}), bf16[32,18,768]{2,1,0:T(8,128)(2,1)S(1)}, u32[]{:S(2)}, u32[]{:S(2)}) async-start(bf16[32,18,768]{2,1,0:T(8,128)(2,1)} %all_to_all.38), calls=%async_computation.9 | async-start | bytes 2359296 | tf_op jit(solution)/shard_map/all_to_all | solution.py:1432
  325.4 59.6 %reduce-scatter.11.cloned.1.call-start = ((), (), s32[]{:S(2)}) async-start(), calls=%async_computation.12 | async-start | bytes 1474560 | tf_op jit(solution)/shard_map/grads_pair/reduce_scatter | solution.py:1460
  361.8 18.5 %collective-permute-start.43 = (bf16[4,192,384]{2,1,0:T(8,128)(2,1)}, bf16[4,192,384]{2,1,0:T(8,128)(2,1)}, u32[]{:S(2)}, u32[]{:S(2)}) collective-permute-start(bf16[4,192,384]{2,1,0:T(8,128)(2,1)} %add_convert_fusion.12), channel_id=1, source_target_pairs={{0,4},{1,3},{2,6},{3,1},{4,0},{5,7},{6,2},{7,5},{8,12},{9,11},{10,... | collective-permute-start | bytes 1769480 | tf_op jit(solution)/shard_map/grads_third/ppermute | solution.py:511
  361.9 18.4 %collective-permute-start.44 = (bf16[4,192,384]{2,1,0:T(8,128)(2,1)}, bf16[4,192,384]{2,1,0:T(8,128)(2,1)}, u32[]{:S(2)}, u32[]{:S(2)}) collective-permute-start(bf16[4,192,384]{2,1,0:T(8,128)(2,1)} %get-tuple-element.434), channel_id=1, source_target_pairs={{0,2},{1,5},{2,0},{3,7},{4,6},{5,1},{6,4},{7,3},{8,10},{9,13},{10,... | collective-permute-start | bytes 1769480 | tf_op jit(solution)/shard_map/grads_third/ppermute | solution.py:519
  363.0 15.5 %collective-permute-start.41 = (bf16[192,384]{1,0:T(8,128)(2,1)S(1)}, bf16[192,384]{1,0:T(8,128)(2,1)S(1)}, u32[]{:S(2)}, u32[]{:S(2)}) collective-permute-start(bf16[192,384]{1,0:T(8,128)(2,1)S(1)} %get-tuple-element.1016), channel_id=1, source_target_pairs={{0,2},{1,5},{2,0},{3,7},{4,6},{5,1},{6,4},{7,3},{8,10},{9,13},{10,... | collective-permute-start | bytes 442376 | tf_op jit(solution)/shard_map/grads_last/ppermute | solution.py:519
  367.1 15.7 %collective-permute-start.42 = (bf16[192,384]{1,0:T(8,128)(2,1)S(1)}, bf16[192,384]{1,0:T(8,128)(2,1)}, u32[]{:S(2)}, u32[]{:S(2)}) collective-permute-start(bf16[192,384]{1,0:T(8,128)(2,1)S(1)} %get-tuple-element.1015), channel_id=1, source_target_pairs={{0,2},{1,5},{2,0},{3,7},{4,6},{5,1},{6,4},{7,3},{8,10},{9,13},{10,... | collective-permute-start | bytes 442376 | tf_op jit(solution)/shard_map/grads_last/ppermute | solution.py:519
  387.6 13.3 %collective-permute-start.47 = (bf16[192,384]{1,0:T(8,128)(2,1)}, bf16[192,384]{1,0:T(8,128)(2,1)S(1)}, u32[]{:S(2)}, u32[]{:S(2)}) collective-permute-start(bf16[192,384]{1,0:T(8,128)(2,1)} %get-tuple-element.439), channel_id=1, source_target_pairs={{0,16},{1,17},{2,18},{3,19},{4,20},{5,21},{6,22},{7,23},{8,24},{9,... | collective-permute-start | bytes 442376 | tf_op jit(solution)/shard_map/grads_third/ppermute | solution.py:535
  387.6 13.3 %collective-permute-start.48 = (bf16[192,384]{1,0:T(8,128)(2,1)}, bf16[192,384]{1,0:T(8,128)(2,1)S(1)}, u32[]{:S(2)}, u32[]{:S(2)}) collective-permute-start(bf16[192,384]{1,0:T(8,128)(2,1)} %get-tuple-element.440), channel_id=1, source_target_pairs={{0,8},{1,9},{2,10},{3,11},{4,12},{5,13},{6,14},{7,15},{8,16},{9,17... | collective-permute-start | bytes 442376 | tf_op jit(solution)/shard_map/grads_third/ppermute | solution.py:535
  (79 other events, 849.6 us)
Sparse Core Ops, SparseCore 0:
  20.2 27.3 all-gather.21
  53.1 72.9 all-gather.23
  282.4 53.4 reduce-scatter.8
  355.0 29.8 reduce-scatter.10
